TPU v7x, 32 devices: a whole 2x2x4 slice. The times are simulated.
32 devices in a mesh: aux: 8 (over z, y), orb: 4 (over x, core).
Axes of the slice: x: 2, y: 2, z: 4, core: 2. Of those that a mesh axis runs over, the one named last changes fastest.
Arguments:
- three_index: bfloat16 [64, 1600, 1600], P('aux', 'orb'), may hold values from -40 to 40, as said below
- density: bfloat16 [64, 1600, 160], P('aux', 'orb'), may hold values from -0.01953125 to 0.01953125
- hess_diag: float32 [1440, 160], replicated, may hold values from 0.5 to 4
Outputs:
- ov_new: bfloat16 [4, 64, 57600], P('orb', None, 'aux')
Inputs may be any that keep to these rules, and one draw needn't show every extreme that they name: three_index[q, p, r] equals three_index[q, r, p].
All inputs are finite; a program needn't handle non-finite values.
Results may differ from a plain program's by a relative error of at most 0.0065.
Values may be sent and summed in bfloat16 or wider, within the bound.
No kernel may reach another device: no remote copies, remote signals or barrier semaphores. Data moves between devices by JAX's collectives and lax.ppermute only.
A program may use at most 64 MiB of HBM per device.

v0:
```python
import math

import jax
import jax.numpy as jnp
from jax import lax
from jax.sharding import PartitionSpec as P


def on_device(three_index, density, hess_diag):
    highest = lax.Precision.HIGHEST
    aux_count, blk_rows, orb_total = three_index.shape
    n_occ = density.shape[2]
    n_vir = orb_total - n_occ
    orb_pos = lax.axis_index("orb")
    partial_fock = jnp.einsum(
        "qrp,qri->pi", three_index, density, preferred_element_type=jnp.float32
    )[n_occ:]
    radius = math.sqrt(n_occ)
    fock_vo = lax.psum(partial_fock, ("aux", "orb"))
    generator = -fock_vo / hess_diag
    gen_norm = jnp.sqrt(jnp.sum(generator * generator))
    rotation = generator * jnp.minimum(1.0, radius / gen_norm)
    occ_eye = jnp.eye(n_occ, dtype=jnp.float32)
    intersection = jnp.dot(rotation.T, rotation, precision=highest)
    squared = jnp.dot(intersection, intersection, precision=highest)
    rot_over = jnp.dot(rotation, intersection, precision=highest)
    u_occ = jnp.concatenate(
        [occ_eye - intersection / 2.0 + squared / 24.0, rotation - rot_over / 6.0], 0
    )
    left_factor = jnp.concatenate(
        [-(occ_eye - intersection / 6.0), -rotation / 2.0 + rot_over / 24.0], 0
    )
    half_rot = jnp.einsum(
        "qrs,si->qri", three_index, u_occ.astype(jnp.bfloat16), preferred_element_type=jnp.float32
    ).astype(jnp.bfloat16)
    row_start = orb_pos * blk_rows
    rows_factor = lax.dynamic_slice_in_dim(left_factor, row_start, blk_rows, 0)
    row_ids = row_start + lax.broadcasted_iota(jnp.int32, (blk_rows, n_vir), 0)
    col_ids = n_occ + lax.broadcasted_iota(jnp.int32, (blk_rows, n_vir), 1)
    u_vir = (
        jnp.where(row_ids == col_ids, 1.0, 0.0)
        + jnp.dot(rows_factor, rotation.T, precision=highest)
    ).astype(jnp.bfloat16)
    summed = lax.psum_scatter(
        jnp.einsum("qri,ra->iqa", half_rot, u_vir, preferred_element_type=jnp.float32),
        "orb",
        scatter_dimension=0,
        tiled=True,
    )
    rotated = jnp.transpose(summed.astype(jnp.bfloat16), (1, 0, 2))
    pair_block = rotated.reshape(aux_count, -1)
    owned = lax.all_to_all(pair_block, "aux", split_axis=1, concat_axis=0, tiled=True)
    return owned[None]


def solution(mesh):
    return jax.shard_map(
        on_device,
        mesh=mesh,
        in_specs=(P("aux", "orb", None), P("aux", "orb", None), P()),
        out_specs=P("orb", None, "aux"),
        check_vma=False,
    )
```

profile of v0, /device:TPU:0, one launch (start us, length us, event | category | flops | bytes accessed | tf_op | source)
XLA Modules:
  0.0 275.9 jit_solution(13161126767174867205)
XLA Ops:
  6.5 0.0 copy-start
  6.5 0.0 all-reduce.2.cloned.1.call-start
  6.5 1.3 copy-done
  7.9 6.1 %convolution_bitcast_fusion = f32[1600,160]{0,1:T(8,128)S(1)} fusion(bf16[8,400,160]{1,2,0:T(8,128)(2,1)S(1)} %copy-done, bf16[8,400,1600]{2,1,0:T(8,128)(2,1)} %param.3), kind=kOutput, calls=%fused_computation.2 | convolution fusion | flops 1638400000 | bytes 12288000 | tf_op jit(solution)/shard_map/qrp,qri->pi/dot_general | solution.py:15
  14.0 0.0 copy-start.1
  14.0 1.3 slice.4
  15.3 0.0 all-reduce.2.cloned.1.call-update
  15.3 0.2 reduce-scatter.2.cloned.1.call-start
  15.6 131.2 %all-reduce.2.cloned.1.call-done = f32[1440,160]{0,1:T(8,128)} async-done(((f32[1440,160]{0,1:T(8,128)}), f32[1440,160]{0,1:T(8,128)}) %all-reduce.2.cloned.1.call-update) | async-done | bytes 921616 | tf_op jit(solution)/shard_map/psum | solution.py:19
  146.7 0.0 copy-done.1
  146.8 2.1 multiply_reduce_fusion
  149.5 1.0 fusion.15
  150.5 0.3 fusion.2
  150.8 1.2 multiply_add_fusion
  152.1 7.4 %convolution_convert_fusion = bf16[160,8,400]{2,0,1:T(8,128)(2,1)S(1)} fusion(bf16[8,400,1600]{2,1,0:T(8,128)(2,1)} %param.3, bf16[1440,160]{0,1:T(8,128)(2,1)S(1)} %get-tuple-element.8, bf16[160,160]{0,1:T(8,128)(2,1)S(1)} %fusion.2), kind=kOutput, calls=%fused_computation.3 | convolution fusion | flops 1639936000 | bytes 11776000 | tf_op jit(solution)/shard_map/qrs,si->qri/dot_general | solution.py:33
  159.5 2.4 fusion
  161.9 5.3 %fusion.19 = f32[1440,1280]{0,1} fusion(bf16[400,1280]{0,1:T(8,128)(2,1)S(1)} %bitcast.28, bf16[400,1440]{1,0:T(8,128)(2,1)S(1)} %fusion), kind=kOutput, calls=%fused_computation.35 | convolution fusion | flops 1474560000 | bytes 9548800
  167.2 0.0 reduce-scatter.2.cloned.1.call-update
  167.2 69.2 %reduce-scatter.2.cloned.1.call-done = f32[40,8,1440]{2,0,1:T(8,128)} async-done(((f32[160,8,1440]{2,0,1:T(8,128)}), f32[40,8,1440]{2,0,1:T(8,128)}) %reduce-scatter.2.cloned.1.call-update) | async-done | bytes 1843216 | tf_op jit(solution)/shard_map/reduce_scatter | solution.py:44
  236.4 1.6 convert_bitcast_fusion
  238.0 1.0 all_to_all.12
  239.1 0.1 copy.5
  239.2 28.9 %all_to_all.16 = bf16[8,8,7200]{2,0,1:T(8,128)(2,1)S(1)} all-to-all(bf16[8,8,7200]{2,0,1:T(8,128)(2,1)S(1)} %copy.5), channel_id=1, replica_groups=mesh['aux'=8,'orb'=4] {'aux'}, dimensions={1} | all-to-all | bytes 1843200 | tf_op jit(solution)/shard_map/all_to_all | solution.py:52
  268.1 0.9 copy.8
  (2 shorter events, 0.0 us)
Async XLA Ops:
  6.5 1.3 copy-start
  6.5 140.2 %all-reduce.2.cloned.1.call-start = ((), (), s32[]{:S(2)}) async-start(), calls=%async_computation.2 | async-start | bytes 1966080 | tf_op jit(solution)/shard_map/psum | solution.py:19
  14.0 132.8 %copy-start.1 = (f32[1440,160]{0,1:T(8,128)S(1)}, f32[1440,160]{0,1:T(8,128)}, u32[]{:S(2)}) copy-start(f32[1440,160]{0,1:T(8,128)} %param.5) | copy-start | bytes 2764804
  15.3 221.1 %reduce-scatter.2.cloned.1.call-start = ((), (), s32[]{:S(2)}) async-start(), calls=%async_computation.3 | async-start | bytes 9830400 | tf_op jit(solution)/shard_map/reduce_scatter | solution.py:44
Sparse Core Ops, SparseCore 0:
  15.5 131.2 all-reduce.1
  167.3 69.0 reduce-scatter.1
where the time goes:
time: 276 us
  waiting for transfers between devices  200 us (72%)
  blocking collectives  28.9 us (10%)
  matrix products  23.8 us (9%)
  between operations  14.2 us (5%)
  local copies, waits for them, and re-layouts  4.71 us (2%)
  other arithmetic  3.73 us (1%)
    psum x1, waiting for transfers between devices, on_device(): fock_vo = lax.psum(partial_fock, ('aux', 'orb'))  131 us
    reduce_scatter x1, waiting for transfers between devices, on_device(): lax.psum_scatter(jnp.einsum('qri,ra->iqa', half_rot, u_vir, preferred_ele...  69.2 us
    all_to_all x1, blocking collectives, on_device(): lax.all_to_all(pair_block, 'aux', split_axis=1, concat_axis=0, tiled=True)  28.9 us
    dot_general x1, matrix products, on_device(): jnp.einsum('qrs,si->qri', three_index, u_occ.astype(jnp.bfloat16), prefer...  7.39 us
    dot_general x1, matrix products, on_device(): jnp.einsum('qrp,qri->pi', three_index, density, preferred_element_type=jn...  6.11 us
  transfers between devices with their start and end apart: 2, of which 2 were waited for; matrix products, arithmetic and copies ran while one was open for 0% of the time, Pallas kernels for 0%

commit v1 on v0

v1 whole, which is shorter than its diff:
```python
import functools
import math

import jax
import jax.numpy as jnp
import numpy as np
from jax import lax
from jax.experimental import pallas as pl
from jax.experimental.pallas import tpu as pltpu
from jax.sharding import PartitionSpec as P

BOTH = ("aux", "orb")
F32 = jnp.float32
BF16 = jnp.bfloat16
LANES = 128
MIB = 1 << 20


def matmul(a, b, dims):
    return lax.dot_general(a, b, (dims, ((), ())), preferred_element_type=F32)


NN = ((1,), (0,))
NT = ((1,), (1,))
TN = ((0,), (0,))


def my_index(n_orb):
    return lax.axis_index("aux") * n_orb + lax.axis_index("orb")


def swap(x, masks):
    return lax.ppermute(x, BOTH, [(d, d ^ mask) for d, mask in enumerate(masks)])


def tracks_of(n_dev):
    bits = n_dev.bit_length() - 1
    return [1, 2, *range(3, bits)], [2, 1, *range(bits - 1, 2, -1)]


def bit(index, which):
    return (index // (1 << which)) % 2


def half_of(index, n_dev):
    return sum(bit(index, k) for k in range(n_dev.bit_length() - 1)) % 2


def assemble(sources, width, rows):
    lane = lax.broadcasted_iota(jnp.int32, (rows, LANES), 1)
    rolled = {}

    def source_tile(which, tile, turn):
        key = (which, tile, turn)
        if key not in rolled:
            value = sources[which][0](tile)
            rolled[key] = pltpu.roll(value, turn, 1) if turn else value
        return rolled[key]

    tiles = []
    for start in range(0, width, LANES):
        result, end_done = None, 0
        for which, (_, src, dst, count) in enumerate(sources):
            low, high = max(dst, start), min(dst + count, start + LANES)
            turn = (dst - src) % LANES
            at = low
            while at < high:
                from_lane = at - dst + src
                tile = from_lane // LANES
                stop = min(high, at + LANES - from_lane % LANES)
                value = source_tile(which, tile, turn)
                if result is None:
                    result = value
                    if at > start:
                        result = jnp.where(lane >= at - start, value, 0.0)
                else:
                    result = jnp.where(lane >= at - start, value, result)
                end_done = stop - start
                at = stop
        if end_done < LANES:
            result = jnp.where(lane < end_done, result, 0.0)
        tiles.append(result)
    return tiles


def fock_kernel(n_orb, n_dev, splits, three_hbm, dens_ref, keep_ref, send_ref, three_ref, acc_ref, sems):
    n_tiles = acc_ref.shape[0]
    q_loc, _, n_mo = three_ref.shape
    n_occ = dens_ref.shape[1]
    base = n_occ // LANES * LANES
    copies = []
    for q in range(q_loc):
        copies.append(pltpu.make_async_copy(three_hbm.at[q], three_ref.at[q], sems.at[q]))
        copies[q].start()
    for q in range(q_loc):
        copies[q].wait()
        part = matmul(dens_ref[q], three_ref[q, :, base:], NN)
        for t in range(n_tiles):
            stop = min(LANES, n_mo - base - t * LANES)
            piece = part[:, t * LANES : t * LANES + stop]
            if q:
                acc_ref[t, :, :stop] += piece
            else:
                if stop < LANES:
                    acc_ref[t] = jnp.zeros(acc_ref.shape[1:], F32)
                acc_ref[t, :, :stop] = piece
    me = my_index(n_orb)
    mine = half_of(me, n_dev)
    half, quarter = n_tiles // 2, n_tiles // 4
    for ref, side in ((keep_ref, mine), (send_ref, 1 - mine)):
        lead = jnp.where(side == 0, bit(me, splits[0]), bit(me, splits[1]))
        for j in range(half):
            first = jnp.where(lead == j // quarter, 0, quarter)
            ref[j] = acc_ref[side * half + first + j % quarter].astype(ref.dtype)


def rotation_kernel(n_orb, n_dev, splits, mine_ref, other_ref, hess_ref, sel_ref, chosen_ref, left_ref, rot_ref, fock_ref, u_ref):
    n_occ, width = fock_ref.shape
    half = mine_ref.shape[0]
    quarter = half // 2
    base = n_occ // LANES * LANES
    n_mo = chosen_ref.shape[1]
    me = my_index(n_orb)
    mine = half_of(me, n_dev)
    for t in range(2 * half):
        side = t // half
        first = jnp.where(bit(me, splits[side]) == t % half // quarter, 0, quarter)
        at = first + t % quarter
        fock_ref[:, t * LANES : (t + 1) * LANES] = jnp.where(
            mine == side, mine_ref[at].astype(F32), other_ref[at].astype(F32))
    gen = -fock_ref[...] / hess_ref[...]
    square = jnp.sum(jnp.sum(gen * gen, axis=0, keepdims=True), axis=1, keepdims=True)
    rot = gen * jnp.minimum(1.0, math.sqrt(n_occ) / jnp.sqrt(square))
    rot_b = rot.astype(BF16)
    rot_ref[...] = rot_b
    over = matmul(rot_b, rot_b, NT)
    over_b = over.astype(BF16)
    over2 = matmul(over_b, over_b, NN)
    over_rot = matmul(over_b, rot_b, NN)
    eye = jnp.where(
        lax.broadcasted_iota(jnp.int32, (n_occ, n_occ), 0) == lax.broadcasted_iota(jnp.int32, (n_occ, n_occ), 1),
        1.0, 0.0)
    u_oo = (eye - over / 2.0 + over2 / 24.0).astype(BF16)
    u_ref[:, :base] = u_oo[:, :base]
    u_ref[:, base:] = (rot - over_rot / 6.0).astype(BF16)
    u_ref[:, base:n_occ] = u_oo[:, base:]
    l_oo = (over / 6.0 - eye).astype(BF16)
    left_ref[:, :base] = l_oo[:, :base]
    left_ref[:, base:] = (over_rot / 24.0 - rot / 2.0).astype(BF16)
    left_ref[:, base:n_occ] = l_oo[:, base:]
    chosen_ref[...] = matmul(sel_ref[...], u_ref[:, :n_mo], NN).astype(BF16)


def half_kernel(n_rows, main, chosen_ref, three_ref, sent_ref, rem_ref, half_ref):
    q_loc, r_loc, n_mo = three_ref.shape
    rem = r_loc - main
    n_dev, dest_rows = sent_ref.shape[:2]

    def store(value, row):
        for k in range(n_rows):
            half_ref[pl.ds(row(k), n_dev, stride=dest_rows), :] = value[k * n_dev : (k + 1) * n_dev, :]

    chosen = chosen_ref[...]
    for q in range(q_loc):
        product = matmul(chosen, three_ref[q, :main, :], NT)
        for c in range(main // LANES):
            store(product[:, c * LANES : (c + 1) * LANES], lambda k, c=c, q=q: (c * n_rows + k) * q_loc + q)
        rem_ref[q * rem : (q + 1) * rem, :] = three_ref[q, main:, :]
    store(matmul(chosen, rem_ref[...], NT), lambda k: main // LANES * n_rows * q_loc + k)
    for d in range(n_dev):
        sent_ref[d] = half_ref[d * dest_rows : (d + 1) * dest_rows, :].astype(BF16)


def owner_kernel(n_rows, n_aux, q_loc, r_loc, main, got_ref, left_ref, rot_ref, out_ref):
    n_orb = got_ref.shape[1]
    places = pl.ds(pl.program_id(0) * n_aux, n_aux)
    n_occ, wide = left_ref.shape
    width = rot_ref.shape[1]
    base = wide - width
    n_mo = n_orb * r_loc
    n_vir = n_mo - n_occ
    rem = r_loc - main
    group = n_rows * q_loc
    rows = n_aux * group
    lane_q = lax.broadcasted_iota(jnp.int32, (n_aux, q_loc, LANES), 2) // rem
    own_q = lane_q == lax.broadcasted_iota(jnp.int32, (n_aux, q_loc, LANES), 1)
    e_row = lax.broadcasted_iota(jnp.int32, (LANES, LANES), 0) % rem
    e_col = lax.broadcasted_iota(jnp.int32, (LANES, LANES), 1)

    sources = []
    rest = jnp.zeros((rows, LANES), F32)
    for b in range(n_orb):
        block = got_ref[places, b, :, :].astype(F32)
        pieces = [block[:, c * group : (c + 1) * group, :].reshape(rows, LANES) for c in range(main // LANES)]
        last = main // LANES * group
        spread = [
            jnp.where(own_q, jnp.broadcast_to(block[:, last + k : last + k + 1, :], own_q.shape), 0.0)
            for k in range(n_rows)
        ]
        spread = jnp.concatenate(spread, 1).reshape(rows, LANES).astype(BF16)
        rest = rest + matmul(spread, jnp.where(e_row + b * rem == e_col, 1.0, 0.0).astype(BF16), NN)
        sources.append((lambda tile, pieces=pieces: pieces[tile], 0, b * r_loc, main))
    for b in range(n_orb):
        sources.append((lambda tile: rest, b * rem, b * r_loc + main, rem))
    sources.sort(key=lambda entry: entry[2])
    half = jnp.concatenate(assemble(sources, wide, rows), 1)
    inner = matmul(half.astype(BF16), left_ref[...], NT).astype(BF16)
    total = half[:, base:] + matmul(inner, rot_ref[...], NN)
    total = total.reshape(n_aux, group, width)
    per_row = [total[:, k * q_loc : (k + 1) * q_loc, :].reshape(n_aux * q_loc, width) for k in range(n_rows)]
    sources = [
        (lambda tile, value=value: value[:, tile * LANES : (tile + 1) * LANES], n_occ - base, k * n_vir, n_vir)
        for k, value in enumerate(per_row)
    ]
    length = n_rows * n_vir
    for at, value in enumerate(assemble(sources, length, n_aux * q_loc)):
        stop = min(length, (at + 1) * LANES)
        out_ref[:, at * LANES : stop] = value[:, : stop - at * LANES].astype(BF16)


def on_device(n_aux, n_orb, three_index, density, hess_diag):
    n_dev = n_aux * n_orb
    q_loc, r_loc, n_mo = three_index.shape
    n_occ = density.shape[2]
    n_vir = n_mo - n_occ
    occ_blk = n_occ // n_orb
    pairs = occ_blk * n_vir // n_aux
    base = n_occ // LANES * LANES
    tiles = -(-(n_mo - base) // LANES)
    width = tiles * LANES
    main = r_loc // LANES * LANES
    assert n_dev & (n_dev - 1) == 0 and n_dev >= 8 and tiles % 4 == 0
    tracks = tracks_of(n_dev)
    splits = (tracks[0][0], tracks[1][0])
    whole = lambda *shape: pl.BlockSpec(shape, lambda *_: (0,) * len(shape))
    in_vmem = pl.BlockSpec(memory_space=pltpu.VMEM)

    half_shape = (tiles // 2, n_occ, LANES)
    in_hbm = pl.BlockSpec(memory_space=pltpu.HBM)
    keep, send, three_vmem = pl.pallas_call(
        functools.partial(fock_kernel, n_orb, n_dev, splits),
        in_specs=[in_hbm, in_vmem],
        out_specs=[in_vmem] * 3,
        out_shape=[
            jax.ShapeDtypeStruct(half_shape, F32),
            jax.ShapeDtypeStruct(half_shape, BF16),
            jax.ShapeDtypeStruct(three_index.shape, BF16),
        ],
        scratch_shapes=[
            pltpu.VMEM((tiles, n_occ, LANES), F32),
            pltpu.SemaphoreType.DMA((q_loc,)),
        ],
        compiler_params=pltpu.CompilerParams(vmem_limit_bytes=38 * MIB),
        cost_estimate=pl.CostEstimate(
            flops=2 * q_loc * r_loc * n_occ * n_mo, bytes_accessed=2 * q_loc * r_loc * n_mo, transcendentals=0),
        name="fock",
    )(three_index, density.transpose(0, 2, 1))
    hess = jnp.pad(
        hess_diag.T, ((0, 0), (n_occ - base, width - (n_mo - base))), constant_values=jnp.inf)

    masks = [[1 | 1 << tracks[half_of(d, n_dev)][k] for d in range(n_dev)] for k in range(len(tracks[0]))]
    part = keep + swap(send, [1] * n_dev).astype(F32)
    part = part[: tiles // 4] + swap(part[tiles // 4 :].astype(BF16), masks[0]).astype(F32)
    for mask in masks[1:]:
        part = part + swap(part.astype(BF16), mask).astype(F32)
    part = part.astype(BF16)
    held = jnp.concatenate([part, swap(part, masks[0])], 0)
    other = swap(held, [1] * n_dev)

    first = [p * pairs // n_vir for p in range(n_aux)]
    n_rows = max(-(-(p + 1) * pairs // n_vir) - first[p] for p in range(n_aux))
    sel = np.zeros((n_rows, n_aux, n_orb, n_occ), np.float32)
    for k in range(n_rows):
        for p in range(n_aux):
            for b in range(n_orb):
                sel[k, p, b, b * occ_blk + min(first[p] + k, occ_blk - 1)] = 1.0
    sel = jnp.asarray(sel.reshape(n_rows * n_dev, n_occ), BF16)

    dest_rows = -(-(main // LANES * n_rows * q_loc + n_rows) // 16) * 16
    wide = base + width
    chosen, left, rot = pl.pallas_call(
        functools.partial(rotation_kernel, n_orb, n_dev, splits),
        in_specs=[in_vmem] * 4,
        out_specs=[in_vmem] * 3,
        out_shape=[
            jax.ShapeDtypeStruct((n_rows * n_dev, n_mo), BF16),
            jax.ShapeDtypeStruct((n_occ, wide), BF16),
            jax.ShapeDtypeStruct((n_occ, width), BF16),
        ],
        scratch_shapes=[pltpu.VMEM((n_occ, width), F32), pltpu.VMEM((n_occ, wide), BF16)],
        compiler_params=pltpu.CompilerParams(vmem_limit_bytes=16 * MIB),
        cost_estimate=pl.CostEstimate(flops=8 * n_occ * n_occ * n_mo, bytes_accessed=4 * MIB, transcendentals=0),
        name="rotation",
    )(held, other, hess, sel)
    sent = pl.pallas_call(
        functools.partial(half_kernel, n_rows, main),
        in_specs=[in_vmem] * 2,
        out_specs=in_vmem,
        out_shape=jax.ShapeDtypeStruct((n_dev, dest_rows, LANES), BF16),
        scratch_shapes=[
            pltpu.VMEM((q_loc * (r_loc - main), n_mo), BF16),
            pltpu.VMEM((n_dev * dest_rows, LANES), F32),
        ],
        compiler_params=pltpu.CompilerParams(vmem_limit_bytes=40 * MIB),
        cost_estimate=pl.CostEstimate(
            flops=2 * q_loc * r_loc * n_rows * n_dev * n_mo, bytes_accessed=2 * q_loc * r_loc * n_mo, transcendentals=0),
        name="half_rotation",
    )(chosen, three_vmem)

    got = lax.all_to_all(sent, BOTH, 0, 0, tiled=True).reshape(n_aux, n_orb, dest_rows, LANES)
    aux_step = min(n_aux, 8)
    out = pl.pallas_call(
        functools.partial(owner_kernel, n_rows, aux_step, q_loc, r_loc, main),
        grid=(n_aux // aux_step,),
        in_specs=[in_vmem] * 3,
        out_specs=pl.BlockSpec((aux_step * q_loc, n_rows * n_vir), lambda g: (g, 0)),
        out_shape=jax.ShapeDtypeStruct((n_aux * q_loc, n_rows * n_vir), BF16),
        compiler_params=pltpu.CompilerParams(vmem_limit_bytes=40 * MIB),
        cost_estimate=pl.CostEstimate(
            flops=4 * n_aux * q_loc * n_rows * n_occ * n_mo, bytes_accessed=8 * MIB, transcendentals=0),
        name="owner_rows",
    )(got, left, rot)
    if n_rows * n_vir != pairs:
        start = (lax.axis_index("aux") * pairs) % n_vir
        out = lax.dynamic_slice_in_dim(out, start, pairs, 1)
    return out[None]


def solution(mesh):
    def body(*args):
        return on_device(mesh.shape["aux"], mesh.shape["orb"], *args)

    return jax.shard_map(
        body,
        mesh=mesh,
        in_specs=(P("aux", "orb", None), P("aux", "orb", None), P()),
        out_specs=P("orb", None, "aux"),
        check_vma=False,
    )
```

time: 276 us -> 76.2 us (0.28)
  waiting for transfers between devices: 200 us -> 15.9 us
  matrix products: 23.8 us -> 0 us
  between operations: 14.2 us -> 0.06 us
  Pallas kernels: 0 us -> 13.5 us
  starting transfers between devices: 0.22 us -> 12.9 us
  other arithmetic: 3.73 us -> 0.33 us
  local copies, waits for them, and re-layouts: 4.71 us -> 1.66 us
    psum x1 -> x0, waiting for transfers between devices: 131 us -> none  [on_device(): fock_vo = lax.psum(partial_fock, ('aux', 'orb'))]
    reduce_scatter x1 -> x0, waiting for transfers between devices: 69.2 us -> none  [on_device(): lax.psum_scatter(jnp.einsum('qri,ra->iqa', half_rot, u_vir, preferred_ele...]
    dot_general x6 -> x0, matrix products: 18.5 us -> none  [the longest x1 7.39 us: on_device(): jnp.einsum('qrs,si->qri', three_index, u_occ.astype(jnp.bfloat16), prefer...]
    ppermute x0 -> x7, waiting for transfers between devices: none -> 15.9 us  [swap(): lax.ppermute(x, BOTH, [(d, d ^ mask) for d, mask in enumerate(masks)])]
    pallas_call x0 -> x4, Pallas kernels: none -> 13.5 us  [the longest x1 4.89 us: on_device(): pl.pallas_call(functools.partial(fock_kernel, n_orb, n_dev, splits), in_s...]
    ppermute x0 -> x7, starting transfers between devices: none -> 12.9 us  [swap(): lax.ppermute(x, BOTH, [(d, d ^ mask) for d, mask in enumerate(masks)])]
    unnamed x1 -> x0, matrix products: 5.28 us -> none
  transfers between devices with their start and end apart: 2 -> 7, of which waited for: 2 -> 7; matrix products, arithmetic and copies ran while one was open for 0% -> 0% of each run, Pallas kernels for 0% -> 0%
where the time goes in v1:
time: 76.2 us; the launch traced here: 76 us
  blocking collectives  31.6 us (41%)
  waiting for transfers between devices  15.9 us (21%)
  Pallas kernels  13.5 us (18%)
  starting transfers between devices  12.9 us (17%)
  local copies, waits for them, and re-layouts  1.66 us (2%)
    all_to_all x1, blocking collectives, on_device(): lax.all_to_all(sent, BOTH, 0, 0, tiled=True)  31.6 us
    ppermute x7, waiting for transfers between devices, swap(): lax.ppermute(x, BOTH, [(d, d ^ mask) for d, mask in enumerate(masks)])  15.9 us
    ppermute x7, starting transfers between devices, swap(): lax.ppermute(x, BOTH, [(d, d ^ mask) for d, mask in enumerate(masks)])  12.9 us
    pallas_call x1, Pallas kernels, on_device(): pl.pallas_call(functools.partial(fock_kernel, n_orb, n_dev, splits), in_s...  4.89 us
    pallas_call x1, Pallas kernels, on_device(): pl.pallas_call(functools.partial(half_kernel, n_rows, main), in_specs=[in...  4.73 us
    pallas_call x1, Pallas kernels, on_device(): pl.pallas_call(functools.partial(owner_kernel, n_rows, aux_step, q_loc, r...  2.41 us
  transfers between devices with their start and end apart: 7, of which 7 were waited for; matrix products, arithmetic and copies ran while one was open for 0% of the time, Pallas kernels for 0%

profile of v1, /device:TPU:0, one launch (start us, length us, event | category | flops | bytes accessed | tf_op | source)
XLA Modules:
  0.0 76.0 jit_solution(16002618681093217045)
XLA Ops:
  0.0 1.3 %copy-done = bf16[8,400,160]{1,2,0:T(8,128)(2,1)S(1)} copy-done((bf16[8,400,160]{1,2,0:T(8,128)(2,1)S(1)}, bf16[8,400,160]{1,2,0:T(8,128)(2,1)}, u32[]{:S(2)}) %copy-start) | copy-done | bytes 1024024
  1.3 4.9 %fock.1 = (f32[6,160,128]{2,1,0:T(8,128)S(1)}, bf16[6,160,128]{2,1,0:T(8,128)(2,1)S(1)}, bf16[8,400,1600]{2,1,0:T(8,128)(2,1)S(1)}) custom-call(bf16[8,400,1600]{2,1,0:T(8,128)(2,1)} %three_hbm.1, bf16[8,160,400]{2,1,0:T(8,128)(2,1)S(1)} %bitcast.5), custom_call_target="tpu_custom_call" | custom-call | flops 1638400000 | bytes 10240000 | tf_op jit(solution)/shard_map/fock/pallas_call | solution.py:240
  6.2 0.5 collective-permute-start
  6.8 1.1 %collective-permute-done = bf16[6,160,128]{2,1,0:T(8,128)(2,1)S(1)} collective-permute-done((bf16[6,160,128]{2,1,0:T(8,128)(2,1)S(1)}, bf16[6,160,128]{2,1,0:T(8,128)(2,1)S(1)}, u32[]{:S(2)}, u32[]{:S(2)}) %collective-permute-start) | collective-permute-done | bytes 245792 | tf_op jit(solution)/shard_map/ppermute | solution.py:33
  7.9 0.1 convert_add_fusion
  8.0 2.7 %collective-permute-start.1 = (bf16[3,160,128]{2,1,0:T(8,128)(2,1)S(1)}, bf16[3,160,128]{2,1,0:T(8,128)(2,1)S(1)}, u32[]{:S(2)}, u32[]{:S(2)}) collective-permute-start(bf16[3,160,128]{2,1,0:T(8,128)(2,1)S(1)} %slice.21), channel_id=1, source_target_pairs={{0,3},{1,4},{2,7},{3,0},{4,1},{5,6},{6,5},{7,2},{8,13},{9,10},{10,... | collective-permute-start | bytes 368648 | tf_op jit(solution)/shard_map/ppermute | solution.py:33
  10.6 2.6 %collective-permute-done.1 = bf16[3,160,128]{2,1,0:T(8,128)(2,1)S(1)} collective-permute-done((bf16[3,160,128]{2,1,0:T(8,128)(2,1)S(1)}, bf16[3,160,128]{2,1,0:T(8,128)(2,1)S(1)}, u32[]{:S(2)}, u32[]{:S(2)}) %collective-permute-start.1) | collective-permute-done | bytes 122912 | tf_op jit(solution)/shard_map/ppermute | solution.py:33
  13.2 1.8 %collective-permute-start.2 = (bf16[3,160,128]{2,1,0:T(8,128)(2,1)S(1)}, bf16[3,160,128]{2,1,0:T(8,128)(2,1)S(1)}, u32[]{:S(2)}, u32[]{:S(2)}) collective-permute-start(bf16[3,160,128]{2,1,0:T(8,128)(2,1)S(1)} %fusion.2), channel_id=1, source_target_pairs={{0,5},{1,2},{2,1},{3,6},{4,7},{5,0},{6,3},{7,4},{8,11},{9,12},{10,... | collective-permute-start | bytes 368648 | tf_op jit(solution)/shard_map/ppermute | solution.py:33
  15.1 2.6 %collective-permute-done.2 = bf16[3,160,128]{2,1,0:T(8,128)(2,1)S(1)} collective-permute-done((bf16[3,160,128]{2,1,0:T(8,128)(2,1)S(1)}, bf16[3,160,128]{2,1,0:T(8,128)(2,1)S(1)}, u32[]{:S(2)}, u32[]{:S(2)}) %collective-permute-start.2) | collective-permute-done | bytes 122912 | tf_op jit(solution)/shard_map/ppermute | solution.py:33
  17.7 1.9 %collective-permute-start.3 = (bf16[3,160,128]{2,1,0:T(8,128)(2,1)S(1)}, bf16[3,160,128]{2,1,0:T(8,128)(2,1)S(1)}, u32[]{:S(2)}, u32[]{:S(2)}) collective-permute-start(bf16[3,160,128]{2,1,0:T(8,128)(2,1)S(1)} %fusion), channel_id=1, source_target_pairs={{0,9},{1,16},{2,19},{3,10},{4,21},{5,12},{6,15},{7,22},{8,25},{9,0... | collective-permute-start | bytes 368648 | tf_op jit(solution)/shard_map/ppermute | solution.py:33
  19.6 3.1 %collective-permute-done.3 = bf16[3,160,128]{2,1,0:T(8,128)(2,1)S(1)} collective-permute-done((bf16[3,160,128]{2,1,0:T(8,128)(2,1)S(1)}, bf16[3,160,128]{2,1,0:T(8,128)(2,1)S(1)}, u32[]{:S(2)}, u32[]{:S(2)}) %collective-permute-start.3) | collective-permute-done | bytes 122912 | tf_op jit(solution)/shard_map/ppermute | solution.py:33
  22.6 0.1 fusion.1
  22.7 3.5 %collective-permute-start.4 = (bf16[3,160,128]{2,1,0:T(8,128)(2,1)S(1)}, bf16[3,160,128]{2,1,0:T(8,128)(2,1)S(1)}, u32[]{:S(2)}, u32[]{:S(2)}) collective-permute-start(bf16[3,160,128]{2,1,0:T(8,128)(2,1)S(1)} %fusion.1), channel_id=1, source_target_pairs={{0,17},{1,8},{2,11},{3,18},{4,13},{5,20},{6,23},{7,14},{8,1},{9,24... | collective-permute-start | bytes 368648 | tf_op jit(solution)/shard_map/ppermute | solution.py:33
  26.2 3.1 %collective-permute-done.4 = bf16[3,160,128]{2,1,0:T(8,128)(2,1)S(1)} collective-permute-done((bf16[3,160,128]{2,1,0:T(8,128)(2,1)S(1)}, bf16[3,160,128]{2,1,0:T(8,128)(2,1)S(1)}, u32[]{:S(2)}, u32[]{:S(2)}) %collective-permute-start.4) | collective-permute-done | bytes 122912 | tf_op jit(solution)/shard_map/ppermute | solution.py:33
  29.3 0.1 add_convert_fusion
  29.4 2.2 %collective-permute-start.5 = (bf16[3,160,128]{2,1,0:T(8,128)(2,1)S(1)}, bf16[3,160,128]{2,1,0:T(8,128)(2,1)S(1)}, u32[]{:S(2)}, u32[]{:S(2)}) collective-permute-start(bf16[3,160,128]{2,1,0:T(8,128)(2,1)S(1)} %add_convert_fusion), channel_id=1, source_target_pairs={{0,3},{1,4},{2,7},{3,0},{4,1},{5,6},{6,5},{7,2},{8,13},{9,10},{10,... | collective-permute-start | bytes 368648 | tf_op jit(solution)/shard_map/ppermute | solution.py:33
  31.6 2.6 %collective-permute-done.5 = bf16[3,160,128]{2,1,0:T(8,128)(2,1)S(1)} collective-permute-done((bf16[3,160,128]{2,1,0:T(8,128)(2,1)S(1)}, bf16[3,160,128]{2,1,0:T(8,128)(2,1)S(1)}, u32[]{:S(2)}, u32[]{:S(2)}) %collective-permute-start.5) | collective-permute-done | bytes 122912 | tf_op jit(solution)/shard_map/ppermute | solution.py:33
  34.2 0.3 collective-permute-start.6
  34.5 0.3 pad.4.hess_ref
  34.8 1.0 %collective-permute-done.6.other_ref = bf16[6,160,128]{2,1,0:T(8,128)(2,1)S(1)} collective-permute-done((bf16[6,160,128]{2,1,0:T(8,128)(2,1)S(1)}, bf16[6,160,128]{2,1,0:T(8,128)(2,1)S(1)}, u32[]{:S(2)}, u32[]{:S(2)}) %collective-permute-start.6) | collective-permute-done | bytes 245792 | tf_op jit(solution)/shard_map/ppermute | solution.py:33
  35.8 1.5 %rotation.1 = (bf16[160,1600]{1,0:T(8,128)(2,1)S(1)}, bf16[160,1664]{1,0:T(8,128)(2,1)S(1)}, bf16[160,1536]{1,0:T(8,128)(2,1)S(1)}) custom-call(bf16[6,160,128]{2,1,0:T(8,128)(2,1)S(1)} %pad_maximum_fusion.mine_ref, bf16[6,160,128]{2,1,0:T(8,128)(2,1)S(1)} %collective-permute-done.6.other_ref, f32[160,1536]{1,0:T(8,128)S(1)} %pad.4.hess_ref, ...), custom_call_target="tpu_custom_call" | custom-call | flops 327680000 | bytes 4194304 | tf_op jit(solution)/shard_map/rotation/pallas_call | solution.py:281
  37.2 4.7 %half_rotation.1 = bf16[32,128,128]{2,1,0:T(8,128)(2,1)S(1)} custom-call(bf16[160,1600]{1,0:T(8,128)(2,1)S(1)} %get-tuple-element.13.chosen_ref, bf16[8,400,1600]{2,1,0:T(8,128)(2,1)S(1)} %get-tuple-element.14.three_ref), custom_call_target="tpu_custom_call" | custom-call | flops 1638400000 | bytes 10240000 | tf_op jit(solution)/shard_map/half_rotation/pallas_call | solution.py:295
  42.0 31.6 %all_to_all.5 = bf16[32,128,128]{2,1,0:T(8,128)(2,1)S(1)} all-to-all(bf16[32,128,128]{2,1,0:T(8,128)(2,1)S(1)} %half_rotation.1), channel_id=1, replica_groups=mesh['aux'=8,'orb'=4] {'aux','orb'}, dimensions={0} | all-to-all | bytes 2097152 | tf_op jit(solution)/shard_map/all_to_all | solution.py:310
  73.6 2.4 %owner_rows.1 = bf16[64,7200]{1,0:T(8,128)(2,1)} custom-call(bf16[8,4,128,128]{3,2,1,0:T(8,128)(2,1)S(1)} %bitcast.4, bf16[160,1664]{1,0:T(8,128)(2,1)S(1)} %get-tuple-element.15.left_ref, bf16[160,1536]{1,0:T(8,128)(2,1)S(1)} %get-tuple-element.16.rot_ref), custom_call_target="tpu_custom_call" | custom-call | flops 327680000 | bytes 8388608 | tf_op jit(solution)/shard_map/owner_rows/pallas_call | solution.py:312
  (9 shorter events, 0.1 us)
Async XLA Ops:
  0.0 1.3 %copy-start = (bf16[8,400,160]{1,2,0:T(8,128)(2,1)S(1)}, bf16[8,400,160]{1,2,0:T(8,128)(2,1)}, u32[]{:S(2)}) copy-start(bf16[8,400,160]{1,2,0:T(8,128)(2,1)} %param.5) | copy-start | bytes 3072004
  1.3 33.2 %copy-start.2 = (f32[1440,160]{0,1:T(8,128)S(1)}, f32[1440,160]{0,1:T(8,128)}, u32[]{:S(2)}) copy-start(f32[1440,160]{0,1:T(8,128)} %param.6) | copy-start | bytes 2764804
  1.3 34.4 %copy-start.1 = (bf16[160,160]{1,0:T(8,128)(2,1)S(1)}, bf16[160,160]{1,0:T(8,128)(2,1)}, u32[]{:S(2)}) copy-start(bf16[160,160]{1,0:T(8,128)(2,1)} %constant.4.clone.sel_ref) | copy-start | bytes 153604
  6.2 1.7 %collective-permute-start = (bf16[6,160,128]{2,1,0:T(8,128)(2,1)S(1)}, bf16[6,160,128]{2,1,0:T(8,128)(2,1)S(1)}, u32[]{:S(2)}, u32[]{:S(2)}) collective-permute-start(bf16[6,160,128]{2,1,0:T(8,128)(2,1)S(1)} %get-tuple-element.12), channel_id=1, source_target_pairs={{0,1},{1,0},{2,3},{3,2},{4,5},{5,4},{6,7},{7,6},{8,9},{9,8},{10,11... | collective-permute-start | bytes 737288 | tf_op jit(solution)/shard_map/ppermute | solution.py:33
  8.0 5.2 %collective-permute-start.1 = (bf16[3,160,128]{2,1,0:T(8,128)(2,1)S(1)}, bf16[3,160,128]{2,1,0:T(8,128)(2,1)S(1)}, u32[]{:S(2)}, u32[]{:S(2)}) collective-permute-start(bf16[3,160,128]{2,1,0:T(8,128)(2,1)S(1)} %slice.21), channel_id=1, source_target_pairs={{0,3},{1,4},{2,7},{3,0},{4,1},{5,6},{6,5},{7,2},{8,13},{9,10},{10,... | collective-permute-start | bytes 368648 | tf_op jit(solution)/shard_map/ppermute | solution.py:33
  13.2 4.4 %collective-permute-start.2 = (bf16[3,160,128]{2,1,0:T(8,128)(2,1)S(1)}, bf16[3,160,128]{2,1,0:T(8,128)(2,1)S(1)}, u32[]{:S(2)}, u32[]{:S(2)}) collective-permute-start(bf16[3,160,128]{2,1,0:T(8,128)(2,1)S(1)} %fusion.2), channel_id=1, source_target_pairs={{0,5},{1,2},{2,1},{3,6},{4,7},{5,0},{6,3},{7,4},{8,11},{9,12},{10,... | collective-permute-start | bytes 368648 | tf_op jit(solution)/shard_map/ppermute | solution.py:33
  17.7 4.9 %collective-permute-start.3 = (bf16[3,160,128]{2,1,0:T(8,128)(2,1)S(1)}, bf16[3,160,128]{2,1,0:T(8,128)(2,1)S(1)}, u32[]{:S(2)}, u32[]{:S(2)}) collective-permute-start(bf16[3,160,128]{2,1,0:T(8,128)(2,1)S(1)} %fusion), channel_id=1, source_target_pairs={{0,9},{1,16},{2,19},{3,10},{4,21},{5,12},{6,15},{7,22},{8,25},{9,0... | collective-permute-start | bytes 368648 | tf_op jit(solution)/shard_map/ppermute | solution.py:33
  22.7 6.6 %collective-permute-start.4 = (bf16[3,160,128]{2,1,0:T(8,128)(2,1)S(1)}, bf16[3,160,128]{2,1,0:T(8,128)(2,1)S(1)}, u32[]{:S(2)}, u32[]{:S(2)}) collective-permute-start(bf16[3,160,128]{2,1,0:T(8,128)(2,1)S(1)} %fusion.1), channel_id=1, source_target_pairs={{0,17},{1,8},{2,11},{3,18},{4,13},{5,20},{6,23},{7,14},{8,1},{9,24... | collective-permute-start | bytes 368648 | tf_op jit(solution)/shard_map/ppermute | solution.py:33
  29.4 4.8 %collective-permute-start.5 = (bf16[3,160,128]{2,1,0:T(8,128)(2,1)S(1)}, bf16[3,160,128]{2,1,0:T(8,128)(2,1)S(1)}, u32[]{:S(2)}, u32[]{:S(2)}) collective-permute-start(bf16[3,160,128]{2,1,0:T(8,128)(2,1)S(1)} %add_convert_fusion), channel_id=1, source_target_pairs={{0,3},{1,4},{2,7},{3,0},{4,1},{5,6},{6,5},{7,2},{8,13},{9,10},{10,... | collective-permute-start | bytes 368648 | tf_op jit(solution)/shard_map/ppermute | solution.py:33
  34.2 1.6 %collective-permute-start.6 = (bf16[6,160,128]{2,1,0:T(8,128)(2,1)S(1)}, bf16[6,160,128]{2,1,0:T(8,128)(2,1)S(1)}, u32[]{:S(2)}, u32[]{:S(2)}) collective-permute-start(bf16[6,160,128]{2,1,0:T(8,128)(2,1)S(1)} %pad_maximum_fusion.mine_ref), channel_id=1, source_target_pairs={{0,1},{1,0},{2,3},{3,2},{4,5},{5,4},{6,7},{7,6},{8,9},{9,8},{10,11... | collective-permute-start | bytes 737288 | tf_op jit(solution)/shard_map/ppermute | solution.py:33

commit v2 on v1

--- a/solution.py
+++ b/solution.py
@@ -83,10 +83,11 @@
     return tiles
 
 
-def fock_kernel(n_orb, n_dev, splits, three_hbm, dens_ref, keep_ref, send_ref, three_ref, acc_ref, sems):
-    n_tiles = acc_ref.shape[0]
+def fock_kernel(n_orb, n_dev, tracks, three_hbm, dens_ref, *refs):
+    *part_refs, three_ref, acc_ref, sems = refs
     q_loc, _, n_mo = three_ref.shape
     n_occ = dens_ref.shape[1]
+    n_tiles = acc_ref.shape[0] // n_occ
     base = n_occ // LANES * LANES
     copies = []
     for q in range(q_loc):
@@ -97,37 +98,42 @@
         part = matmul(dens_ref[q], three_ref[q, :, base:], NN)
         for t in range(n_tiles):
             stop = min(LANES, n_mo - base - t * LANES)
+            rows = slice(t * n_occ, (t + 1) * n_occ)
             piece = part[:, t * LANES : t * LANES + stop]
             if q:
-                acc_ref[t, :, :stop] += piece
+                acc_ref[rows, :stop] += piece
             else:
                 if stop < LANES:
-                    acc_ref[t] = jnp.zeros(acc_ref.shape[1:], F32)
-                acc_ref[t, :, :stop] = piece
+                    acc_ref[rows, :] = jnp.zeros((n_occ, LANES), F32)
+                acc_ref[rows, :stop] = piece
     me = my_index(n_orb)
     mine = half_of(me, n_dev)
-    half, quarter = n_tiles // 2, n_tiles // 4
-    for ref, side in ((keep_ref, mine), (send_ref, 1 - mine)):
-        lead = jnp.where(side == 0, bit(me, splits[0]), bit(me, splits[1]))
-        for j in range(half):
-            first = jnp.where(lead == j // quarter, 0, quarter)
-            ref[j] = acc_ref[side * half + first + j % quarter].astype(ref.dtype)
-
-
-def rotation_kernel(n_orb, n_dev, splits, mine_ref, other_ref, hess_ref, sel_ref, chosen_ref, left_ref, rot_ref, fock_ref, u_ref):
+    n_rows = n_tiles * n_occ // 8
+    for chain in (0, 1):
+        for ref, side in zip(part_refs[chain::2], (mine, 1 - mine)):
+            lead = jnp.where(side == 0, bit(me, tracks[0][0]), bit(me, tracks[1][0]))
+            for j in (0, 1):
+                start = pl.multiple_of((side * 4 + chain * 2 + (lead + j) % 2) * n_rows, n_rows)
+                ref[j] = acc_ref[pl.ds(start, n_rows), :].astype(ref.dtype)
+
+
+def rotation_kernel(n_orb, n_dev, tracks, mine_0, mine_1, other_0, other_1, hess_ref, sel_ref, chosen_ref, left_ref, rot_ref, fock_ref, u_ref):
     n_occ, width = fock_ref.shape
-    half = mine_ref.shape[0]
-    quarter = half // 2
     base = n_occ // LANES * LANES
-    n_mo = chosen_ref.shape[1]
+    n_mo = chosen_ref.shape[0]
+    mine_refs, other_refs = (mine_0, mine_1), (other_0, other_1)
+    n_rows = mine_0.shape[1]
+    step = math.gcd(n_rows, n_occ)
     me = my_index(n_orb)
     mine = half_of(me, n_dev)
-    for t in range(2 * half):
-        side = t // half
-        first = jnp.where(bit(me, splits[side]) == t % half // quarter, 0, quarter)
-        at = first + t % quarter
-        fock_ref[:, t * LANES : (t + 1) * LANES] = jnp.where(
-            mine == side, mine_ref[at].astype(F32), other_ref[at].astype(F32))
+    for start in range(0, 8 * n_rows, step):
+        tile, row = divmod(start, n_occ)
+        piece, at = divmod(start, n_rows)
+        side, chain, j = piece // 4, piece // 2 % 2, piece % 2
+        place = (j + bit(me, tracks[side][0])) % 2
+        rows = slice(at, at + step)
+        fock_ref[row : row + step, tile * LANES : (tile + 1) * LANES] = jnp.where(
+            mine == side, mine_refs[chain][place, rows, :].astype(F32), other_refs[chain][place, rows, :].astype(F32))
     gen = -fock_ref[...] / hess_ref[...]
     square = jnp.sum(jnp.sum(gen * gen, axis=0, keepdims=True), axis=1, keepdims=True)
     rot = gen * jnp.minimum(1.0, math.sqrt(n_occ) / jnp.sqrt(square))
@@ -148,27 +154,49 @@
     left_ref[:, :base] = l_oo[:, :base]
     left_ref[:, base:] = (over_rot / 24.0 - rot / 2.0).astype(BF16)
     left_ref[:, base:n_occ] = l_oo[:, base:]
-    chosen_ref[...] = matmul(sel_ref[...], u_ref[:, :n_mo], NN).astype(BF16)
+    chosen = matmul(sel_ref[...], u_ref[...], NN)
+    chosen_ref[...] = chosen.T[:n_mo].astype(BF16)
+
+
+def swap_rows(tiles):
+    row = lax.broadcasted_iota(jnp.int32, tiles[0].shape, 0)
+    for step in (1, 2, 4):
+        low = (row // step) % 2 == 0
+        after = list(tiles)
+        for t in range(8):
+            if t & step == 0:
+                first, second = tiles[t], tiles[t | step]
+                after[t] = jnp.where(low, first, pltpu.roll(second, step, 0))
+                after[t | step] = jnp.where(low, pltpu.roll(first, 8 - step, 0), second)
+        tiles = after
+    return tiles
 
 
 def half_kernel(n_rows, main, chosen_ref, three_ref, sent_ref, rem_ref, half_ref):
     q_loc, r_loc, n_mo = three_ref.shape
     rem = r_loc - main
     n_dev, dest_rows = sent_ref.shape[:2]
-
-    def store(value, row):
-        for k in range(n_rows):
-            half_ref[pl.ds(row(k), n_dev, stride=dest_rows), :] = value[k * n_dev : (k + 1) * n_dev, :]
-
-    chosen = chosen_ref[...]
     for q in range(q_loc):
-        product = matmul(chosen, three_ref[q, :main, :], NT)
-        for c in range(main // LANES):
-            store(product[:, c * LANES : (c + 1) * LANES], lambda k, c=c, q=q: (c * n_rows + k) * q_loc + q)
-        rem_ref[q * rem : (q + 1) * rem, :] = three_ref[q, main:, :]
-    store(matmul(chosen, rem_ref[...], NT), lambda k: main // LANES * n_rows * q_loc + k)
-    for d in range(n_dev):
-        sent_ref[d] = half_ref[d * dest_rows : (d + 1) * dest_rows, :].astype(BF16)
+        product = matmul(three_ref[q], chosen_ref[...], NN)
+        half_ref[q] = product[:main].T
+        rem_ref[q * rem : (q + 1) * rem, :] = product[main:]
+    turned = rem_ref[...].T
+
+    def group(at, dest):
+        tile, k = divmod(at, n_rows)
+        if tile < main // LANES:
+            rows = slice(k * n_dev + dest, k * n_dev + dest + 8)
+            return swap_rows([half_ref[q, rows, tile * LANES : (tile + 1) * LANES] for q in range(q_loc)])
+        zero = jnp.zeros((8, LANES), F32)
+        if at > main // LANES * n_rows:
+            return [zero] * 8
+        rest = [turned[k * n_dev + dest : k * n_dev + dest + 8, :] for k in range(n_rows)]
+        return swap_rows(rest + [zero] * (8 - n_rows))
+
+    for dest in range(0, n_dev, 8):
+        for at in range(0, dest_rows // 8, 2):
+            for d, pair in enumerate(zip(group(at, dest), group(at + 1, dest))):
+                sent_ref[dest + d, at * 8 : at * 8 + 16, :] = jnp.concatenate(pair, 0).astype(BF16)
 
 
 def owner_kernel(n_rows, n_aux, q_loc, r_loc, main, got_ref, left_ref, rot_ref, out_ref):
@@ -231,23 +259,24 @@
     main = r_loc // LANES * LANES
     assert n_dev & (n_dev - 1) == 0 and n_dev >= 8 and tiles % 4 == 0
     tracks = tracks_of(n_dev)
-    splits = (tracks[0][0], tracks[1][0])
     whole = lambda *shape: pl.BlockSpec(shape, lambda *_: (0,) * len(shape))
     in_vmem = pl.BlockSpec(memory_space=pltpu.VMEM)
 
-    half_shape = (tiles // 2, n_occ, LANES)
+    half_shape = (2, tiles * n_occ // 8, LANES)
     in_hbm = pl.BlockSpec(memory_space=pltpu.HBM)
-    keep, send, three_vmem = pl.pallas_call(
-        functools.partial(fock_kernel, n_orb, n_dev, splits),
+    *parts, three_vmem = pl.pallas_call(
+        functools.partial(fock_kernel, n_orb, n_dev, tracks),
         in_specs=[in_hbm, in_vmem],
-        out_specs=[in_vmem] * 3,
+        out_specs=[in_vmem] * 5,
         out_shape=[
             jax.ShapeDtypeStruct(half_shape, F32),
+            jax.ShapeDtypeStruct(half_shape, F32),
+            jax.ShapeDtypeStruct(half_shape, BF16),
             jax.ShapeDtypeStruct(half_shape, BF16),
             jax.ShapeDtypeStruct(three_index.shape, BF16),
         ],
         scratch_shapes=[
-            pltpu.VMEM((tiles, n_occ, LANES), F32),
+            pltpu.VMEM((tiles * n_occ, LANES), F32),
             pltpu.SemaphoreType.DMA((q_loc,)),
         ],
         compiler_params=pltpu.CompilerParams(vmem_limit_bytes=38 * MIB),
@@ -259,14 +288,17 @@
         hess_diag.T, ((0, 0), (n_occ - base, width - (n_mo - base))), constant_values=jnp.inf)
 
     masks = [[1 | 1 << tracks[half_of(d, n_dev)][k] for d in range(n_dev)] for k in range(len(tracks[0]))]
-    part = keep + swap(send, [1] * n_dev).astype(F32)
-    part = part[: tiles // 4] + swap(part[tiles // 4 :].astype(BF16), masks[0]).astype(F32)
-    for mask in masks[1:]:
-        part = part + swap(part.astype(BF16), mask).astype(F32)
-    part = part.astype(BF16)
-    held = jnp.concatenate([part, swap(part, masks[0])], 0)
-    other = swap(held, [1] * n_dev)
-
+    held, other = [], []
+    for chain in (0, 1):
+        part = parts[chain] + swap(parts[2 + chain], [1] * n_dev).astype(F32)
+        piece = part[0] + swap(part[1].astype(BF16), masks[0]).astype(F32)
+        for mask in masks[1:]:
+            piece = piece + swap(piece.astype(BF16), mask).astype(F32)
+        piece = piece.astype(BF16)
+        held.append(jnp.stack([piece, swap(piece, masks[0])]))
+        other.append(swap(held[chain], [1] * n_dev))
+
+    assert q_loc == 8
     first = [p * pairs // n_vir for p in range(n_aux)]
     n_rows = max(-(-(p + 1) * pairs // n_vir) - first[p] for p in range(n_aux))
     sel = np.zeros((n_rows, n_aux, n_orb, n_occ), np.float32)
@@ -279,11 +311,11 @@
     dest_rows = -(-(main // LANES * n_rows * q_loc + n_rows) // 16) * 16
     wide = base + width
     chosen, left, rot = pl.pallas_call(
-        functools.partial(rotation_kernel, n_orb, n_dev, splits),
-        in_specs=[in_vmem] * 4,
+        functools.partial(rotation_kernel, n_orb, n_dev, tracks),
+        in_specs=[in_vmem] * 6,
         out_specs=[in_vmem] * 3,
         out_shape=[
-            jax.ShapeDtypeStruct((n_rows * n_dev, n_mo), BF16),
+            jax.ShapeDtypeStruct((n_mo, n_rows * n_dev), BF16),
             jax.ShapeDtypeStruct((n_occ, wide), BF16),
             jax.ShapeDtypeStruct((n_occ, width), BF16),
         ],
@@ -291,15 +323,15 @@
         compiler_params=pltpu.CompilerParams(vmem_limit_bytes=16 * MIB),
         cost_estimate=pl.CostEstimate(flops=8 * n_occ * n_occ * n_mo, bytes_accessed=4 * MIB, transcendentals=0),
         name="rotation",
-    )(held, other, hess, sel)
+    )(*held, *other, hess, sel)
     sent = pl.pallas_call(
         functools.partial(half_kernel, n_rows, main),
         in_specs=[in_vmem] * 2,
         out_specs=in_vmem,
         out_shape=jax.ShapeDtypeStruct((n_dev, dest_rows, LANES), BF16),
         scratch_shapes=[
-            pltpu.VMEM((q_loc * (r_loc - main), n_mo), BF16),
-            pltpu.VMEM((n_dev * dest_rows, LANES), F32),
+            pltpu.VMEM((q_loc * (r_loc - main), n_rows * n_dev), F32),
+            pltpu.VMEM((q_loc, n_rows * n_dev, main), F32),
         ],
         compiler_params=pltpu.CompilerParams(vmem_limit_bytes=40 * MIB),
         cost_estimate=pl.CostEstimate(

time: 76.2 us -> 72.2 us (0.948)
  waiting for transfers between devices: 15.9 us -> 7.67 us
  starting transfers between devices: 12.9 us -> 18.6 us
  Pallas kernels: 13.5 us -> 12.4 us
    ppermute x7 -> x14, waiting for transfers between devices: 15.9 us -> 7.67 us  [swap(): lax.ppermute(x, BOTH, [(d, d ^ mask) for d, mask in enumerate(masks)])]
    ppermute x7 -> x14, starting transfers between devices: 12.9 us -> 18.6 us  [swap(): lax.ppermute(x, BOTH, [(d, d ^ mask) for d, mask in enumerate(masks)])]
    pallas_call x1, Pallas kernels: 4.73 us -> 3.47 us  [on_device(): pl.pallas_call(functools.partial(half_kernel, n_rows, main), in_specs=[in...]
  transfers between devices with their start and end apart: 7 -> 14, of which waited for: 7 -> 10; matrix products, arithmetic and copies ran while one was open for 0% -> 1% of each run, Pallas kernels for 0% -> 0%
where the time goes in v2:
time: 72.2 us; the launch traced here: 72.1 us
  blocking collectives  31.3 us (43%)
  starting transfers between devices  18.6 us (26%)
  Pallas kernels  12.4 us (17%)
  waiting for transfers between devices  7.67 us (11%)
  local copies, waits for them, and re-layouts  1.66 us (2%)
    all_to_all x1, blocking collectives, on_device(): lax.all_to_all(sent, BOTH, 0, 0, tiled=True)  31.3 us
    ppermute x14, starting transfers between devices, swap(): lax.ppermute(x, BOTH, [(d, d ^ mask) for d, mask in enumerate(masks)])  18.6 us
    ppermute x14, waiting for transfers between devices, swap(): lax.ppermute(x, BOTH, [(d, d ^ mask) for d, mask in enumerate(masks)])  7.67 us
    pallas_call x1, Pallas kernels, on_device(): pl.pallas_call(functools.partial(fock_kernel, n_orb, n_dev, tracks), in_s...  4.89 us
    pallas_call x1, Pallas kernels, on_device(): pl.pallas_call(functools.partial(half_kernel, n_rows, main), in_specs=[in...  3.47 us
    pallas_call x1, Pallas kernels, on_device(): pl.pallas_call(functools.partial(owner_kernel, n_rows, aux_step, q_loc, r...  2.41 us
    pallas_call x1, Pallas kernels, on_device(): pl.pallas_call(functools.partial(rotation_kernel, n_orb, n_dev, tracks),...  1.61 us
  transfers between devices with their start and end apart: 14, of which 10 were waited for; matrix products, arithmetic and copies ran while one was open for 1% of the time, Pallas kernels for 0%

profile of v2, /device:TPU:0, one launch (start us, length us, event | category | flops | bytes accessed | tf_op | source)
XLA Modules:
  0.0 72.1 jit_solution(3351144083598870244)
XLA Ops:
  0.0 1.3 %copy-done = bf16[8,400,160]{1,2,0:T(8,128)(2,1)S(1)} copy-done((bf16[8,400,160]{1,2,0:T(8,128)(2,1)S(1)}, bf16[8,400,160]{1,2,0:T(8,128)(2,1)}, u32[]{:S(2)}) %copy-start) | copy-done | bytes 1024024
  1.3 4.9 %fock.1 = (f32[2,240,128]{2,1,0:T(8,128)S(1)}, f32[2,240,128]{2,1,0:T(8,128)S(1)}, bf16[2,240,128]{2,1,0:T(8,128)(2,1)S(1)}, bf16[2,240,128]{2,1,0:T(8,128)(2,1)S(1)}, bf16[8,400,1600]{2,1,0:T(8,128)(2,1)S(1)}) custom-call(bf16[8,400,1600]{2,1,0:T(8,128)(2,1)} %three_hbm.1, bf16[8,160,400]{2,1,0:T(8,128)(2,1)S(1)} %bitcast.37), custom_call_target="tpu_custom_call" | custom-call | flops 1638400000 | bytes 10240000 | tf_op jit(solution)/shard_map/fock/pallas_call | solution.py:267
  6.2 0.5 collective-permute-start
  6.8 0.9 %collective-permute-done = bf16[2,240,128]{2,1,0:T(8,128)(2,1)S(1)} collective-permute-done((bf16[2,240,128]{2,1,0:T(8,128)(2,1)S(1)}, bf16[2,240,128]{2,1,0:T(8,128)(2,1)S(1)}, u32[]{:S(2)}, u32[]{:S(2)}) %collective-permute-start) | collective-permute-done | bytes 122912 | tf_op jit(solution)/shard_map/ppermute | solution.py:33
  7.8 2.7 %collective-permute-start.1 = (bf16[240,128]{1,0:T(8,128)(2,1)S(1)}, bf16[240,128]{1,0:T(8,128)(2,1)S(1)}, u32[]{:S(2)}, u32[]{:S(2)}) collective-permute-start(bf16[240,128]{1,0:T(8,128)(2,1)S(1)} %fusion.4), channel_id=1, source_target_pairs={{0,3},{1,4},{2,7},{3,0},{4,1},{5,6},{6,5},{7,2},{8,13},{9,10},{10,... | collective-permute-start | bytes 184328 | tf_op jit(solution)/shard_map/ppermute | solution.py:33
  10.8 1.5 %collective-permute-done.1 = bf16[240,128]{1,0:T(8,128)(2,1)S(1)} collective-permute-done((bf16[240,128]{1,0:T(8,128)(2,1)S(1)}, bf16[240,128]{1,0:T(8,128)(2,1)S(1)}, u32[]{:S(2)}, u32[]{:S(2)}) %collective-permute-start.1) | collective-permute-done | bytes 61472 | tf_op jit(solution)/shard_map/ppermute | solution.py:33
  12.4 2.1 %collective-permute-start.2 = (bf16[240,128]{1,0:T(8,128)(2,1)S(1)}, bf16[240,128]{1,0:T(8,128)(2,1)S(1)}, u32[]{:S(2)}, u32[]{:S(2)}) collective-permute-start(bf16[240,128]{1,0:T(8,128)(2,1)S(1)} %fusion.8), channel_id=1, source_target_pairs={{0,5},{1,2},{2,1},{3,6},{4,7},{5,0},{6,3},{7,4},{8,11},{9,12},{10,... | collective-permute-start | bytes 184328 | tf_op jit(solution)/shard_map/ppermute | solution.py:33
  14.5 1.3 %collective-permute-start.8 = (bf16[240,128]{1,0:T(8,128)(2,1)S(1)}, bf16[240,128]{1,0:T(8,128)(2,1)S(1)}, u32[]{:S(2)}, u32[]{:S(2)}) collective-permute-start(bf16[240,128]{1,0:T(8,128)(2,1)S(1)} %fusion.9), channel_id=1, source_target_pairs={{0,5},{1,2},{2,1},{3,6},{4,7},{5,0},{6,3},{7,4},{8,11},{9,12},{10,... | collective-permute-start | bytes 184328 | tf_op jit(solution)/shard_map/ppermute | solution.py:33
  15.8 0.6 collective-permute-done.2
  16.4 1.6 %collective-permute-start.3 = (bf16[240,128]{1,0:T(8,128)(2,1)S(1)}, bf16[240,128]{1,0:T(8,128)(2,1)S(1)}, u32[]{:S(2)}, u32[]{:S(2)}) collective-permute-start(bf16[240,128]{1,0:T(8,128)(2,1)S(1)} %fusion.2), channel_id=1, source_target_pairs={{0,9},{1,16},{2,19},{3,10},{4,21},{5,12},{6,15},{7,22},{8,25},{9,0... | collective-permute-start | bytes 184328 | tf_op jit(solution)/shard_map/ppermute | solution.py:33
  18.3 1.3 %collective-permute-start.9 = (bf16[240,128]{1,0:T(8,128)(2,1)S(1)}, bf16[240,128]{1,0:T(8,128)(2,1)S(1)}, u32[]{:S(2)}, u32[]{:S(2)}) collective-permute-start(bf16[240,128]{1,0:T(8,128)(2,1)S(1)} %fusion.3), channel_id=1, source_target_pairs={{0,9},{1,16},{2,19},{3,10},{4,21},{5,12},{6,15},{7,22},{8,25},{9,0... | collective-permute-start | bytes 184328 | tf_op jit(solution)/shard_map/ppermute | solution.py:33
  19.6 0.6 collective-permute-done.3
  20.2 3.1 %collective-permute-start.4 = (bf16[240,128]{1,0:T(8,128)(2,1)S(1)}, bf16[240,128]{1,0:T(8,128)(2,1)S(1)}, u32[]{:S(2)}, u32[]{:S(2)}) collective-permute-start(bf16[240,128]{1,0:T(8,128)(2,1)S(1)} %fusion.6), channel_id=1, source_target_pairs={{0,17},{1,8},{2,11},{3,18},{4,13},{5,20},{6,23},{7,14},{8,1},{9,24... | collective-permute-start | bytes 184328 | tf_op jit(solution)/shard_map/ppermute | solution.py:33
  23.3 1.8 %collective-permute-start.10 = (bf16[240,128]{1,0:T(8,128)(2,1)S(1)}, bf16[240,128]{1,0:T(8,128)(2,1)S(1)}, u32[]{:S(2)}, u32[]{:S(2)}) collective-permute-start(bf16[240,128]{1,0:T(8,128)(2,1)S(1)} %fusion.7), channel_id=1, source_target_pairs={{0,17},{1,8},{2,11},{3,18},{4,13},{5,20},{6,23},{7,14},{8,1},{9,24... | collective-permute-start | bytes 184328 | tf_op jit(solution)/shard_map/ppermute | solution.py:33
  25.1 0.6 collective-permute-done.4
  25.7 1.9 %collective-permute-start.5 = (bf16[240,128]{1,0:T(8,128)(2,1)S(1)}, bf16[240,128]{1,0:T(8,128)(2,1)S(1)}, u32[]{:S(2)}, u32[]{:S(2)}) collective-permute-start(bf16[240,128]{1,0:T(8,128)(2,1)S(1)} %add_convert_fusion.1), channel_id=1, source_target_pairs={{0,3},{1,4},{2,7},{3,0},{4,1},{5,6},{6,5},{7,2},{8,13},{9,10},{10,... | collective-permute-start | bytes 184328 | tf_op jit(solution)/shard_map/ppermute | solution.py:33
  28.0 1.3 %collective-permute-start.11 = (bf16[240,128]{1,0:T(8,128)(2,1)S(1)}, bf16[240,128]{1,0:T(8,128)(2,1)S(1)}, u32[]{:S(2)}, u32[]{:S(2)}) collective-permute-start(bf16[240,128]{1,0:T(8,128)(2,1)S(1)} %add_convert_fusion), channel_id=1, source_target_pairs={{0,3},{1,4},{2,7},{3,0},{4,1},{5,6},{6,5},{7,2},{8,13},{9,10},{10,... | collective-permute-start | bytes 184328 | tf_op jit(solution)/shard_map/ppermute | solution.py:33
  29.7 2.1 %collective-permute-done.11 = bf16[240,128]{1,0:T(8,128)(2,1)S(1)} collective-permute-done((bf16[240,128]{1,0:T(8,128)(2,1)S(1)}, bf16[240,128]{1,0:T(8,128)(2,1)S(1)}, u32[]{:S(2)}, u32[]{:S(2)}) %collective-permute-start.11) | collective-permute-done | bytes 61472 | tf_op jit(solution)/shard_map/ppermute | solution.py:33
  31.8 0.5 collective-permute-start.13
  32.6 0.6 collective-permute-done.13.other_1
  33.2 1.6 %rotation.1 = (bf16[1600,160]{1,0:T(8,128)(2,1)S(1)}, bf16[160,1664]{1,0:T(8,128)(2,1)S(1)}, bf16[160,1536]{1,0:T(8,128)(2,1)S(1)}) custom-call(bf16[2,240,128]{2,1,0:T(8,128)(2,1)S(1)} %pad_maximum_fusion.mine_0, bf16[2,240,128]{2,1,0:T(8,128)(2,1)S(1)} %pad_maximum_fusion.1.mine_1, bf16[2,240,128]{2,1,0:T(8,128)(2,1)S(1)} %collective-permute-done.12.other_0, ...), custom_call_target="tpu_custom_call" | custom-call | flops 327680000 | bytes 4194304 | tf_op jit(solution)/shard_map/rotation/pallas_call | solution.py:313
  34.9 3.5 %half_rotation.1 = bf16[32,128,128]{2,1,0:T(8,128)(2,1)S(1)} custom-call(bf16[1600,160]{1,0:T(8,128)(2,1)S(1)} %get-tuple-element.17.chosen_ref, bf16[8,400,1600]{2,1,0:T(8,128)(2,1)S(1)} %get-tuple-element.18.three_ref), custom_call_target="tpu_custom_call" | custom-call | flops 1638400000 | bytes 10240000 | tf_op jit(solution)/shard_map/half_rotation/pallas_call | solution.py:327
  38.3 31.3 %all_to_all.5 = bf16[32,128,128]{2,1,0:T(8,128)(2,1)S(1)} all-to-all(bf16[32,128,128]{2,1,0:T(8,128)(2,1)S(1)} %half_rotation.1), channel_id=1, replica_groups=mesh['aux'=8,'orb'=4] {'aux','orb'}, dimensions={0} | all-to-all | bytes 2097152 | tf_op jit(solution)/shard_map/all_to_all | solution.py:342
  69.7 2.4 %owner_rows.1 = bf16[64,7200]{1,0:T(8,128)(2,1)} custom-call(bf16[8,4,128,128]{3,2,1,0:T(8,128)(2,1)S(1)} %bitcast.36, bf16[160,1664]{1,0:T(8,128)(2,1)S(1)} %get-tuple-element.19.left_ref, bf16[160,1536]{1,0:T(8,128)(2,1)S(1)} %get-tuple-element.20.rot_ref), custom_call_target="tpu_custom_call" | custom-call | flops 327680000 | bytes 8388608 | tf_op jit(solution)/shard_map/owner_rows/pallas_call | solution.py:344
  (30 shorter events, 2.0 us)
Async XLA Ops:
  0.0 1.3 %copy-start = (bf16[8,400,160]{1,2,0:T(8,128)(2,1)S(1)}, bf16[8,400,160]{1,2,0:T(8,128)(2,1)}, u32[]{:S(2)}) copy-start(bf16[8,400,160]{1,2,0:T(8,128)(2,1)} %param.5) | copy-start | bytes 3072004
  1.3 30.9 %copy-start.2 = (f32[1440,160]{0,1:T(8,128)S(1)}, f32[1440,160]{0,1:T(8,128)}, u32[]{:S(2)}) copy-start(f32[1440,160]{0,1:T(8,128)} %param.6) | copy-start | bytes 2764804
  1.3 31.9 %copy-start.1 = (bf16[160,160]{1,0:T(8,128)(2,1)S(1)}, bf16[160,160]{1,0:T(8,128)(2,1)}, u32[]{:S(2)}) copy-start(bf16[160,160]{1,0:T(8,128)(2,1)} %constant.4.clone.sel_ref) | copy-start | bytes 153604
  6.2 1.5 %collective-permute-start = (bf16[2,240,128]{2,1,0:T(8,128)(2,1)S(1)}, bf16[2,240,128]{2,1,0:T(8,128)(2,1)S(1)}, u32[]{:S(2)}, u32[]{:S(2)}) collective-permute-start(bf16[2,240,128]{2,1,0:T(8,128)(2,1)S(1)} %get-tuple-element.14), channel_id=1, source_target_pairs={{0,1},{1,0},{2,3},{3,2},{4,5},{5,4},{6,7},{7,6},{8,9},{9,8},{10,11... | collective-permute-start | bytes 368648 | tf_op jit(solution)/shard_map/ppermute | solution.py:33
  6.8 3.7 %collective-permute-start.6 = (bf16[2,240,128]{2,1,0:T(8,128)(2,1)S(1)}, bf16[2,240,128]{2,1,0:T(8,128)(2,1)S(1)}, u32[]{:S(2)}, u32[]{:S(2)}) collective-permute-start(bf16[2,240,128]{2,1,0:T(8,128)(2,1)S(1)} %get-tuple-element.16), channel_id=1, source_target_pairs={{0,1},{1,0},{2,3},{3,2},{4,5},{5,4},{6,7},{7,6},{8,9},{9,8},{10,11... | collective-permute-start | bytes 368648 | tf_op jit(solution)/shard_map/ppermute | solution.py:33
  7.8 4.6 %collective-permute-start.1 = (bf16[240,128]{1,0:T(8,128)(2,1)S(1)}, bf16[240,128]{1,0:T(8,128)(2,1)S(1)}, u32[]{:S(2)}, u32[]{:S(2)}) collective-permute-start(bf16[240,128]{1,0:T(8,128)(2,1)S(1)} %fusion.4), channel_id=1, source_target_pairs={{0,3},{1,4},{2,7},{3,0},{4,1},{5,6},{6,5},{7,2},{8,13},{9,10},{10,... | collective-permute-start | bytes 184328 | tf_op jit(solution)/shard_map/ppermute | solution.py:33
  10.5 4.0 %collective-permute-start.7 = (bf16[240,128]{1,0:T(8,128)(2,1)S(1)}, bf16[240,128]{1,0:T(8,128)(2,1)S(1)}, u32[]{:S(2)}, u32[]{:S(2)}) collective-permute-start(bf16[240,128]{1,0:T(8,128)(2,1)S(1)} %fusion.5), channel_id=1, source_target_pairs={{0,3},{1,4},{2,7},{3,0},{4,1},{5,6},{6,5},{7,2},{8,13},{9,10},{10,... | collective-permute-start | bytes 184328 | tf_op jit(solution)/shard_map/ppermute | solution.py:33
  12.4 4.0 %collective-permute-start.2 = (bf16[240,128]{1,0:T(8,128)(2,1)S(1)}, bf16[240,128]{1,0:T(8,128)(2,1)S(1)}, u32[]{:S(2)}, u32[]{:S(2)}) collective-permute-start(bf16[240,128]{1,0:T(8,128)(2,1)S(1)} %fusion.8), channel_id=1, source_target_pairs={{0,5},{1,2},{2,1},{3,6},{4,7},{5,0},{6,3},{7,4},{8,11},{9,12},{10,... | collective-permute-start | bytes 184328 | tf_op jit(solution)/shard_map/ppermute | solution.py:33
  14.5 3.7 %collective-permute-start.8 = (bf16[240,128]{1,0:T(8,128)(2,1)S(1)}, bf16[240,128]{1,0:T(8,128)(2,1)S(1)}, u32[]{:S(2)}, u32[]{:S(2)}) collective-permute-start(bf16[240,128]{1,0:T(8,128)(2,1)S(1)} %fusion.9), channel_id=1, source_target_pairs={{0,5},{1,2},{2,1},{3,6},{4,7},{5,0},{6,3},{7,4},{8,11},{9,12},{10,... | collective-permute-start | bytes 184328 | tf_op jit(solution)/shard_map/ppermute | solution.py:33
  16.4 3.7 %collective-permute-start.3 = (bf16[240,128]{1,0:T(8,128)(2,1)S(1)}, bf16[240,128]{1,0:T(8,128)(2,1)S(1)}, u32[]{:S(2)}, u32[]{:S(2)}) collective-permute-start(bf16[240,128]{1,0:T(8,128)(2,1)S(1)} %fusion.2), channel_id=1, source_target_pairs={{0,9},{1,16},{2,19},{3,10},{4,21},{5,12},{6,15},{7,22},{8,25},{9,0... | collective-permute-start | bytes 184328 | tf_op jit(solution)/shard_map/ppermute | solution.py:33
  18.3 5.0 %collective-permute-start.9 = (bf16[240,128]{1,0:T(8,128)(2,1)S(1)}, bf16[240,128]{1,0:T(8,128)(2,1)S(1)}, u32[]{:S(2)}, u32[]{:S(2)}) collective-permute-start(bf16[240,128]{1,0:T(8,128)(2,1)S(1)} %fusion.3), channel_id=1, source_target_pairs={{0,9},{1,16},{2,19},{3,10},{4,21},{5,12},{6,15},{7,22},{8,25},{9,0... | collective-permute-start | bytes 184328 | tf_op jit(solution)/shard_map/ppermute | solution.py:33
  20.2 5.5 %collective-permute-start.4 = (bf16[240,128]{1,0:T(8,128)(2,1)S(1)}, bf16[240,128]{1,0:T(8,128)(2,1)S(1)}, u32[]{:S(2)}, u32[]{:S(2)}) collective-permute-start(bf16[240,128]{1,0:T(8,128)(2,1)S(1)} %fusion.6), channel_id=1, source_target_pairs={{0,17},{1,8},{2,11},{3,18},{4,13},{5,20},{6,23},{7,14},{8,1},{9,24... | collective-permute-start | bytes 184328 | tf_op jit(solution)/shard_map/ppermute | solution.py:33
  23.3 4.6 %collective-permute-start.10 = (bf16[240,128]{1,0:T(8,128)(2,1)S(1)}, bf16[240,128]{1,0:T(8,128)(2,1)S(1)}, u32[]{:S(2)}, u32[]{:S(2)}) collective-permute-start(bf16[240,128]{1,0:T(8,128)(2,1)S(1)} %fusion.7), channel_id=1, source_target_pairs={{0,17},{1,8},{2,11},{3,18},{4,13},{5,20},{6,23},{7,14},{8,1},{9,24... | collective-permute-start | bytes 184328 | tf_op jit(solution)/shard_map/ppermute | solution.py:33
  25.7 3.8 %collective-permute-start.5 = (bf16[240,128]{1,0:T(8,128)(2,1)S(1)}, bf16[240,128]{1,0:T(8,128)(2,1)S(1)}, u32[]{:S(2)}, u32[]{:S(2)}) collective-permute-start(bf16[240,128]{1,0:T(8,128)(2,1)S(1)} %add_convert_fusion.1), channel_id=1, source_target_pairs={{0,3},{1,4},{2,7},{3,0},{4,1},{5,6},{6,5},{7,2},{8,13},{9,10},{10,... | collective-permute-start | bytes 184328 | tf_op jit(solution)/shard_map/ppermute | solution.py:33
  28.0 3.7 %collective-permute-start.11 = (bf16[240,128]{1,0:T(8,128)(2,1)S(1)}, bf16[240,128]{1,0:T(8,128)(2,1)S(1)}, u32[]{:S(2)}, u32[]{:S(2)}) collective-permute-start(bf16[240,128]{1,0:T(8,128)(2,1)S(1)} %add_convert_fusion), channel_id=1, source_target_pairs={{0,3},{1,4},{2,7},{3,0},{4,1},{5,6},{6,5},{7,2},{8,13},{9,10},{10,... | collective-permute-start | bytes 184328 | tf_op jit(solution)/shard_map/ppermute | solution.py:33
  29.5 3.1 %collective-permute-start.12 = (bf16[2,240,128]{2,1,0:T(8,128)(2,1)S(1)}, bf16[2,240,128]{2,1,0:T(8,128)(2,1)S(1)}, u32[]{:S(2)}, u32[]{:S(2)}) collective-permute-start(bf16[2,240,128]{2,1,0:T(8,128)(2,1)S(1)} %pad_maximum_fusion.mine_0), channel_id=1, source_target_pairs={{0,1},{1,0},{2,3},{3,2},{4,5},{5,4},{6,7},{7,6},{8,9},{9,8},{10,11... | collective-permute-start | bytes 368648 | tf_op jit(solution)/shard_map/ppermute | solution.py:33
  31.8 1.5 %collective-permute-start.13 = (bf16[2,240,128]{2,1,0:T(8,128)(2,1)S(1)}, bf16[2,240,128]{2,1,0:T(8,128)(2,1)S(1)}, u32[]{:S(2)}, u32[]{:S(2)}) collective-permute-start(bf16[2,240,128]{2,1,0:T(8,128)(2,1)S(1)} %pad_maximum_fusion.1.mine_1), channel_id=1, source_target_pairs={{0,1},{1,0},{2,3},{3,2},{4,5},{5,4},{6,7},{7,6},{8,9},{9,8},{10,11... | collective-permute-start | bytes 368648 | tf_op jit(solution)/shard_map/ppermute | solution.py:33

commit v3 on v2

--- a/solution.py
+++ b/solution.py
@@ -83,38 +83,73 @@
     return tiles
 
 
-def fock_kernel(n_orb, n_dev, tracks, three_hbm, dens_ref, *refs):
-    *part_refs, three_ref, acc_ref, sems = refs
-    q_loc, _, n_mo = three_ref.shape
+def load_kernel(three_hbm, three_ref, sems):
+    copies = [
+        pltpu.make_async_copy(three_hbm.at[q], three_ref.at[q], sems.at[q]) for q in range(three_ref.shape[0])
+    ]
+    for copy in copies:
+        copy.start()
+    for copy in copies:
+        copy.wait()
+
+
+def fock_half(side, lead, n_rows, base, slices, ready, dens_ref, part_refs, acc_ref):
     n_occ = dens_ref.shape[1]
     n_tiles = acc_ref.shape[0] // n_occ
-    base = n_occ // LANES * LANES
-    copies = []
-    for q in range(q_loc):
-        copies.append(pltpu.make_async_copy(three_hbm.at[q], three_ref.at[q], sems.at[q]))
-        copies[q].start()
-    for q in range(q_loc):
-        copies[q].wait()
-        part = matmul(dens_ref[q], three_ref[q, :, base:], NN)
-        for t in range(n_tiles):
-            stop = min(LANES, n_mo - base - t * LANES)
-            rows = slice(t * n_occ, (t + 1) * n_occ)
-            piece = part[:, t * LANES : t * LANES + stop]
-            if q:
-                acc_ref[rows, :stop] += piece
-            else:
-                if stop < LANES:
-                    acc_ref[rows, :] = jnp.zeros((n_occ, LANES), F32)
-                acc_ref[rows, :stop] = piece
+    for static in (0, 1):
+
+        @pl.when(side == static)
+        def _(static=static):
+            low = base + static * n_tiles * LANES
+            for q, three in enumerate(slices):
+                ready(q)
+                high = min(three.shape[1], low + n_tiles * LANES)
+                part = matmul(dens_ref[q], three[:, low:high], NN)
+                for t in range(n_tiles):
+                    stop = min(LANES, high - low - t * LANES)
+                    rows = slice(t * n_occ, (t + 1) * n_occ)
+                    piece = part[:, t * LANES : t * LANES + stop]
+                    if q:
+                        acc_ref[rows, :stop] += piece
+                    else:
+                        if stop < LANES:
+                            acc_ref[rows, :] = jnp.zeros((n_occ, LANES), F32)
+                        acc_ref[rows, :stop] = piece
+
+    for chain, ref in enumerate(part_refs):
+        for j in (0, 1):
+            start = pl.multiple_of((chain * 2 + (lead + j) % 2) * n_rows, n_rows)
+            ref[j] = acc_ref[pl.ds(start, n_rows), :].astype(ref.dtype)
+
+
+def side_and_lead(own, n_orb, n_dev, tracks):
     me = my_index(n_orb)
-    mine = half_of(me, n_dev)
-    n_rows = n_tiles * n_occ // 8
-    for chain in (0, 1):
-        for ref, side in zip(part_refs[chain::2], (mine, 1 - mine)):
-            lead = jnp.where(side == 0, bit(me, tracks[0][0]), bit(me, tracks[1][0]))
-            for j in (0, 1):
-                start = pl.multiple_of((side * 4 + chain * 2 + (lead + j) % 2) * n_rows, n_rows)
-                ref[j] = acc_ref[pl.ds(start, n_rows), :].astype(ref.dtype)
+    side = half_of(me, n_dev) if own else 1 - half_of(me, n_dev)
+    return side, jnp.where(side == 0, bit(me, tracks[0][0]), bit(me, tracks[1][0]))
+
+
+def send_kernel(n_orb, n_dev, tracks, n_rows, base, three_hbm, first_ref, dens_ref,
+                part_0, part_1, last_ref, acc_ref, sems):
+    n_first, n_last = first_ref.shape[0], last_ref.shape[0]
+    copies = [
+        pltpu.make_async_copy(three_hbm.at[n_first + q], last_ref.at[q], sems.at[q]) for q in range(n_last)
+    ]
+    for copy in copies:
+        copy.start()
+    slices = [first_ref.at[q] for q in range(n_first)] + [last_ref.at[q] for q in range(n_last)]
+
+    def ready(q):
+        if q >= n_first:
+            copies[q - n_first].wait()
+
+    side, lead = side_and_lead(False, n_orb, n_dev, tracks)
+    fock_half(side, lead, n_rows, base, slices, ready, dens_ref, (part_0, part_1), acc_ref)
+
+
+def keep_kernel(n_orb, n_dev, tracks, n_rows, base, first_ref, last_ref, dens_ref, part_0, part_1, acc_ref):
+    slices = [ref.at[q] for ref in (first_ref, last_ref) for q in range(ref.shape[0])]
+    side, lead = side_and_lead(True, n_orb, n_dev, tracks)
+    fock_half(side, lead, n_rows, base, slices, lambda q: None, dens_ref, (part_0, part_1), acc_ref)
 
 
 def rotation_kernel(n_orb, n_dev, tracks, mine_0, mine_1, other_0, other_1, hess_ref, sel_ref, chosen_ref, left_ref, rot_ref, fock_ref, u_ref):
@@ -172,12 +207,13 @@
     return tiles
 
 
-def half_kernel(n_rows, main, chosen_ref, three_ref, sent_ref, rem_ref, half_ref):
-    q_loc, r_loc, n_mo = three_ref.shape
+def half_kernel(n_rows, main, chosen_ref, first_ref, last_ref, sent_ref, rem_ref, half_ref):
+    slices = [ref.at[q] for ref in (first_ref, last_ref) for q in range(ref.shape[0])]
+    q_loc, r_loc = len(slices), first_ref.shape[1]
     rem = r_loc - main
     n_dev, dest_rows = sent_ref.shape[:2]
     for q in range(q_loc):
-        product = matmul(three_ref[q], chosen_ref[...], NN)
+        product = matmul(slices[q][...], chosen_ref[...], NN)
         half_ref[q] = product[:main].T
         rem_ref[q * rem : (q + 1) * rem, :] = product[main:]
     turned = rem_ref[...].T
@@ -264,33 +300,53 @@
 
     half_shape = (2, tiles * n_occ // 8, LANES)
     in_hbm = pl.BlockSpec(memory_space=pltpu.HBM)
-    *parts, three_vmem = pl.pallas_call(
-        functools.partial(fock_kernel, n_orb, n_dev, tracks),
-        in_specs=[in_hbm, in_vmem],
-        out_specs=[in_vmem] * 5,
+    n_first = q_loc // 2
+    n_last = q_loc - n_first
+    piece_rows = tiles * n_occ // 8
+    acc = pltpu.VMEM((tiles // 2 * n_occ, LANES), F32)
+    cost = lambda flops, moved: pl.CostEstimate(flops=flops, bytes_accessed=moved, transcendentals=0)
+    three_a = pl.pallas_call(
+        load_kernel,
+        in_specs=[in_hbm],
+        out_specs=in_vmem,
+        out_shape=jax.ShapeDtypeStruct((n_first, r_loc, n_mo), BF16),
+        scratch_shapes=[pltpu.SemaphoreType.DMA((n_first,))],
+        compiler_params=pltpu.CompilerParams(vmem_limit_bytes=43 * MIB),
+        cost_estimate=cost(0, 4 * n_first * r_loc * n_mo),
+        name="load",
+    )(three_index)
+    dens = density.transpose(0, 2, 1)
+    *send, three_b = pl.pallas_call(
+        functools.partial(send_kernel, n_orb, n_dev, tracks, piece_rows, base),
+        in_specs=[in_hbm, in_vmem, in_vmem],
+        out_specs=[in_vmem] * 3,
         out_shape=[
-            jax.ShapeDtypeStruct(half_shape, F32),
-            jax.ShapeDtypeStruct(half_shape, F32),
             jax.ShapeDtypeStruct(half_shape, BF16),
             jax.ShapeDtypeStruct(half_shape, BF16),
-            jax.ShapeDtypeStruct(three_index.shape, BF16),
+            jax.ShapeDtypeStruct((n_last, r_loc, n_mo), BF16),
         ],
-        scratch_shapes=[
-            pltpu.VMEM((tiles * n_occ, LANES), F32),
-            pltpu.SemaphoreType.DMA((q_loc,)),
-        ],
-        compiler_params=pltpu.CompilerParams(vmem_limit_bytes=38 * MIB),
-        cost_estimate=pl.CostEstimate(
-            flops=2 * q_loc * r_loc * n_occ * n_mo, bytes_accessed=2 * q_loc * r_loc * n_mo, transcendentals=0),
-        name="fock",
-    )(three_index, density.transpose(0, 2, 1))
+        scratch_shapes=[acc, pltpu.SemaphoreType.DMA((n_last,))],
+        compiler_params=pltpu.CompilerParams(vmem_limit_bytes=39 * MIB),
+        cost_estimate=cost(q_loc * r_loc * n_occ * n_mo, 4 * n_last * r_loc * n_mo),
+        name="fock_sent",
+    )(three_index, three_a, dens)
+    keep = pl.pallas_call(
+        functools.partial(keep_kernel, n_orb, n_dev, tracks, piece_rows, base),
+        in_specs=[in_vmem] * 3,
+        out_specs=[in_vmem] * 2,
+        out_shape=[jax.ShapeDtypeStruct(half_shape, F32)] * 2,
+        scratch_shapes=[acc],
+        compiler_params=pltpu.CompilerParams(vmem_limit_bytes=16 * MIB),
+        cost_estimate=cost(q_loc * r_loc * n_occ * n_mo, MIB),
+        name="fock_kept",
+    )(three_a, three_b, dens)
     hess = jnp.pad(
         hess_diag.T, ((0, 0), (n_occ - base, width - (n_mo - base))), constant_values=jnp.inf)
 
     masks = [[1 | 1 << tracks[half_of(d, n_dev)][k] for d in range(n_dev)] for k in range(len(tracks[0]))]
     held, other = [], []
     for chain in (0, 1):
-        part = parts[chain] + swap(parts[2 + chain], [1] * n_dev).astype(F32)
+        part = keep[chain] + swap(send[chain], [1] * n_dev).astype(F32)
         piece = part[0] + swap(part[1].astype(BF16), masks[0]).astype(F32)
         for mask in masks[1:]:
             piece = piece + swap(piece.astype(BF16), mask).astype(F32)
@@ -326,7 +382,7 @@
     )(*held, *other, hess, sel)
     sent = pl.pallas_call(
         functools.partial(half_kernel, n_rows, main),
-        in_specs=[in_vmem] * 2,
+        in_specs=[in_vmem] * 3,
         out_specs=in_vmem,
         out_shape=jax.ShapeDtypeStruct((n_dev, dest_rows, LANES), BF16),
         scratch_shapes=[
@@ -337,7 +393,7 @@
         cost_estimate=pl.CostEstimate(
             flops=2 * q_loc * r_loc * n_rows * n_dev * n_mo, bytes_accessed=2 * q_loc * r_loc * n_mo, transcendentals=0),
         name="half_rotation",
-    )(chosen, three_vmem)
+    )(chosen, three_a, three_b)
 
     got = lax.all_to_all(sent, BOTH, 0, 0, tiled=True).reshape(n_aux, n_orb, dest_rows, LANES)
     aux_step = min(n_aux, 8)

time: 72.2 us -> 72.3 us (level)
  Pallas kernels: 12.4 us -> 14.3 us
  local copies, waits for them, and re-layouts: 1.66 us -> 0.59 us
  waiting for transfers between devices: 7.67 us -> 6.66 us
    pallas_call x1 -> x3, Pallas kernels: 4.89 us -> 6.79 us  [the longest x1 2.92 us: on_device(): pl.pallas_call(functools.partial(send_kernel, n_orb, n_dev, tracks, piece...]
    unnamed x6, local copies, waits for them, and re-layouts: 1.32 us -> 0.25 us
    ppermute x14, waiting for transfers between devices: 7.67 us -> 6.66 us  [swap(): lax.ppermute(x, BOTH, [(d, d ^ mask) for d, mask in enumerate(masks)])]
  transfers between devices with their start and end apart: 14 -> 14, of which waited for: 10 -> 8; matrix products, arithmetic and copies ran while one was open for 1% -> 1% of each run, Pallas kernels for 0% -> 2%
where the time goes in v3:
time: 72.3 us; the launch traced here: 72.2 us
  blocking collectives  31.4 us (43%)
  starting transfers between devices  18.8 us (26%)
  Pallas kernels  14.3 us (20%)
  waiting for transfers between devices  6.66 us (9%)
    all_to_all x1, blocking collectives, on_device(): lax.all_to_all(sent, BOTH, 0, 0, tiled=True)  31.4 us
    ppermute x14, starting transfers between devices, swap(): lax.ppermute(x, BOTH, [(d, d ^ mask) for d, mask in enumerate(masks)])  18.8 us
    ppermute x14, waiting for transfers between devices, swap(): lax.ppermute(x, BOTH, [(d, d ^ mask) for d, mask in enumerate(masks)])  6.66 us
    pallas_call x1, Pallas kernels, on_device(): pl.pallas_call(functools.partial(half_kernel, n_rows, main), in_specs=[in...  3.47 us
    pallas_call x1, Pallas kernels, on_device(): pl.pallas_call(functools.partial(send_kernel, n_orb, n_dev, tracks, piece...  2.92 us
    pallas_call x1, Pallas kernels, on_device(): pl.pallas_call(load_kernel, in_specs=[in_hbm], out_specs=in_vmem, out_sha...  2.66 us
    pallas_call x1, Pallas kernels, on_device(): pl.pallas_call(functools.partial(owner_kernel, n_rows, aux_step, q_loc, r...  2.41 us
    pallas_call x1, Pallas kernels, on_device(): pl.pallas_call(functools.partial(rotation_kernel, n_orb, n_dev, tracks),...  1.6 us
  transfers between devices with their start and end apart: 14, of which 8 were waited for; matrix products, arithmetic and copies ran while one was open for 1% of the time, Pallas kernels for 2%

profile of v3, /device:TPU:0, one launch (start us, length us, event | category | flops | bytes accessed | tf_op | source)
XLA Modules:
  0.0 72.2 jit_solution(4108376609635423302)
XLA Ops:
  0.0 2.7 %load.1.first_ref = bf16[4,400,1600]{2,1,0:T(8,128)(2,1)S(1)} custom-call(bf16[8,400,1600]{2,1,0:T(8,128)(2,1)} %three_hbm.3), custom_call_target="tpu_custom_call" | custom-call | bytes 10240000 | tf_op jit(solution)/shard_map/load/pallas_call | solution.py:308
  2.9 2.9 %fock_sent.1 = (bf16[2,240,128]{2,1,0:T(8,128)(2,1)S(1)}, bf16[2,240,128]{2,1,0:T(8,128)(2,1)S(1)}, bf16[4,400,1600]{2,1,0:T(8,128)(2,1)S(1)}) custom-call(bf16[8,400,1600]{2,1,0:T(8,128)(2,1)} %three_hbm.3, bf16[4,400,1600]{2,1,0:T(8,128)(2,1)S(1)} %load.1.first_ref, bf16[8,160,400]{2,1,0:T(8,128)(2,1)S(1)} %bitcast.36), custom_call_target="tpu_custom_call" | custom-call | flops 819200000 | bytes 10240000 | tf_op jit(solution)/shard_map/fock_sent/pallas_call | solution.py:319
  5.8 0.5 collective-permute-start.6
  6.4 1.2 %fock_kept.1 = (f32[2,240,128]{2,1,0:T(8,128)S(1)}, f32[2,240,128]{2,1,0:T(8,128)S(1)}) custom-call(bf16[4,400,1600]{2,1,0:T(8,128)(2,1)S(1)} %load.1.first_ref, bf16[4,400,1600]{2,1,0:T(8,128)(2,1)S(1)} %get-tuple-element.13.last_ref, bf16[8,160,400]{2,1,0:T(8,128)(2,1)S(1)} %bitcast.37), custom_call_target="tpu_custom_call" | custom-call | flops 819200000 | bytes 1048576 | tf_op jit(solution)/shard_map/fock_kept/pallas_call | solution.py:333
  7.7 2.7 %collective-permute-start.7 = (bf16[240,128]{1,0:T(8,128)(2,1)S(1)}, bf16[240,128]{1,0:T(8,128)(2,1)S(1)}, u32[]{:S(2)}, u32[]{:S(2)}) collective-permute-start(bf16[240,128]{1,0:T(8,128)(2,1)S(1)} %fusion.5), channel_id=1, source_target_pairs={{0,3},{1,4},{2,7},{3,0},{4,1},{5,6},{6,5},{7,2},{8,13},{9,10},{10,... | collective-permute-start | bytes 184328 | tf_op jit(solution)/shard_map/ppermute | solution.py:33
  10.5 1.8 %collective-permute-done.7 = bf16[240,128]{1,0:T(8,128)(2,1)S(1)} collective-permute-done((bf16[240,128]{1,0:T(8,128)(2,1)S(1)}, bf16[240,128]{1,0:T(8,128)(2,1)S(1)}, u32[]{:S(2)}, u32[]{:S(2)}) %collective-permute-start.7) | collective-permute-done | bytes 61472 | tf_op jit(solution)/shard_map/ppermute | solution.py:33
  12.3 2.1 %collective-permute-start.8 = (bf16[240,128]{1,0:T(8,128)(2,1)S(1)}, bf16[240,128]{1,0:T(8,128)(2,1)S(1)}, u32[]{:S(2)}, u32[]{:S(2)}) collective-permute-start(bf16[240,128]{1,0:T(8,128)(2,1)S(1)} %fusion.9), channel_id=1, source_target_pairs={{0,5},{1,2},{2,1},{3,6},{4,7},{5,0},{6,3},{7,4},{8,11},{9,12},{10,... | collective-permute-start | bytes 184328 | tf_op jit(solution)/shard_map/ppermute | solution.py:33
  14.5 1.4 %collective-permute-start.2 = (bf16[240,128]{1,0:T(8,128)(2,1)S(1)}, bf16[240,128]{1,0:T(8,128)(2,1)S(1)}, u32[]{:S(2)}, u32[]{:S(2)}) collective-permute-start(bf16[240,128]{1,0:T(8,128)(2,1)S(1)} %fusion.8), channel_id=1, source_target_pairs={{0,5},{1,2},{2,1},{3,6},{4,7},{5,0},{6,3},{7,4},{8,11},{9,12},{10,... | collective-permute-start | bytes 184328 | tf_op jit(solution)/shard_map/ppermute | solution.py:33
  15.8 0.5 collective-permute-done.8
  16.4 1.6 %collective-permute-start.9 = (bf16[240,128]{1,0:T(8,128)(2,1)S(1)}, bf16[240,128]{1,0:T(8,128)(2,1)S(1)}, u32[]{:S(2)}, u32[]{:S(2)}) collective-permute-start(bf16[240,128]{1,0:T(8,128)(2,1)S(1)} %fusion.3), channel_id=1, source_target_pairs={{0,9},{1,16},{2,19},{3,10},{4,21},{5,12},{6,15},{7,22},{8,25},{9,0... | collective-permute-start | bytes 184328 | tf_op jit(solution)/shard_map/ppermute | solution.py:33
  18.2 1.4 %collective-permute-start.3 = (bf16[240,128]{1,0:T(8,128)(2,1)S(1)}, bf16[240,128]{1,0:T(8,128)(2,1)S(1)}, u32[]{:S(2)}, u32[]{:S(2)}) collective-permute-start(bf16[240,128]{1,0:T(8,128)(2,1)S(1)} %fusion.2), channel_id=1, source_target_pairs={{0,9},{1,16},{2,19},{3,10},{4,21},{5,12},{6,15},{7,22},{8,25},{9,0... | collective-permute-start | bytes 184328 | tf_op jit(solution)/shard_map/ppermute | solution.py:33
  19.6 0.5 collective-permute-done.9
  20.1 3.2 %collective-permute-start.10 = (bf16[240,128]{1,0:T(8,128)(2,1)S(1)}, bf16[240,128]{1,0:T(8,128)(2,1)S(1)}, u32[]{:S(2)}, u32[]{:S(2)}) collective-permute-start(bf16[240,128]{1,0:T(8,128)(2,1)S(1)} %fusion.7), channel_id=1, source_target_pairs={{0,17},{1,8},{2,11},{3,18},{4,13},{5,20},{6,23},{7,14},{8,1},{9,24... | collective-permute-start | bytes 184328 | tf_op jit(solution)/shard_map/ppermute | solution.py:33
  23.3 1.7 %collective-permute-start.4 = (bf16[240,128]{1,0:T(8,128)(2,1)S(1)}, bf16[240,128]{1,0:T(8,128)(2,1)S(1)}, u32[]{:S(2)}, u32[]{:S(2)}) collective-permute-start(bf16[240,128]{1,0:T(8,128)(2,1)S(1)} %fusion.6), channel_id=1, source_target_pairs={{0,17},{1,8},{2,11},{3,18},{4,13},{5,20},{6,23},{7,14},{8,1},{9,24... | collective-permute-start | bytes 184328 | tf_op jit(solution)/shard_map/ppermute | solution.py:33
  25.1 0.6 collective-permute-done.10
  25.8 1.8 %collective-permute-start.11 = (bf16[240,128]{1,0:T(8,128)(2,1)S(1)}, bf16[240,128]{1,0:T(8,128)(2,1)S(1)}, u32[]{:S(2)}, u32[]{:S(2)}) collective-permute-start(bf16[240,128]{1,0:T(8,128)(2,1)S(1)} %add_convert_fusion), channel_id=1, source_target_pairs={{0,3},{1,4},{2,7},{3,0},{4,1},{5,6},{6,5},{7,2},{8,13},{9,10},{10,... | collective-permute-start | bytes 184328 | tf_op jit(solution)/shard_map/ppermute | solution.py:33
  28.0 1.6 %collective-permute-start.5 = (bf16[240,128]{1,0:T(8,128)(2,1)S(1)}, bf16[240,128]{1,0:T(8,128)(2,1)S(1)}, u32[]{:S(2)}, u32[]{:S(2)}) collective-permute-start(bf16[240,128]{1,0:T(8,128)(2,1)S(1)} %add_convert_fusion.1), channel_id=1, source_target_pairs={{0,3},{1,4},{2,7},{3,0},{4,1},{5,6},{6,5},{7,2},{8,13},{9,10},{10,... | collective-permute-start | bytes 184328 | tf_op jit(solution)/shard_map/ppermute | solution.py:33
  29.7 2.0 %collective-permute-done.5 = bf16[240,128]{1,0:T(8,128)(2,1)S(1)} collective-permute-done((bf16[240,128]{1,0:T(8,128)(2,1)S(1)}, bf16[240,128]{1,0:T(8,128)(2,1)S(1)}, u32[]{:S(2)}, u32[]{:S(2)}) %collective-permute-start.5) | collective-permute-done | bytes 61472 | tf_op jit(solution)/shard_map/ppermute | solution.py:33
  31.8 0.5 collective-permute-start.12
  32.6 0.6 collective-permute-done.12.other_0
  33.3 1.6 %rotation.1 = (bf16[1600,160]{1,0:T(8,128)(2,1)S(1)}, bf16[160,1664]{1,0:T(8,128)(2,1)S(1)}, bf16[160,1536]{1,0:T(8,128)(2,1)S(1)}) custom-call(bf16[2,240,128]{2,1,0:T(8,128)(2,1)S(1)} %pad_maximum_fusion.mine_0, bf16[2,240,128]{2,1,0:T(8,128)(2,1)S(1)} %pad_maximum_fusion.1.mine_1, bf16[2,240,128]{2,1,0:T(8,128)(2,1)S(1)} %collective-permute-done.12.other_0, ...), custom_call_target="tpu_custom_call" | custom-call | flops 327680000 | bytes 4194304 | tf_op jit(solution)/shard_map/rotation/pallas_call | solution.py:369
  34.9 3.5 %half_rotation.1 = bf16[32,128,128]{2,1,0:T(8,128)(2,1)S(1)} custom-call(bf16[1600,160]{1,0:T(8,128)(2,1)S(1)} %get-tuple-element.18.chosen_ref, bf16[4,400,1600]{2,1,0:T(8,128)(2,1)S(1)} %load.1.first_ref, bf16[4,400,1600]{2,1,0:T(8,128)(2,1)S(1)} %get-tuple-element.13.last_ref), custom_call_target="tpu_custom_call" | custom-call | flops 1638400000 | bytes 10240000 | tf_op jit(solution)/shard_map/half_rotation/pallas_call | solution.py:383
  38.3 31.4 %all_to_all.5 = bf16[32,128,128]{2,1,0:T(8,128)(2,1)S(1)} all-to-all(bf16[32,128,128]{2,1,0:T(8,128)(2,1)S(1)} %half_rotation.1), channel_id=1, replica_groups=mesh['aux'=8,'orb'=4] {'aux','orb'}, dimensions={0} | all-to-all | bytes 2097152 | tf_op jit(solution)/shard_map/all_to_all | solution.py:398
  69.7 2.4 %owner_rows.1 = bf16[64,7200]{1,0:T(8,128)(2,1)} custom-call(bf16[8,4,128,128]{3,2,1,0:T(8,128)(2,1)S(1)} %bitcast.38, bf16[160,1664]{1,0:T(8,128)(2,1)S(1)} %get-tuple-element.19.left_ref, bf16[160,1536]{1,0:T(8,128)(2,1)S(1)} %get-tuple-element.20.rot_ref), custom_call_target="tpu_custom_call" | custom-call | flops 327680000 | bytes 8388608 | tf_op jit(solution)/shard_map/owner_rows/pallas_call | solution.py:400
  (32 shorter events, 1.8 us)
Async XLA Ops:
  0.0 2.9 %copy-start = (bf16[8,400,160]{1,2,0:T(8,128)(2,1)S(1)}, bf16[8,400,160]{1,2,0:T(8,128)(2,1)}, u32[]{:S(2)}) copy-start(bf16[8,400,160]{1,2,0:T(8,128)(2,1)} %param.5) | copy-start | bytes 3072004
  5.8 1.8 %collective-permute-start.6 = (bf16[2,240,128]{2,1,0:T(8,128)(2,1)S(1)}, bf16[2,240,128]{2,1,0:T(8,128)(2,1)S(1)}, u32[]{:S(2)}, u32[]{:S(2)}) collective-permute-start(bf16[2,240,128]{2,1,0:T(8,128)(2,1)S(1)} %get-tuple-element.17), channel_id=1, source_target_pairs={{0,1},{1,0},{2,3},{3,2},{4,5},{5,4},{6,7},{7,6},{8,9},{9,8},{10,11... | collective-permute-start | bytes 368648 | tf_op jit(solution)/shard_map/ppermute | solution.py:33
  6.3 4.0 %collective-permute-start = (bf16[2,240,128]{2,1,0:T(8,128)(2,1)S(1)}, bf16[2,240,128]{2,1,0:T(8,128)(2,1)S(1)}, u32[]{:S(2)}, u32[]{:S(2)}) collective-permute-start(bf16[2,240,128]{2,1,0:T(8,128)(2,1)S(1)} %get-tuple-element.15), channel_id=1, source_target_pairs={{0,1},{1,0},{2,3},{3,2},{4,5},{5,4},{6,7},{7,6},{8,9},{9,8},{10,11... | collective-permute-start | bytes 368648 | tf_op jit(solution)/shard_map/ppermute | solution.py:33
  7.6 24.6 %copy-start.2 = (f32[1440,160]{0,1:T(8,128)S(1)}, f32[1440,160]{0,1:T(8,128)}, u32[]{:S(2)}) copy-start(f32[1440,160]{0,1:T(8,128)} %param.6) | copy-start | bytes 2764804
  7.6 25.6 %copy-start.1 = (bf16[160,160]{1,0:T(8,128)(2,1)S(1)}, bf16[160,160]{1,0:T(8,128)(2,1)}, u32[]{:S(2)}) copy-start(bf16[160,160]{1,0:T(8,128)(2,1)} %constant.4.clone.sel_ref) | copy-start | bytes 153604
  7.7 4.6 %collective-permute-start.7 = (bf16[240,128]{1,0:T(8,128)(2,1)S(1)}, bf16[240,128]{1,0:T(8,128)(2,1)S(1)}, u32[]{:S(2)}, u32[]{:S(2)}) collective-permute-start(bf16[240,128]{1,0:T(8,128)(2,1)S(1)} %fusion.5), channel_id=1, source_target_pairs={{0,3},{1,4},{2,7},{3,0},{4,1},{5,6},{6,5},{7,2},{8,13},{9,10},{10,... | collective-permute-start | bytes 184328 | tf_op jit(solution)/shard_map/ppermute | solution.py:33
  10.4 4.0 %collective-permute-start.1 = (bf16[240,128]{1,0:T(8,128)(2,1)S(1)}, bf16[240,128]{1,0:T(8,128)(2,1)S(1)}, u32[]{:S(2)}, u32[]{:S(2)}) collective-permute-start(bf16[240,128]{1,0:T(8,128)(2,1)S(1)} %fusion.4), channel_id=1, source_target_pairs={{0,3},{1,4},{2,7},{3,0},{4,1},{5,6},{6,5},{7,2},{8,13},{9,10},{10,... | collective-permute-start | bytes 184328 | tf_op jit(solution)/shard_map/ppermute | solution.py:33
  12.3 4.0 %collective-permute-start.8 = (bf16[240,128]{1,0:T(8,128)(2,1)S(1)}, bf16[240,128]{1,0:T(8,128)(2,1)S(1)}, u32[]{:S(2)}, u32[]{:S(2)}) collective-permute-start(bf16[240,128]{1,0:T(8,128)(2,1)S(1)} %fusion.9), channel_id=1, source_target_pairs={{0,5},{1,2},{2,1},{3,6},{4,7},{5,0},{6,3},{7,4},{8,11},{9,12},{10,... | collective-permute-start | bytes 184328 | tf_op jit(solution)/shard_map/ppermute | solution.py:33
  14.5 3.7 %collective-permute-start.2 = (bf16[240,128]{1,0:T(8,128)(2,1)S(1)}, bf16[240,128]{1,0:T(8,128)(2,1)S(1)}, u32[]{:S(2)}, u32[]{:S(2)}) collective-permute-start(bf16[240,128]{1,0:T(8,128)(2,1)S(1)} %fusion.8), channel_id=1, source_target_pairs={{0,5},{1,2},{2,1},{3,6},{4,7},{5,0},{6,3},{7,4},{8,11},{9,12},{10,... | collective-permute-start | bytes 184328 | tf_op jit(solution)/shard_map/ppermute | solution.py:33
  16.4 3.7 %collective-permute-start.9 = (bf16[240,128]{1,0:T(8,128)(2,1)S(1)}, bf16[240,128]{1,0:T(8,128)(2,1)S(1)}, u32[]{:S(2)}, u32[]{:S(2)}) collective-permute-start(bf16[240,128]{1,0:T(8,128)(2,1)S(1)} %fusion.3), channel_id=1, source_target_pairs={{0,9},{1,16},{2,19},{3,10},{4,21},{5,12},{6,15},{7,22},{8,25},{9,0... | collective-permute-start | bytes 184328 | tf_op jit(solution)/shard_map/ppermute | solution.py:33
  18.2 5.1 %collective-permute-start.3 = (bf16[240,128]{1,0:T(8,128)(2,1)S(1)}, bf16[240,128]{1,0:T(8,128)(2,1)S(1)}, u32[]{:S(2)}, u32[]{:S(2)}) collective-permute-start(bf16[240,128]{1,0:T(8,128)(2,1)S(1)} %fusion.2), channel_id=1, source_target_pairs={{0,9},{1,16},{2,19},{3,10},{4,21},{5,12},{6,15},{7,22},{8,25},{9,0... | collective-permute-start | bytes 184328 | tf_op jit(solution)/shard_map/ppermute | solution.py:33
  20.1 5.6 %collective-permute-start.10 = (bf16[240,128]{1,0:T(8,128)(2,1)S(1)}, bf16[240,128]{1,0:T(8,128)(2,1)S(1)}, u32[]{:S(2)}, u32[]{:S(2)}) collective-permute-start(bf16[240,128]{1,0:T(8,128)(2,1)S(1)} %fusion.7), channel_id=1, source_target_pairs={{0,17},{1,8},{2,11},{3,18},{4,13},{5,20},{6,23},{7,14},{8,1},{9,24... | collective-permute-start | bytes 184328 | tf_op jit(solution)/shard_map/ppermute | solution.py:33
  23.3 4.7 %collective-permute-start.4 = (bf16[240,128]{1,0:T(8,128)(2,1)S(1)}, bf16[240,128]{1,0:T(8,128)(2,1)S(1)}, u32[]{:S(2)}, u32[]{:S(2)}) collective-permute-start(bf16[240,128]{1,0:T(8,128)(2,1)S(1)} %fusion.6), channel_id=1, source_target_pairs={{0,17},{1,8},{2,11},{3,18},{4,13},{5,20},{6,23},{7,14},{8,1},{9,24... | collective-permute-start | bytes 184328 | tf_op jit(solution)/shard_map/ppermute | solution.py:33
  25.8 3.9 %collective-permute-start.11 = (bf16[240,128]{1,0:T(8,128)(2,1)S(1)}, bf16[240,128]{1,0:T(8,128)(2,1)S(1)}, u32[]{:S(2)}, u32[]{:S(2)}) collective-permute-start(bf16[240,128]{1,0:T(8,128)(2,1)S(1)} %add_convert_fusion), channel_id=1, source_target_pairs={{0,3},{1,4},{2,7},{3,0},{4,1},{5,6},{6,5},{7,2},{8,13},{9,10},{10,... | collective-permute-start | bytes 184328 | tf_op jit(solution)/shard_map/ppermute | solution.py:33
  28.0 3.7 %collective-permute-start.5 = (bf16[240,128]{1,0:T(8,128)(2,1)S(1)}, bf16[240,128]{1,0:T(8,128)(2,1)S(1)}, u32[]{:S(2)}, u32[]{:S(2)}) collective-permute-start(bf16[240,128]{1,0:T(8,128)(2,1)S(1)} %add_convert_fusion.1), channel_id=1, source_target_pairs={{0,3},{1,4},{2,7},{3,0},{4,1},{5,6},{6,5},{7,2},{8,13},{9,10},{10,... | collective-permute-start | bytes 184328 | tf_op jit(solution)/shard_map/ppermute | solution.py:33
  29.6 3.0 %collective-permute-start.13 = (bf16[2,240,128]{2,1,0:T(8,128)(2,1)S(1)}, bf16[2,240,128]{2,1,0:T(8,128)(2,1)S(1)}, u32[]{:S(2)}, u32[]{:S(2)}) collective-permute-start(bf16[2,240,128]{2,1,0:T(8,128)(2,1)S(1)} %pad_maximum_fusion.1.mine_1), channel_id=1, source_target_pairs={{0,1},{1,0},{2,3},{3,2},{4,5},{5,4},{6,7},{7,6},{8,9},{9,8},{10,11... | collective-permute-start | bytes 368648 | tf_op jit(solution)/shard_map/ppermute | solution.py:33
  31.8 1.5 %collective-permute-start.12 = (bf16[2,240,128]{2,1,0:T(8,128)(2,1)S(1)}, bf16[2,240,128]{2,1,0:T(8,128)(2,1)S(1)}, u32[]{:S(2)}, u32[]{:S(2)}) collective-permute-start(bf16[2,240,128]{2,1,0:T(8,128)(2,1)S(1)} %pad_maximum_fusion.mine_0), channel_id=1, source_target_pairs={{0,1},{1,0},{2,3},{3,2},{4,5},{5,4},{6,7},{7,6},{8,9},{9,8},{10,11... | collective-permute-start | bytes 368648 | tf_op jit(solution)/shard_map/ppermute | solution.py:33

commit v4 on v2

--- a/solution.py
+++ b/solution.py
@@ -23,6 +23,10 @@
 NN = ((1,), (0,))
 NT = ((1,), (1,))
 TN = ((0,), (0,))
+
+
+def to_hbm(x):
+    return pltpu.with_memory_space_constraint(x, pltpu.HBM)
 
 
 def my_index(n_orb):
@@ -83,18 +87,23 @@
     return tiles
 
 
-def fock_kernel(n_orb, n_dev, tracks, three_hbm, dens_ref, *refs):
-    *part_refs, three_ref, acc_ref, sems = refs
+def fock_kernel(n_orb, n_dev, tracks, three_hbm, dens_hbm, *refs):
+    *part_refs, three_ref, acc_ref, dens_ref, sems, dens_sems = refs
     q_loc, _, n_mo = three_ref.shape
     n_occ = dens_ref.shape[1]
     n_tiles = acc_ref.shape[0] // n_occ
     base = n_occ // LANES * LANES
     copies = []
     for q in range(q_loc):
-        copies.append(pltpu.make_async_copy(three_hbm.at[q], three_ref.at[q], sems.at[q]))
-        copies[q].start()
+        copies.append((
+            pltpu.make_async_copy(dens_hbm.at[q], dens_ref.at[q], dens_sems.at[q]),
+            pltpu.make_async_copy(three_hbm.at[q], three_ref.at[q], sems.at[q]),
+        ))
+        for copy in copies[q]:
+            copy.start()
     for q in range(q_loc):
-        copies[q].wait()
+        for copy in copies[q]:
+            copy.wait()
         part = matmul(dens_ref[q], three_ref[q, :, base:], NN)
         for t in range(n_tiles):
             stop = min(LANES, n_mo - base - t * LANES)
@@ -266,7 +275,7 @@
     in_hbm = pl.BlockSpec(memory_space=pltpu.HBM)
     *parts, three_vmem = pl.pallas_call(
         functools.partial(fock_kernel, n_orb, n_dev, tracks),
-        in_specs=[in_hbm, in_vmem],
+        in_specs=[in_hbm, in_hbm],
         out_specs=[in_vmem] * 5,
         out_shape=[
             jax.ShapeDtypeStruct(half_shape, F32),
@@ -277,13 +286,15 @@
         ],
         scratch_shapes=[
             pltpu.VMEM((tiles * n_occ, LANES), F32),
+            pltpu.VMEM((q_loc, n_occ, r_loc), BF16),
+            pltpu.SemaphoreType.DMA((q_loc,)),
             pltpu.SemaphoreType.DMA((q_loc,)),
         ],
         compiler_params=pltpu.CompilerParams(vmem_limit_bytes=38 * MIB),
         cost_estimate=pl.CostEstimate(
             flops=2 * q_loc * r_loc * n_occ * n_mo, bytes_accessed=2 * q_loc * r_loc * n_mo, transcendentals=0),
         name="fock",
-    )(three_index, density.transpose(0, 2, 1))
+    )(to_hbm(three_index), to_hbm(density.transpose(0, 2, 1)))
     hess = jnp.pad(
         hess_diag.T, ((0, 0), (n_occ - base, width - (n_mo - base))), constant_values=jnp.inf)
 

time: 72.2 us -> 71.2 us (0.986)
  local copies, waits for them, and re-layouts: 1.66 us -> 0.34 us
    unnamed x6 -> x4, local copies, waits for them, and re-layouts: 1.32 us -> 0.01 us
where the time goes in v4:
time: 71.2 us; the launch traced here: 71 us
  blocking collectives  31.3 us (44%)
  starting transfers between devices  18.6 us (26%)
  Pallas kernels  12.7 us (18%)
  waiting for transfers between devices  7.68 us (11%)
    all_to_all x1, blocking collectives, on_device(): lax.all_to_all(sent, BOTH, 0, 0, tiled=True)  31.3 us
    ppermute x14, starting transfers between devices, swap(): lax.ppermute(x, BOTH, [(d, d ^ mask) for d, mask in enumerate(masks)])  18.6 us
    ppermute x14, waiting for transfers between devices, swap(): lax.ppermute(x, BOTH, [(d, d ^ mask) for d, mask in enumerate(masks)])  7.68 us
    pallas_call x1, Pallas kernels, on_device(): pl.pallas_call(functools.partial(fock_kernel, n_orb, n_dev, tracks), in_s...  5.17 us
    pallas_call x1, Pallas kernels, on_device(): pl.pallas_call(functools.partial(half_kernel, n_rows, main), in_specs=[in...  3.47 us
    pallas_call x1, Pallas kernels, on_device(): pl.pallas_call(functools.partial(owner_kernel, n_rows, aux_step, q_loc, r...  2.41 us
    pallas_call x1, Pallas kernels, on_device(): pl.pallas_call(functools.partial(rotation_kernel, n_orb, n_dev, tracks),...  1.61 us
  transfers between devices with their start and end apart: 14, of which 10 were waited for; matrix products, arithmetic and copies ran while one was open for 1% of the time, Pallas kernels for 0%

profile of v4, /device:TPU:0, one launch (start us, length us, event | category | flops | bytes accessed | tf_op | source)
XLA Modules:
  0.0 71.0 jit_solution(3718470274143032222)
XLA Ops:
  0.0 5.2 %fock.1 = (f32[2,240,128]{2,1,0:T(8,128)S(1)}, f32[2,240,128]{2,1,0:T(8,128)S(1)}, bf16[2,240,128]{2,1,0:T(8,128)(2,1)S(1)}, bf16[2,240,128]{2,1,0:T(8,128)(2,1)S(1)}, bf16[8,400,1600]{2,1,0:T(8,128)(2,1)S(1)}) custom-call(bf16[8,400,1600]{2,1,0:T(8,128)(2,1)} %three_hbm.1, bf16[8,160,400]{2,1,0:T(8,128)(2,1)} %bitcast.37), custom_call_target="tpu_custom_call" | custom-call | flops 1638400000 | bytes 10240000 | tf_op jit(solution)/shard_map/fock/pallas_call | solution.py:276
  5.2 0.5 collective-permute-start
  5.8 0.9 %collective-permute-done = bf16[2,240,128]{2,1,0:T(8,128)(2,1)S(1)} collective-permute-done((bf16[2,240,128]{2,1,0:T(8,128)(2,1)S(1)}, bf16[2,240,128]{2,1,0:T(8,128)(2,1)S(1)}, u32[]{:S(2)}, u32[]{:S(2)}) %collective-permute-start) | collective-permute-done | bytes 122912 | tf_op jit(solution)/shard_map/ppermute | solution.py:37
  6.7 2.7 %collective-permute-start.1 = (bf16[240,128]{1,0:T(8,128)(2,1)S(1)}, bf16[240,128]{1,0:T(8,128)(2,1)S(1)}, u32[]{:S(2)}, u32[]{:S(2)}) collective-permute-start(bf16[240,128]{1,0:T(8,128)(2,1)S(1)} %fusion.4), channel_id=1, source_target_pairs={{0,3},{1,4},{2,7},{3,0},{4,1},{5,6},{6,5},{7,2},{8,13},{9,10},{10,... | collective-permute-start | bytes 184328 | tf_op jit(solution)/shard_map/ppermute | solution.py:37
  9.7 1.5 %collective-permute-done.1 = bf16[240,128]{1,0:T(8,128)(2,1)S(1)} collective-permute-done((bf16[240,128]{1,0:T(8,128)(2,1)S(1)}, bf16[240,128]{1,0:T(8,128)(2,1)S(1)}, u32[]{:S(2)}, u32[]{:S(2)}) %collective-permute-start.1) | collective-permute-done | bytes 61472 | tf_op jit(solution)/shard_map/ppermute | solution.py:37
  11.3 2.1 %collective-permute-start.2 = (bf16[240,128]{1,0:T(8,128)(2,1)S(1)}, bf16[240,128]{1,0:T(8,128)(2,1)S(1)}, u32[]{:S(2)}, u32[]{:S(2)}) collective-permute-start(bf16[240,128]{1,0:T(8,128)(2,1)S(1)} %fusion.8), channel_id=1, source_target_pairs={{0,5},{1,2},{2,1},{3,6},{4,7},{5,0},{6,3},{7,4},{8,11},{9,12},{10,... | collective-permute-start | bytes 184328 | tf_op jit(solution)/shard_map/ppermute | solution.py:37
  13.5 1.2 %collective-permute-start.8 = (bf16[240,128]{1,0:T(8,128)(2,1)S(1)}, bf16[240,128]{1,0:T(8,128)(2,1)S(1)}, u32[]{:S(2)}, u32[]{:S(2)}) collective-permute-start(bf16[240,128]{1,0:T(8,128)(2,1)S(1)} %fusion.9), channel_id=1, source_target_pairs={{0,5},{1,2},{2,1},{3,6},{4,7},{5,0},{6,3},{7,4},{8,11},{9,12},{10,... | collective-permute-start | bytes 184328 | tf_op jit(solution)/shard_map/ppermute | solution.py:37
  14.7 0.6 collective-permute-done.2
  15.4 1.6 %collective-permute-start.3 = (bf16[240,128]{1,0:T(8,128)(2,1)S(1)}, bf16[240,128]{1,0:T(8,128)(2,1)S(1)}, u32[]{:S(2)}, u32[]{:S(2)}) collective-permute-start(bf16[240,128]{1,0:T(8,128)(2,1)S(1)} %fusion.2), channel_id=1, source_target_pairs={{0,9},{1,16},{2,19},{3,10},{4,21},{5,12},{6,15},{7,22},{8,25},{9,0... | collective-permute-start | bytes 184328 | tf_op jit(solution)/shard_map/ppermute | solution.py:37
  17.2 1.3 %collective-permute-start.9 = (bf16[240,128]{1,0:T(8,128)(2,1)S(1)}, bf16[240,128]{1,0:T(8,128)(2,1)S(1)}, u32[]{:S(2)}, u32[]{:S(2)}) collective-permute-start(bf16[240,128]{1,0:T(8,128)(2,1)S(1)} %fusion.3), channel_id=1, source_target_pairs={{0,9},{1,16},{2,19},{3,10},{4,21},{5,12},{6,15},{7,22},{8,25},{9,0... | collective-permute-start | bytes 184328 | tf_op jit(solution)/shard_map/ppermute | solution.py:37
  18.5 0.6 collective-permute-done.3
  19.1 3.1 %collective-permute-start.4 = (bf16[240,128]{1,0:T(8,128)(2,1)S(1)}, bf16[240,128]{1,0:T(8,128)(2,1)S(1)}, u32[]{:S(2)}, u32[]{:S(2)}) collective-permute-start(bf16[240,128]{1,0:T(8,128)(2,1)S(1)} %fusion.6), channel_id=1, source_target_pairs={{0,17},{1,8},{2,11},{3,18},{4,13},{5,20},{6,23},{7,14},{8,1},{9,24... | collective-permute-start | bytes 184328 | tf_op jit(solution)/shard_map/ppermute | solution.py:37
  22.3 1.8 %collective-permute-start.10 = (bf16[240,128]{1,0:T(8,128)(2,1)S(1)}, bf16[240,128]{1,0:T(8,128)(2,1)S(1)}, u32[]{:S(2)}, u32[]{:S(2)}) collective-permute-start(bf16[240,128]{1,0:T(8,128)(2,1)S(1)} %fusion.7), channel_id=1, source_target_pairs={{0,17},{1,8},{2,11},{3,18},{4,13},{5,20},{6,23},{7,14},{8,1},{9,24... | collective-permute-start | bytes 184328 | tf_op jit(solution)/shard_map/ppermute | solution.py:37
  24.0 0.6 collective-permute-done.4
  24.7 1.9 %collective-permute-start.5 = (bf16[240,128]{1,0:T(8,128)(2,1)S(1)}, bf16[240,128]{1,0:T(8,128)(2,1)S(1)}, u32[]{:S(2)}, u32[]{:S(2)}) collective-permute-start(bf16[240,128]{1,0:T(8,128)(2,1)S(1)} %add_convert_fusion.1), channel_id=1, source_target_pairs={{0,3},{1,4},{2,7},{3,0},{4,1},{5,6},{6,5},{7,2},{8,13},{9,10},{10,... | collective-permute-start | bytes 184328 | tf_op jit(solution)/shard_map/ppermute | solution.py:37
  26.5 0.4 collective-permute-done.10
  27.0 1.3 %collective-permute-start.11 = (bf16[240,128]{1,0:T(8,128)(2,1)S(1)}, bf16[240,128]{1,0:T(8,128)(2,1)S(1)}, u32[]{:S(2)}, u32[]{:S(2)}) collective-permute-start(bf16[240,128]{1,0:T(8,128)(2,1)S(1)} %add_convert_fusion), channel_id=1, source_target_pairs={{0,3},{1,4},{2,7},{3,0},{4,1},{5,6},{6,5},{7,2},{8,13},{9,10},{10,... | collective-permute-start | bytes 184328 | tf_op jit(solution)/shard_map/ppermute | solution.py:37
  28.6 2.1 %collective-permute-done.11 = bf16[240,128]{1,0:T(8,128)(2,1)S(1)} collective-permute-done((bf16[240,128]{1,0:T(8,128)(2,1)S(1)}, bf16[240,128]{1,0:T(8,128)(2,1)S(1)}, u32[]{:S(2)}, u32[]{:S(2)}) %collective-permute-start.11) | collective-permute-done | bytes 61472 | tf_op jit(solution)/shard_map/ppermute | solution.py:37
  30.7 0.5 collective-permute-start.13
  31.5 0.6 collective-permute-done.13.other_1
  32.2 1.6 %rotation.1 = (bf16[1600,160]{1,0:T(8,128)(2,1)S(1)}, bf16[160,1664]{1,0:T(8,128)(2,1)S(1)}, bf16[160,1536]{1,0:T(8,128)(2,1)S(1)}) custom-call(bf16[2,240,128]{2,1,0:T(8,128)(2,1)S(1)} %pad_maximum_fusion.mine_0, bf16[2,240,128]{2,1,0:T(8,128)(2,1)S(1)} %pad_maximum_fusion.1.mine_1, bf16[2,240,128]{2,1,0:T(8,128)(2,1)S(1)} %collective-permute-done.12.other_0, ...), custom_call_target="tpu_custom_call" | custom-call | flops 327680000 | bytes 4194304 | tf_op jit(solution)/shard_map/rotation/pallas_call | solution.py:324
  33.8 3.5 %half_rotation.1 = bf16[32,128,128]{2,1,0:T(8,128)(2,1)S(1)} custom-call(bf16[1600,160]{1,0:T(8,128)(2,1)S(1)} %get-tuple-element.17.chosen_ref, bf16[8,400,1600]{2,1,0:T(8,128)(2,1)S(1)} %get-tuple-element.18.three_ref), custom_call_target="tpu_custom_call" | custom-call | flops 1638400000 | bytes 10240000 | tf_op jit(solution)/shard_map/half_rotation/pallas_call | solution.py:338
  37.3 31.3 %all_to_all.5 = bf16[32,128,128]{2,1,0:T(8,128)(2,1)S(1)} all-to-all(bf16[32,128,128]{2,1,0:T(8,128)(2,1)S(1)} %half_rotation.1), channel_id=1, replica_groups=mesh['aux'=8,'orb'=4] {'aux','orb'}, dimensions={0} | all-to-all | bytes 2097152 | tf_op jit(solution)/shard_map/all_to_all | solution.py:353
  68.6 2.4 %owner_rows.1 = bf16[64,7200]{1,0:T(8,128)(2,1)} custom-call(bf16[8,4,128,128]{3,2,1,0:T(8,128)(2,1)S(1)} %bitcast.36, bf16[160,1664]{1,0:T(8,128)(2,1)S(1)} %get-tuple-element.19.left_ref, bf16[160,1536]{1,0:T(8,128)(2,1)S(1)} %get-tuple-element.20.rot_ref), custom_call_target="tpu_custom_call" | custom-call | flops 327680000 | bytes 8388608 | tf_op jit(solution)/shard_map/owner_rows/pallas_call | solution.py:355
  (28 shorter events, 1.6 us)
Async XLA Ops:
  0.0 32.2 %copy-start = (bf16[160,160]{1,0:T(8,128)(2,1)S(1)}, bf16[160,160]{1,0:T(8,128)(2,1)}, u32[]{:S(2)}) copy-start(bf16[160,160]{1,0:T(8,128)(2,1)} %constant.4.clone.sel_ref) | copy-start | bytes 153604
  0.0 31.2 %copy-start.1 = (f32[1440,160]{0,1:T(8,128)S(1)}, f32[1440,160]{0,1:T(8,128)}, u32[]{:S(2)}) copy-start(f32[1440,160]{0,1:T(8,128)} %param.6) | copy-start | bytes 2764804
  5.2 1.5 %collective-permute-start = (bf16[2,240,128]{2,1,0:T(8,128)(2,1)S(1)}, bf16[2,240,128]{2,1,0:T(8,128)(2,1)S(1)}, u32[]{:S(2)}, u32[]{:S(2)}) collective-permute-start(bf16[2,240,128]{2,1,0:T(8,128)(2,1)S(1)} %get-tuple-element.14), channel_id=1, source_target_pairs={{0,1},{1,0},{2,3},{3,2},{4,5},{5,4},{6,7},{7,6},{8,9},{9,8},{10,11... | collective-permute-start | bytes 368648 | tf_op jit(solution)/shard_map/ppermute | solution.py:37
  5.7 3.7 %collective-permute-start.6 = (bf16[2,240,128]{2,1,0:T(8,128)(2,1)S(1)}, bf16[2,240,128]{2,1,0:T(8,128)(2,1)S(1)}, u32[]{:S(2)}, u32[]{:S(2)}) collective-permute-start(bf16[2,240,128]{2,1,0:T(8,128)(2,1)S(1)} %get-tuple-element.16), channel_id=1, source_target_pairs={{0,1},{1,0},{2,3},{3,2},{4,5},{5,4},{6,7},{7,6},{8,9},{9,8},{10,11... | collective-permute-start | bytes 368648 | tf_op jit(solution)/shard_map/ppermute | solution.py:37
  6.7 4.6 %collective-permute-start.1 = (bf16[240,128]{1,0:T(8,128)(2,1)S(1)}, bf16[240,128]{1,0:T(8,128)(2,1)S(1)}, u32[]{:S(2)}, u32[]{:S(2)}) collective-permute-start(bf16[240,128]{1,0:T(8,128)(2,1)S(1)} %fusion.4), channel_id=1, source_target_pairs={{0,3},{1,4},{2,7},{3,0},{4,1},{5,6},{6,5},{7,2},{8,13},{9,10},{10,... | collective-permute-start | bytes 184328 | tf_op jit(solution)/shard_map/ppermute | solution.py:37
  9.4 4.0 %collective-permute-start.7 = (bf16[240,128]{1,0:T(8,128)(2,1)S(1)}, bf16[240,128]{1,0:T(8,128)(2,1)S(1)}, u32[]{:S(2)}, u32[]{:S(2)}) collective-permute-start(bf16[240,128]{1,0:T(8,128)(2,1)S(1)} %fusion.5), channel_id=1, source_target_pairs={{0,3},{1,4},{2,7},{3,0},{4,1},{5,6},{6,5},{7,2},{8,13},{9,10},{10,... | collective-permute-start | bytes 184328 | tf_op jit(solution)/shard_map/ppermute | solution.py:37
  11.3 4.0 %collective-permute-start.2 = (bf16[240,128]{1,0:T(8,128)(2,1)S(1)}, bf16[240,128]{1,0:T(8,128)(2,1)S(1)}, u32[]{:S(2)}, u32[]{:S(2)}) collective-permute-start(bf16[240,128]{1,0:T(8,128)(2,1)S(1)} %fusion.8), channel_id=1, source_target_pairs={{0,5},{1,2},{2,1},{3,6},{4,7},{5,0},{6,3},{7,4},{8,11},{9,12},{10,... | collective-permute-start | bytes 184328 | tf_op jit(solution)/shard_map/ppermute | solution.py:37
  13.5 3.7 %collective-permute-start.8 = (bf16[240,128]{1,0:T(8,128)(2,1)S(1)}, bf16[240,128]{1,0:T(8,128)(2,1)S(1)}, u32[]{:S(2)}, u32[]{:S(2)}) collective-permute-start(bf16[240,128]{1,0:T(8,128)(2,1)S(1)} %fusion.9), channel_id=1, source_target_pairs={{0,5},{1,2},{2,1},{3,6},{4,7},{5,0},{6,3},{7,4},{8,11},{9,12},{10,... | collective-permute-start | bytes 184328 | tf_op jit(solution)/shard_map/ppermute | solution.py:37
  15.4 3.7 %collective-permute-start.3 = (bf16[240,128]{1,0:T(8,128)(2,1)S(1)}, bf16[240,128]{1,0:T(8,128)(2,1)S(1)}, u32[]{:S(2)}, u32[]{:S(2)}) collective-permute-start(bf16[240,128]{1,0:T(8,128)(2,1)S(1)} %fusion.2), channel_id=1, source_target_pairs={{0,9},{1,16},{2,19},{3,10},{4,21},{5,12},{6,15},{7,22},{8,25},{9,0... | collective-permute-start | bytes 184328 | tf_op jit(solution)/shard_map/ppermute | solution.py:37
  17.2 5.0 %collective-permute-start.9 = (bf16[240,128]{1,0:T(8,128)(2,1)S(1)}, bf16[240,128]{1,0:T(8,128)(2,1)S(1)}, u32[]{:S(2)}, u32[]{:S(2)}) collective-permute-start(bf16[240,128]{1,0:T(8,128)(2,1)S(1)} %fusion.3), channel_id=1, source_target_pairs={{0,9},{1,16},{2,19},{3,10},{4,21},{5,12},{6,15},{7,22},{8,25},{9,0... | collective-permute-start | bytes 184328 | tf_op jit(solution)/shard_map/ppermute | solution.py:37
  19.1 5.5 %collective-permute-start.4 = (bf16[240,128]{1,0:T(8,128)(2,1)S(1)}, bf16[240,128]{1,0:T(8,128)(2,1)S(1)}, u32[]{:S(2)}, u32[]{:S(2)}) collective-permute-start(bf16[240,128]{1,0:T(8,128)(2,1)S(1)} %fusion.6), channel_id=1, source_target_pairs={{0,17},{1,8},{2,11},{3,18},{4,13},{5,20},{6,23},{7,14},{8,1},{9,24... | collective-permute-start | bytes 184328 | tf_op jit(solution)/shard_map/ppermute | solution.py:37
  22.3 4.6 %collective-permute-start.10 = (bf16[240,128]{1,0:T(8,128)(2,1)S(1)}, bf16[240,128]{1,0:T(8,128)(2,1)S(1)}, u32[]{:S(2)}, u32[]{:S(2)}) collective-permute-start(bf16[240,128]{1,0:T(8,128)(2,1)S(1)} %fusion.7), channel_id=1, source_target_pairs={{0,17},{1,8},{2,11},{3,18},{4,13},{5,20},{6,23},{7,14},{8,1},{9,24... | collective-permute-start | bytes 184328 | tf_op jit(solution)/shard_map/ppermute | solution.py:37
  24.7 3.8 %collective-permute-start.5 = (bf16[240,128]{1,0:T(8,128)(2,1)S(1)}, bf16[240,128]{1,0:T(8,128)(2,1)S(1)}, u32[]{:S(2)}, u32[]{:S(2)}) collective-permute-start(bf16[240,128]{1,0:T(8,128)(2,1)S(1)} %add_convert_fusion.1), channel_id=1, source_target_pairs={{0,3},{1,4},{2,7},{3,0},{4,1},{5,6},{6,5},{7,2},{8,13},{9,10},{10,... | collective-permute-start | bytes 184328 | tf_op jit(solution)/shard_map/ppermute | solution.py:37
  27.0 3.7 %collective-permute-start.11 = (bf16[240,128]{1,0:T(8,128)(2,1)S(1)}, bf16[240,128]{1,0:T(8,128)(2,1)S(1)}, u32[]{:S(2)}, u32[]{:S(2)}) collective-permute-start(bf16[240,128]{1,0:T(8,128)(2,1)S(1)} %add_convert_fusion), channel_id=1, source_target_pairs={{0,3},{1,4},{2,7},{3,0},{4,1},{5,6},{6,5},{7,2},{8,13},{9,10},{10,... | collective-permute-start | bytes 184328 | tf_op jit(solution)/shard_map/ppermute | solution.py:37
  28.4 3.1 %collective-permute-start.12 = (bf16[2,240,128]{2,1,0:T(8,128)(2,1)S(1)}, bf16[2,240,128]{2,1,0:T(8,128)(2,1)S(1)}, u32[]{:S(2)}, u32[]{:S(2)}) collective-permute-start(bf16[2,240,128]{2,1,0:T(8,128)(2,1)S(1)} %pad_maximum_fusion.mine_0), channel_id=1, source_target_pairs={{0,1},{1,0},{2,3},{3,2},{4,5},{5,4},{6,7},{7,6},{8,9},{9,8},{10,11... | collective-permute-start | bytes 368648 | tf_op jit(solution)/shard_map/ppermute | solution.py:37
  30.7 1.5 %collective-permute-start.13 = (bf16[2,240,128]{2,1,0:T(8,128)(2,1)S(1)}, bf16[2,240,128]{2,1,0:T(8,128)(2,1)S(1)}, u32[]{:S(2)}, u32[]{:S(2)}) collective-permute-start(bf16[2,240,128]{2,1,0:T(8,128)(2,1)S(1)} %pad_maximum_fusion.1.mine_1), channel_id=1, source_target_pairs={{0,1},{1,0},{2,3},{3,2},{4,5},{5,4},{6,7},{7,6},{8,9},{9,8},{10,11... | collective-permute-start | bytes 368648 | tf_op jit(solution)/shard_map/ppermute | solution.py:37

commit v5 on v3

--- a/solution.py
+++ b/solution.py
@@ -23,6 +23,10 @@
 NN = ((1,), (0,))
 NT = ((1,), (1,))
 TN = ((0,), (0,))
+
+
+def to_hbm(x):
+    return pltpu.with_memory_space_constraint(x, pltpu.HBM)
 
 
 def my_index(n_orb):
@@ -83,17 +87,7 @@
     return tiles
 
 
-def load_kernel(three_hbm, three_ref, sems):
-    copies = [
-        pltpu.make_async_copy(three_hbm.at[q], three_ref.at[q], sems.at[q]) for q in range(three_ref.shape[0])
-    ]
-    for copy in copies:
-        copy.start()
-    for copy in copies:
-        copy.wait()
-
-
-def fock_half(side, lead, n_rows, base, slices, ready, dens_ref, part_refs, acc_ref):
+def fock_half(side, lead, n_rows, base, ready, three_ref, dens_ref, part_refs, acc_ref):
     n_occ = dens_ref.shape[1]
     n_tiles = acc_ref.shape[0] // n_occ
     for static in (0, 1):
@@ -101,10 +95,10 @@
         @pl.when(side == static)
         def _(static=static):
             low = base + static * n_tiles * LANES
-            for q, three in enumerate(slices):
+            high = min(three_ref.shape[2], low + n_tiles * LANES)
+            for q in range(three_ref.shape[0]):
                 ready(q)
-                high = min(three.shape[1], low + n_tiles * LANES)
-                part = matmul(dens_ref[q], three[:, low:high], NN)
+                part = matmul(dens_ref[q], three_ref[q, :, low:high], NN)
                 for t in range(n_tiles):
                     stop = min(LANES, high - low - t * LANES)
                     rows = slice(t * n_occ, (t + 1) * n_occ)
@@ -128,28 +122,28 @@
     return side, jnp.where(side == 0, bit(me, tracks[0][0]), bit(me, tracks[1][0]))
 
 
-def send_kernel(n_orb, n_dev, tracks, n_rows, base, three_hbm, first_ref, dens_ref,
-                part_0, part_1, last_ref, acc_ref, sems):
-    n_first, n_last = first_ref.shape[0], last_ref.shape[0]
-    copies = [
-        pltpu.make_async_copy(three_hbm.at[n_first + q], last_ref.at[q], sems.at[q]) for q in range(n_last)
-    ]
-    for copy in copies:
-        copy.start()
-    slices = [first_ref.at[q] for q in range(n_first)] + [last_ref.at[q] for q in range(n_last)]
+def send_kernel(n_orb, n_dev, tracks, n_rows, base, three_hbm, dens_hbm,
+                part_0, part_1, three_ref, dens_ref, acc_ref, sems, dens_sems):
+    copies = []
+    for q in range(three_ref.shape[0]):
+        copies.append((
+            pltpu.make_async_copy(dens_hbm.at[q], dens_ref.at[q], dens_sems.at[q]),
+            pltpu.make_async_copy(three_hbm.at[q], three_ref.at[q], sems.at[q]),
+        ))
+        for copy in copies[q]:
+            copy.start()
 
     def ready(q):
-        if q >= n_first:
-            copies[q - n_first].wait()
+        for copy in copies[q]:
+            copy.wait()
 
     side, lead = side_and_lead(False, n_orb, n_dev, tracks)
-    fock_half(side, lead, n_rows, base, slices, ready, dens_ref, (part_0, part_1), acc_ref)
-
-
-def keep_kernel(n_orb, n_dev, tracks, n_rows, base, first_ref, last_ref, dens_ref, part_0, part_1, acc_ref):
-    slices = [ref.at[q] for ref in (first_ref, last_ref) for q in range(ref.shape[0])]
+    fock_half(side, lead, n_rows, base, ready, three_ref, dens_ref, (part_0, part_1), acc_ref)
+
+
+def keep_kernel(n_orb, n_dev, tracks, n_rows, base, three_ref, dens_ref, part_0, part_1, acc_ref):
     side, lead = side_and_lead(True, n_orb, n_dev, tracks)
-    fock_half(side, lead, n_rows, base, slices, lambda q: None, dens_ref, (part_0, part_1), acc_ref)
+    fock_half(side, lead, n_rows, base, lambda q: None, three_ref, dens_ref, (part_0, part_1), acc_ref)
 
 
 def rotation_kernel(n_orb, n_dev, tracks, mine_0, mine_1, other_0, other_1, hess_ref, sel_ref, chosen_ref, left_ref, rot_ref, fock_ref, u_ref):
@@ -189,8 +183,8 @@
     left_ref[:, :base] = l_oo[:, :base]
     left_ref[:, base:] = (over_rot / 24.0 - rot / 2.0).astype(BF16)
     left_ref[:, base:n_occ] = l_oo[:, base:]
-    chosen = matmul(sel_ref[...], u_ref[...], NN)
-    chosen_ref[...] = chosen.T[:n_mo].astype(BF16)
+    chosen = matmul(u_ref[...], sel_ref[...], ((0,), (1,)))
+    chosen_ref[...] = chosen[:n_mo].astype(BF16)
 
 
 def swap_rows(tiles):
@@ -207,13 +201,12 @@
     return tiles
 
 
-def half_kernel(n_rows, main, chosen_ref, first_ref, last_ref, sent_ref, rem_ref, half_ref):
-    slices = [ref.at[q] for ref in (first_ref, last_ref) for q in range(ref.shape[0])]
-    q_loc, r_loc = len(slices), first_ref.shape[1]
+def half_kernel(n_rows, main, chosen_ref, three_ref, sent_ref, rem_ref, half_ref):
+    q_loc, r_loc, n_mo = three_ref.shape
     rem = r_loc - main
     n_dev, dest_rows = sent_ref.shape[:2]
     for q in range(q_loc):
-        product = matmul(slices[q][...], chosen_ref[...], NN)
+        product = matmul(three_ref[q], chosen_ref[...], NN)
         half_ref[q] = product[:main].T
         rem_ref[q * rem : (q + 1) * rem, :] = product[main:]
     turned = rem_ref[...].T
@@ -300,46 +293,37 @@
 
     half_shape = (2, tiles * n_occ // 8, LANES)
     in_hbm = pl.BlockSpec(memory_space=pltpu.HBM)
-    n_first = q_loc // 2
-    n_last = q_loc - n_first
     piece_rows = tiles * n_occ // 8
     acc = pltpu.VMEM((tiles // 2 * n_occ, LANES), F32)
-    cost = lambda flops, moved: pl.CostEstimate(flops=flops, bytes_accessed=moved, transcendentals=0)
-    three_a = pl.pallas_call(
-        load_kernel,
-        in_specs=[in_hbm],
-        out_specs=in_vmem,
-        out_shape=jax.ShapeDtypeStruct((n_first, r_loc, n_mo), BF16),
-        scratch_shapes=[pltpu.SemaphoreType.DMA((n_first,))],
-        compiler_params=pltpu.CompilerParams(vmem_limit_bytes=43 * MIB),
-        cost_estimate=cost(0, 4 * n_first * r_loc * n_mo),
-        name="load",
-    )(three_index)
+    cost = lambda moved: pl.CostEstimate(
+        flops=q_loc * r_loc * n_occ * n_mo, bytes_accessed=moved, transcendentals=0)
     dens = density.transpose(0, 2, 1)
-    *send, three_b = pl.pallas_call(
+    *send, three_vmem, dens_vmem = pl.pallas_call(
         functools.partial(send_kernel, n_orb, n_dev, tracks, piece_rows, base),
-        in_specs=[in_hbm, in_vmem, in_vmem],
-        out_specs=[in_vmem] * 3,
+        in_specs=[in_hbm] * 2,
+        out_specs=[in_vmem] * 4,
         out_shape=[
             jax.ShapeDtypeStruct(half_shape, BF16),
             jax.ShapeDtypeStruct(half_shape, BF16),
-            jax.ShapeDtypeStruct((n_last, r_loc, n_mo), BF16),
+            jax.ShapeDtypeStruct(three_index.shape, BF16),
+            jax.ShapeDtypeStruct(dens.shape, BF16),
         ],
-        scratch_shapes=[acc, pltpu.SemaphoreType.DMA((n_last,))],
-        compiler_params=pltpu.CompilerParams(vmem_limit_bytes=39 * MIB),
-        cost_estimate=cost(q_loc * r_loc * n_occ * n_mo, 4 * n_last * r_loc * n_mo),
+        scratch_shapes=[acc, pltpu.SemaphoreType.DMA((q_loc,)), pltpu.SemaphoreType.DMA((q_loc,))],
+        compiler_params=pltpu.CompilerParams(vmem_limit_bytes=32 * MIB),
+        cost_estimate=cost(2 * q_loc * r_loc * n_mo),
         name="fock_sent",
-    )(three_index, three_a, dens)
+    )(to_hbm(three_index), to_hbm(dens))
+    three_vmem = pltpu.with_memory_space_constraint(three_vmem, pltpu.VMEM)
     keep = pl.pallas_call(
         functools.partial(keep_kernel, n_orb, n_dev, tracks, piece_rows, base),
-        in_specs=[in_vmem] * 3,
+        in_specs=[in_vmem] * 2,
         out_specs=[in_vmem] * 2,
         out_shape=[jax.ShapeDtypeStruct(half_shape, F32)] * 2,
         scratch_shapes=[acc],
         compiler_params=pltpu.CompilerParams(vmem_limit_bytes=16 * MIB),
-        cost_estimate=cost(q_loc * r_loc * n_occ * n_mo, MIB),
+        cost_estimate=cost(MIB),
         name="fock_kept",
-    )(three_a, three_b, dens)
+    )(three_vmem, pltpu.with_memory_space_constraint(dens_vmem, pltpu.VMEM))
     hess = jnp.pad(
         hess_diag.T, ((0, 0), (n_occ - base, width - (n_mo - base))), constant_values=jnp.inf)
 
@@ -382,7 +366,7 @@
     )(*held, *other, hess, sel)
     sent = pl.pallas_call(
         functools.partial(half_kernel, n_rows, main),
-        in_specs=[in_vmem] * 3,
+        in_specs=[in_vmem] * 2,
         out_specs=in_vmem,
         out_shape=jax.ShapeDtypeStruct((n_dev, dest_rows, LANES), BF16),
         scratch_shapes=[
@@ -393,7 +377,7 @@
         cost_estimate=pl.CostEstimate(
             flops=2 * q_loc * r_loc * n_rows * n_dev * n_mo, bytes_accessed=2 * q_loc * r_loc * n_mo, transcendentals=0),
         name="half_rotation",
-    )(chosen, three_a, three_b)
+    )(chosen, three_vmem)
 
     got = lax.all_to_all(sent, BOTH, 0, 0, tiled=True).reshape(n_aux, n_orb, dest_rows, LANES)
     aux_step = min(n_aux, 8)

time: 72.3 us -> 71.4 us (0.988)
    pallas_call x1 -> x0, Pallas kernels: 2.66 us -> none  [on_device(): pl.pallas_call(load_kernel, in_specs=[in_hbm], out_specs=in_vmem, out_sha...]
    pallas_call x1, Pallas kernels: 2.92 us -> 4.98 us  [on_device(): pl.pallas_call(functools.partial(send_kernel, n_orb, n_dev, tracks, piece...]
where the time goes in v5:
time: 71.4 us; the launch traced here: 71.2 us
  blocking collectives  31.3 us (44%)
  starting transfers between devices  18.8 us (26%)
  Pallas kernels  13.7 us (19%)
  waiting for transfers between devices  6.66 us (9%)
    all_to_all x1, blocking collectives, on_device(): lax.all_to_all(sent, BOTH, 0, 0, tiled=True)  31.3 us
    ppermute x14, starting transfers between devices, swap(): lax.ppermute(x, BOTH, [(d, d ^ mask) for d, mask in enumerate(masks)])  18.8 us
    ppermute x14, waiting for transfers between devices, swap(): lax.ppermute(x, BOTH, [(d, d ^ mask) for d, mask in enumerate(masks)])  6.66 us
    pallas_call x1, Pallas kernels, on_device(): pl.pallas_call(functools.partial(send_kernel, n_orb, n_dev, tracks, piece...  4.98 us
    pallas_call x1, Pallas kernels, on_device(): pl.pallas_call(functools.partial(half_kernel, n_rows, main), in_specs=[in...  3.47 us
    pallas_call x1, Pallas kernels, on_device(): pl.pallas_call(functools.partial(owner_kernel, n_rows, aux_step, q_loc, r...  2.41 us
    pallas_call x1, Pallas kernels, on_device(): pl.pallas_call(functools.partial(rotation_kernel, n_orb, n_dev, tracks),...  1.62 us
  transfers between devices with their start and end apart: 14, of which 8 were waited for; matrix products, arithmetic and copies ran while one was open for 1% of the time, Pallas kernels for 2%

profile of v5, /device:TPU:0, one launch (start us, length us, event | category | flops | bytes accessed | tf_op | source)
XLA Modules:
  0.0 71.2 jit_solution(10418765604336869036)
XLA Ops:
  0.0 5.0 %fock_sent.1 = (bf16[2,240,128]{2,1,0:T(8,128)(2,1)S(1)}, bf16[2,240,128]{2,1,0:T(8,128)(2,1)S(1)}, bf16[8,400,1600]{2,1,0:T(8,128)(2,1)S(1)}, bf16[8,160,400]{2,1,0:T(8,128)(2,1)S(1)}) custom-call(bf16[8,400,1600]{2,1,0:T(8,128)(2,1)} %three_hbm.1, bf16[8,160,400]{2,1,0:T(8,128)(2,1)} %bitcast.37), custom_call_target="tpu_custom_call" | custom-call | flops 819200000 | bytes 10240000 | tf_op jit(solution)/shard_map/fock_sent/pallas_call | solution.py:301
  5.0 0.5 collective-permute-start
  5.6 1.2 %fock_kept.1 = (f32[2,240,128]{2,1,0:T(8,128)S(1)}, f32[2,240,128]{2,1,0:T(8,128)S(1)}) custom-call(bf16[8,400,1600]{2,1,0:T(8,128)(2,1)S(1)} %get-tuple-element.14.three_ref, bf16[8,160,400]{2,1,0:T(8,128)(2,1)S(1)} %get-tuple-element.15.dens_ref), custom_call_target="tpu_custom_call" | custom-call | flops 819200000 | bytes 1048576 | tf_op jit(solution)/shard_map/fock_kept/pallas_call | solution.py:317
  6.9 2.7 %collective-permute-start.1 = (bf16[240,128]{1,0:T(8,128)(2,1)S(1)}, bf16[240,128]{1,0:T(8,128)(2,1)S(1)}, u32[]{:S(2)}, u32[]{:S(2)}) collective-permute-start(bf16[240,128]{1,0:T(8,128)(2,1)S(1)} %fusion.4), channel_id=1, source_target_pairs={{0,3},{1,4},{2,7},{3,0},{4,1},{5,6},{6,5},{7,2},{8,13},{9,10},{10,... | collective-permute-start | bytes 184328 | tf_op jit(solution)/shard_map/ppermute | solution.py:37
  9.7 1.8 %collective-permute-done.1 = bf16[240,128]{1,0:T(8,128)(2,1)S(1)} collective-permute-done((bf16[240,128]{1,0:T(8,128)(2,1)S(1)}, bf16[240,128]{1,0:T(8,128)(2,1)S(1)}, u32[]{:S(2)}, u32[]{:S(2)}) %collective-permute-start.1) | collective-permute-done | bytes 61472 | tf_op jit(solution)/shard_map/ppermute | solution.py:37
  11.4 2.1 %collective-permute-start.2 = (bf16[240,128]{1,0:T(8,128)(2,1)S(1)}, bf16[240,128]{1,0:T(8,128)(2,1)S(1)}, u32[]{:S(2)}, u32[]{:S(2)}) collective-permute-start(bf16[240,128]{1,0:T(8,128)(2,1)S(1)} %fusion.8), channel_id=1, source_target_pairs={{0,5},{1,2},{2,1},{3,6},{4,7},{5,0},{6,3},{7,4},{8,11},{9,12},{10,... | collective-permute-start | bytes 184328 | tf_op jit(solution)/shard_map/ppermute | solution.py:37
  13.6 1.4 %collective-permute-start.8 = (bf16[240,128]{1,0:T(8,128)(2,1)S(1)}, bf16[240,128]{1,0:T(8,128)(2,1)S(1)}, u32[]{:S(2)}, u32[]{:S(2)}) collective-permute-start(bf16[240,128]{1,0:T(8,128)(2,1)S(1)} %fusion.9), channel_id=1, source_target_pairs={{0,5},{1,2},{2,1},{3,6},{4,7},{5,0},{6,3},{7,4},{8,11},{9,12},{10,... | collective-permute-start | bytes 184328 | tf_op jit(solution)/shard_map/ppermute | solution.py:37
  15.0 0.5 collective-permute-done.2
  15.5 1.6 %collective-permute-start.3 = (bf16[240,128]{1,0:T(8,128)(2,1)S(1)}, bf16[240,128]{1,0:T(8,128)(2,1)S(1)}, u32[]{:S(2)}, u32[]{:S(2)}) collective-permute-start(bf16[240,128]{1,0:T(8,128)(2,1)S(1)} %fusion.2), channel_id=1, source_target_pairs={{0,9},{1,16},{2,19},{3,10},{4,21},{5,12},{6,15},{7,22},{8,25},{9,0... | collective-permute-start | bytes 184328 | tf_op jit(solution)/shard_map/ppermute | solution.py:37
  17.3 1.4 %collective-permute-start.9 = (bf16[240,128]{1,0:T(8,128)(2,1)S(1)}, bf16[240,128]{1,0:T(8,128)(2,1)S(1)}, u32[]{:S(2)}, u32[]{:S(2)}) collective-permute-start(bf16[240,128]{1,0:T(8,128)(2,1)S(1)} %fusion.3), channel_id=1, source_target_pairs={{0,9},{1,16},{2,19},{3,10},{4,21},{5,12},{6,15},{7,22},{8,25},{9,0... | collective-permute-start | bytes 184328 | tf_op jit(solution)/shard_map/ppermute | solution.py:37
  18.8 0.5 collective-permute-done.3
  19.3 3.2 %collective-permute-start.4 = (bf16[240,128]{1,0:T(8,128)(2,1)S(1)}, bf16[240,128]{1,0:T(8,128)(2,1)S(1)}, u32[]{:S(2)}, u32[]{:S(2)}) collective-permute-start(bf16[240,128]{1,0:T(8,128)(2,1)S(1)} %fusion.6), channel_id=1, source_target_pairs={{0,17},{1,8},{2,11},{3,18},{4,13},{5,20},{6,23},{7,14},{8,1},{9,24... | collective-permute-start | bytes 184328 | tf_op jit(solution)/shard_map/ppermute | solution.py:37
  22.5 1.7 %collective-permute-start.10 = (bf16[240,128]{1,0:T(8,128)(2,1)S(1)}, bf16[240,128]{1,0:T(8,128)(2,1)S(1)}, u32[]{:S(2)}, u32[]{:S(2)}) collective-permute-start(bf16[240,128]{1,0:T(8,128)(2,1)S(1)} %fusion.7), channel_id=1, source_target_pairs={{0,17},{1,8},{2,11},{3,18},{4,13},{5,20},{6,23},{7,14},{8,1},{9,24... | collective-permute-start | bytes 184328 | tf_op jit(solution)/shard_map/ppermute | solution.py:37
  24.2 0.6 collective-permute-done.4
  24.9 1.8 %collective-permute-start.5 = (bf16[240,128]{1,0:T(8,128)(2,1)S(1)}, bf16[240,128]{1,0:T(8,128)(2,1)S(1)}, u32[]{:S(2)}, u32[]{:S(2)}) collective-permute-start(bf16[240,128]{1,0:T(8,128)(2,1)S(1)} %add_convert_fusion.1), channel_id=1, source_target_pairs={{0,3},{1,4},{2,7},{3,0},{4,1},{5,6},{6,5},{7,2},{8,13},{9,10},{10,... | collective-permute-start | bytes 184328 | tf_op jit(solution)/shard_map/ppermute | solution.py:37
  26.7 0.4 collective-permute-done.10
  27.2 1.5 %collective-permute-start.11 = (bf16[240,128]{1,0:T(8,128)(2,1)S(1)}, bf16[240,128]{1,0:T(8,128)(2,1)S(1)}, u32[]{:S(2)}, u32[]{:S(2)}) collective-permute-start(bf16[240,128]{1,0:T(8,128)(2,1)S(1)} %add_convert_fusion), channel_id=1, source_target_pairs={{0,3},{1,4},{2,7},{3,0},{4,1},{5,6},{6,5},{7,2},{8,13},{9,10},{10,... | collective-permute-start | bytes 184328 | tf_op jit(solution)/shard_map/ppermute | solution.py:37
  28.9 2.0 %collective-permute-done.11 = bf16[240,128]{1,0:T(8,128)(2,1)S(1)} collective-permute-done((bf16[240,128]{1,0:T(8,128)(2,1)S(1)}, bf16[240,128]{1,0:T(8,128)(2,1)S(1)}, u32[]{:S(2)}, u32[]{:S(2)}) %collective-permute-start.11) | collective-permute-done | bytes 61472 | tf_op jit(solution)/shard_map/ppermute | solution.py:37
  30.9 0.5 collective-permute-start.13
  31.8 0.6 collective-permute-done.13.other_1
  32.4 1.6 %rotation.1 = (bf16[1600,160]{1,0:T(8,128)(2,1)S(1)}, bf16[160,1664]{1,0:T(8,128)(2,1)S(1)}, bf16[160,1536]{1,0:T(8,128)(2,1)S(1)}) custom-call(bf16[2,240,128]{2,1,0:T(8,128)(2,1)S(1)} %pad_maximum_fusion.mine_0, bf16[2,240,128]{2,1,0:T(8,128)(2,1)S(1)} %pad_maximum_fusion.1.mine_1, bf16[2,240,128]{2,1,0:T(8,128)(2,1)S(1)} %collective-permute-done.12.other_0, ...), custom_call_target="tpu_custom_call" | custom-call | flops 327680000 | bytes 4194304 | tf_op jit(solution)/shard_map/rotation/pallas_call | solution.py:353
  34.0 3.5 %half_rotation.1 = bf16[32,128,128]{2,1,0:T(8,128)(2,1)S(1)} custom-call(bf16[1600,160]{1,0:T(8,128)(2,1)S(1)} %get-tuple-element.20.chosen_ref, bf16[8,400,1600]{2,1,0:T(8,128)(2,1)S(1)} %get-tuple-element.14.three_ref), custom_call_target="tpu_custom_call" | custom-call | flops 1638400000 | bytes 10240000 | tf_op jit(solution)/shard_map/half_rotation/pallas_call | solution.py:367
  37.5 31.3 %all_to_all.5 = bf16[32,128,128]{2,1,0:T(8,128)(2,1)S(1)} all-to-all(bf16[32,128,128]{2,1,0:T(8,128)(2,1)S(1)} %half_rotation.1), channel_id=1, replica_groups=mesh['aux'=8,'orb'=4] {'aux','orb'}, dimensions={0} | all-to-all | bytes 2097152 | tf_op jit(solution)/shard_map/all_to_all | solution.py:382
  68.8 2.4 %owner_rows.1 = bf16[64,7200]{1,0:T(8,128)(2,1)} custom-call(bf16[8,4,128,128]{3,2,1,0:T(8,128)(2,1)S(1)} %bitcast.36, bf16[160,1664]{1,0:T(8,128)(2,1)S(1)} %get-tuple-element.21.left_ref, bf16[160,1536]{1,0:T(8,128)(2,1)S(1)} %get-tuple-element.22.rot_ref), custom_call_target="tpu_custom_call" | custom-call | flops 327680000 | bytes 8388608 | tf_op jit(solution)/shard_map/owner_rows/pallas_call | solution.py:384
  (29 shorter events, 1.2 us)
Async XLA Ops:
  5.0 26.4 %copy-start.1 = (f32[1440,160]{0,1:T(8,128)S(1)}, f32[1440,160]{0,1:T(8,128)}, u32[]{:S(2)}) copy-start(f32[1440,160]{0,1:T(8,128)} %param.6) | copy-start | bytes 2764804
  5.0 27.4 %copy-start = (bf16[160,160]{1,0:T(8,128)(2,1)S(1)}, bf16[160,160]{1,0:T(8,128)(2,1)}, u32[]{:S(2)}) copy-start(bf16[160,160]{1,0:T(8,128)(2,1)} %constant.4.clone.sel_ref) | copy-start | bytes 153604
  5.0 1.8 %collective-permute-start = (bf16[2,240,128]{2,1,0:T(8,128)(2,1)S(1)}, bf16[2,240,128]{2,1,0:T(8,128)(2,1)S(1)}, u32[]{:S(2)}, u32[]{:S(2)}) collective-permute-start(bf16[2,240,128]{2,1,0:T(8,128)(2,1)S(1)} %get-tuple-element.17), channel_id=1, source_target_pairs={{0,1},{1,0},{2,3},{3,2},{4,5},{5,4},{6,7},{7,6},{8,9},{9,8},{10,11... | collective-permute-start | bytes 368648 | tf_op jit(solution)/shard_map/ppermute | solution.py:37
  5.5 4.0 %collective-permute-start.6 = (bf16[2,240,128]{2,1,0:T(8,128)(2,1)S(1)}, bf16[2,240,128]{2,1,0:T(8,128)(2,1)S(1)}, u32[]{:S(2)}, u32[]{:S(2)}) collective-permute-start(bf16[2,240,128]{2,1,0:T(8,128)(2,1)S(1)} %get-tuple-element.19), channel_id=1, source_target_pairs={{0,1},{1,0},{2,3},{3,2},{4,5},{5,4},{6,7},{7,6},{8,9},{9,8},{10,11... | collective-permute-start | bytes 368648 | tf_op jit(solution)/shard_map/ppermute | solution.py:37
  6.9 4.6 %collective-permute-start.1 = (bf16[240,128]{1,0:T(8,128)(2,1)S(1)}, bf16[240,128]{1,0:T(8,128)(2,1)S(1)}, u32[]{:S(2)}, u32[]{:S(2)}) collective-permute-start(bf16[240,128]{1,0:T(8,128)(2,1)S(1)} %fusion.4), channel_id=1, source_target_pairs={{0,3},{1,4},{2,7},{3,0},{4,1},{5,6},{6,5},{7,2},{8,13},{9,10},{10,... | collective-permute-start | bytes 184328 | tf_op jit(solution)/shard_map/ppermute | solution.py:37
  9.6 4.0 %collective-permute-start.7 = (bf16[240,128]{1,0:T(8,128)(2,1)S(1)}, bf16[240,128]{1,0:T(8,128)(2,1)S(1)}, u32[]{:S(2)}, u32[]{:S(2)}) collective-permute-start(bf16[240,128]{1,0:T(8,128)(2,1)S(1)} %fusion.5), channel_id=1, source_target_pairs={{0,3},{1,4},{2,7},{3,0},{4,1},{5,6},{6,5},{7,2},{8,13},{9,10},{10,... | collective-permute-start | bytes 184328 | tf_op jit(solution)/shard_map/ppermute | solution.py:37
  11.4 4.0 %collective-permute-start.2 = (bf16[240,128]{1,0:T(8,128)(2,1)S(1)}, bf16[240,128]{1,0:T(8,128)(2,1)S(1)}, u32[]{:S(2)}, u32[]{:S(2)}) collective-permute-start(bf16[240,128]{1,0:T(8,128)(2,1)S(1)} %fusion.8), channel_id=1, source_target_pairs={{0,5},{1,2},{2,1},{3,6},{4,7},{5,0},{6,3},{7,4},{8,11},{9,12},{10,... | collective-permute-start | bytes 184328 | tf_op jit(solution)/shard_map/ppermute | solution.py:37
  13.6 3.7 %collective-permute-start.8 = (bf16[240,128]{1,0:T(8,128)(2,1)S(1)}, bf16[240,128]{1,0:T(8,128)(2,1)S(1)}, u32[]{:S(2)}, u32[]{:S(2)}) collective-permute-start(bf16[240,128]{1,0:T(8,128)(2,1)S(1)} %fusion.9), channel_id=1, source_target_pairs={{0,5},{1,2},{2,1},{3,6},{4,7},{5,0},{6,3},{7,4},{8,11},{9,12},{10,... | collective-permute-start | bytes 184328 | tf_op jit(solution)/shard_map/ppermute | solution.py:37
  15.5 3.7 %collective-permute-start.3 = (bf16[240,128]{1,0:T(8,128)(2,1)S(1)}, bf16[240,128]{1,0:T(8,128)(2,1)S(1)}, u32[]{:S(2)}, u32[]{:S(2)}) collective-permute-start(bf16[240,128]{1,0:T(8,128)(2,1)S(1)} %fusion.2), channel_id=1, source_target_pairs={{0,9},{1,16},{2,19},{3,10},{4,21},{5,12},{6,15},{7,22},{8,25},{9,0... | collective-permute-start | bytes 184328 | tf_op jit(solution)/shard_map/ppermute | solution.py:37
  17.3 5.1 %collective-permute-start.9 = (bf16[240,128]{1,0:T(8,128)(2,1)S(1)}, bf16[240,128]{1,0:T(8,128)(2,1)S(1)}, u32[]{:S(2)}, u32[]{:S(2)}) collective-permute-start(bf16[240,128]{1,0:T(8,128)(2,1)S(1)} %fusion.3), channel_id=1, source_target_pairs={{0,9},{1,16},{2,19},{3,10},{4,21},{5,12},{6,15},{7,22},{8,25},{9,0... | collective-permute-start | bytes 184328 | tf_op jit(solution)/shard_map/ppermute | solution.py:37
  19.3 5.6 %collective-permute-start.4 = (bf16[240,128]{1,0:T(8,128)(2,1)S(1)}, bf16[240,128]{1,0:T(8,128)(2,1)S(1)}, u32[]{:S(2)}, u32[]{:S(2)}) collective-permute-start(bf16[240,128]{1,0:T(8,128)(2,1)S(1)} %fusion.6), channel_id=1, source_target_pairs={{0,17},{1,8},{2,11},{3,18},{4,13},{5,20},{6,23},{7,14},{8,1},{9,24... | collective-permute-start | bytes 184328 | tf_op jit(solution)/shard_map/ppermute | solution.py:37
  22.5 4.7 %collective-permute-start.10 = (bf16[240,128]{1,0:T(8,128)(2,1)S(1)}, bf16[240,128]{1,0:T(8,128)(2,1)S(1)}, u32[]{:S(2)}, u32[]{:S(2)}) collective-permute-start(bf16[240,128]{1,0:T(8,128)(2,1)S(1)} %fusion.7), channel_id=1, source_target_pairs={{0,17},{1,8},{2,11},{3,18},{4,13},{5,20},{6,23},{7,14},{8,1},{9,24... | collective-permute-start | bytes 184328 | tf_op jit(solution)/shard_map/ppermute | solution.py:37
  24.9 3.8 %collective-permute-start.5 = (bf16[240,128]{1,0:T(8,128)(2,1)S(1)}, bf16[240,128]{1,0:T(8,128)(2,1)S(1)}, u32[]{:S(2)}, u32[]{:S(2)}) collective-permute-start(bf16[240,128]{1,0:T(8,128)(2,1)S(1)} %add_convert_fusion.1), channel_id=1, source_target_pairs={{0,3},{1,4},{2,7},{3,0},{4,1},{5,6},{6,5},{7,2},{8,13},{9,10},{10,... | collective-permute-start | bytes 184328 | tf_op jit(solution)/shard_map/ppermute | solution.py:37
  27.2 3.7 %collective-permute-start.11 = (bf16[240,128]{1,0:T(8,128)(2,1)S(1)}, bf16[240,128]{1,0:T(8,128)(2,1)S(1)}, u32[]{:S(2)}, u32[]{:S(2)}) collective-permute-start(bf16[240,128]{1,0:T(8,128)(2,1)S(1)} %add_convert_fusion), channel_id=1, source_target_pairs={{0,3},{1,4},{2,7},{3,0},{4,1},{5,6},{6,5},{7,2},{8,13},{9,10},{10,... | collective-permute-start | bytes 184328 | tf_op jit(solution)/shard_map/ppermute | solution.py:37
  28.8 3.0 %collective-permute-start.12 = (bf16[2,240,128]{2,1,0:T(8,128)(2,1)S(1)}, bf16[2,240,128]{2,1,0:T(8,128)(2,1)S(1)}, u32[]{:S(2)}, u32[]{:S(2)}) collective-permute-start(bf16[2,240,128]{2,1,0:T(8,128)(2,1)S(1)} %pad_maximum_fusion.mine_0), channel_id=1, source_target_pairs={{0,1},{1,0},{2,3},{3,2},{4,5},{5,4},{6,7},{7,6},{8,9},{9,8},{10,11... | collective-permute-start | bytes 368648 | tf_op jit(solution)/shard_map/ppermute | solution.py:37
  30.9 1.5 %collective-permute-start.13 = (bf16[2,240,128]{2,1,0:T(8,128)(2,1)S(1)}, bf16[2,240,128]{2,1,0:T(8,128)(2,1)S(1)}, u32[]{:S(2)}, u32[]{:S(2)}) collective-permute-start(bf16[2,240,128]{2,1,0:T(8,128)(2,1)S(1)} %pad_maximum_fusion.1.mine_1), channel_id=1, source_target_pairs={{0,1},{1,0},{2,3},{3,2},{4,5},{5,4},{6,7},{7,6},{8,9},{9,8},{10,11... | collective-permute-start | bytes 368648 | tf_op jit(solution)/shard_map/ppermute | solution.py:37

commit v6 on v4

--- a/solution.py
+++ b/solution.py
@@ -117,28 +117,31 @@
                 acc_ref[rows, :stop] = piece
     me = my_index(n_orb)
     mine = half_of(me, n_dev)
-    n_rows = n_tiles * n_occ // 8
-    for chain in (0, 1):
-        for ref, side in zip(part_refs[chain::2], (mine, 1 - mine)):
+    chains = len(part_refs) // 2
+    n_rows = n_tiles * n_occ // (4 * chains)
+    for chain in range(chains):
+        for ref, side in zip(part_refs[chain::chains], (mine, 1 - mine)):
             lead = jnp.where(side == 0, bit(me, tracks[0][0]), bit(me, tracks[1][0]))
             for j in (0, 1):
-                start = pl.multiple_of((side * 4 + chain * 2 + (lead + j) % 2) * n_rows, n_rows)
+                start = pl.multiple_of(((side * chains + chain) * 2 + (lead + j) % 2) * n_rows, n_rows)
                 ref[j] = acc_ref[pl.ds(start, n_rows), :].astype(ref.dtype)
 
 
-def rotation_kernel(n_orb, n_dev, tracks, mine_0, mine_1, other_0, other_1, hess_ref, sel_ref, chosen_ref, left_ref, rot_ref, fock_ref, u_ref):
+def rotation_kernel(n_orb, n_dev, tracks, *refs):
+    *held_refs, hess_ref, sel_ref, chosen_ref, left_ref, rot_ref, fock_ref, u_ref = refs
+    chains = len(held_refs) // 2
+    mine_refs, other_refs = held_refs[:chains], held_refs[chains:]
     n_occ, width = fock_ref.shape
     base = n_occ // LANES * LANES
     n_mo = chosen_ref.shape[0]
-    mine_refs, other_refs = (mine_0, mine_1), (other_0, other_1)
-    n_rows = mine_0.shape[1]
+    n_rows = mine_refs[0].shape[1]
     step = math.gcd(n_rows, n_occ)
     me = my_index(n_orb)
     mine = half_of(me, n_dev)
-    for start in range(0, 8 * n_rows, step):
+    for start in range(0, 4 * chains * n_rows, step):
         tile, row = divmod(start, n_occ)
         piece, at = divmod(start, n_rows)
-        side, chain, j = piece // 4, piece // 2 % 2, piece % 2
+        side, chain, j = piece // (2 * chains), piece // 2 % chains, piece % 2
         place = (j + bit(me, tracks[side][0])) % 2
         rows = slice(at, at + step)
         fock_ref[row : row + step, tile * LANES : (tile + 1) * LANES] = jnp.where(
@@ -271,17 +274,16 @@
     whole = lambda *shape: pl.BlockSpec(shape, lambda *_: (0,) * len(shape))
     in_vmem = pl.BlockSpec(memory_space=pltpu.VMEM)
 
-    half_shape = (2, tiles * n_occ // 8, LANES)
+    chains = 3
+    half_shape = (2, tiles * n_occ // (4 * chains), LANES)
     in_hbm = pl.BlockSpec(memory_space=pltpu.HBM)
     *parts, three_vmem = pl.pallas_call(
         functools.partial(fock_kernel, n_orb, n_dev, tracks),
         in_specs=[in_hbm, in_hbm],
-        out_specs=[in_vmem] * 5,
+        out_specs=[in_vmem] * (2 * chains + 1),
         out_shape=[
-            jax.ShapeDtypeStruct(half_shape, F32),
-            jax.ShapeDtypeStruct(half_shape, F32),
-            jax.ShapeDtypeStruct(half_shape, BF16),
-            jax.ShapeDtypeStruct(half_shape, BF16),
+            *[jax.ShapeDtypeStruct(half_shape, F32)] * chains,
+            *[jax.ShapeDtypeStruct(half_shape, BF16)] * chains,
             jax.ShapeDtypeStruct(three_index.shape, BF16),
         ],
         scratch_shapes=[
@@ -300,8 +302,8 @@
 
     masks = [[1 | 1 << tracks[half_of(d, n_dev)][k] for d in range(n_dev)] for k in range(len(tracks[0]))]
     held, other = [], []
-    for chain in (0, 1):
-        part = parts[chain] + swap(parts[2 + chain], [1] * n_dev).astype(F32)
+    for chain in range(chains):
+        part = parts[chain] + swap(parts[chains + chain], [1] * n_dev).astype(F32)
         piece = part[0] + swap(part[1].astype(BF16), masks[0]).astype(F32)
         for mask in masks[1:]:
             piece = piece + swap(piece.astype(BF16), mask).astype(F32)
@@ -323,7 +325,7 @@
     wide = base + width
     chosen, left, rot = pl.pallas_call(
         functools.partial(rotation_kernel, n_orb, n_dev, tracks),
-        in_specs=[in_vmem] * 6,
+        in_specs=[in_vmem] * (2 * chains + 2),
         out_specs=[in_vmem] * 3,
         out_shape=[
             jax.ShapeDtypeStruct((n_mo, n_rows * n_dev), BF16),

time: 71.2 us -> 71.1 us (level)
  starting transfers between devices: 18.6 us -> 24.4 us
  waiting for transfers between devices: 7.68 us -> 3.14 us
  blocking collectives: 31.3 us -> 29.9 us
    ppermute x14 -> x21, starting transfers between devices: 18.6 us -> 24.4 us  [swap(): lax.ppermute(x, BOTH, [(d, d ^ mask) for d, mask in enumerate(masks)])]
    ppermute x14 -> x21, waiting for transfers between devices: 7.68 us -> 3.14 us  [swap(): lax.ppermute(x, BOTH, [(d, d ^ mask) for d, mask in enumerate(masks)])]
    all_to_all x1, blocking collectives: 31.3 us -> 29.9 us  [on_device(): lax.all_to_all(sent, BOTH, 0, 0, tiled=True)]
  transfers between devices with their start and end apart: 14 -> 21, of which waited for: 10 -> 7; matrix products, arithmetic and copies ran while one was open for 1% -> 1% of each run, Pallas kernels for 0% -> 0%
where the time goes in v6:
time: 71.1 us; the launch traced here: 70.9 us
  blocking collectives  29.9 us (42%)
  starting transfers between devices  24.4 us (34%)
  Pallas kernels  12.7 us (18%)
  waiting for transfers between devices  3.14 us (4%)
    all_to_all x1, blocking collectives, on_device(): lax.all_to_all(sent, BOTH, 0, 0, tiled=True)  29.9 us
    ppermute x21, starting transfers between devices, swap(): lax.ppermute(x, BOTH, [(d, d ^ mask) for d, mask in enumerate(masks)])  24.4 us
    pallas_call x1, Pallas kernels, on_device(): pl.pallas_call(functools.partial(fock_kernel, n_orb, n_dev, tracks), in_s...  5.17 us
    pallas_call x1, Pallas kernels, on_device(): pl.pallas_call(functools.partial(half_kernel, n_rows, main), in_specs=[in...  3.47 us
    ppermute x21, waiting for transfers between devices, swap(): lax.ppermute(x, BOTH, [(d, d ^ mask) for d, mask in enumerate(masks)])  3.14 us
    pallas_call x1, Pallas kernels, on_device(): pl.pallas_call(functools.partial(owner_kernel, n_rows, aux_step, q_loc, r...  2.41 us
    pallas_call x1, Pallas kernels, on_device(): pl.pallas_call(functools.partial(rotation_kernel, n_orb, n_dev, tracks),...  1.6 us
  transfers between devices with their start and end apart: 21, of which 7 were waited for; matrix products, arithmetic and copies ran while one was open for 1% of the time, Pallas kernels for 0%

profile of v6, /device:TPU:0, one launch (start us, length us, event | category | flops | bytes accessed | tf_op | source)
XLA Modules:
  0.0 70.9 jit_solution(13141192287985470063)
XLA Ops:
  0.0 5.2 %fock.1 = (f32[2,160,128]{2,1,0:T(8,128)S(1)}, f32[2,160,128]{2,1,0:T(8,128)S(1)}, f32[2,160,128]{2,1,0:T(8,128)S(1)}, bf16[2,160,128]{2,1,0:T(8,128)(2,1)S(1)},...) custom-call(bf16[8,400,1600]{2,1,0:T(8,128)(2,1)} %three_hbm.1, ...), custom_call_target="tpu_custom_call" | custom-call | flops 1638400000 | bytes 10240000 | tf_op jit(solution)/shard_map/fock/pallas_call | solution.py:280
  5.2 0.5 collective-permute-start
  6.7 2.7 %collective-permute-start.1 = (bf16[160,128]{1,0:T(8,128)(2,1)S(1)}, bf16[160,128]{1,0:T(8,128)(2,1)S(1)}, u32[]{:S(2)}, u32[]{:S(2)}) collective-permute-start(bf16[160,128]{1,0:T(8,128)(2,1)S(1)} %fusion.6), channel_id=1, source_target_pairs={{0,3},{1,4},{2,7},{3,0},{4,1},{5,6},{6,5},{7,2},{8,13},{9,10},{10,... | collective-permute-start | bytes 122888 | tf_op jit(solution)/shard_map/ppermute | solution.py:37
  9.7 1.6 %collective-permute-start.13 = (bf16[160,128]{1,0:T(8,128)(2,1)S(1)}, bf16[160,128]{1,0:T(8,128)(2,1)S(1)}, u32[]{:S(2)}, u32[]{:S(2)}) collective-permute-start(bf16[160,128]{1,0:T(8,128)(2,1)S(1)} %fusion.8), channel_id=1, source_target_pairs={{0,3},{1,4},{2,7},{3,0},{4,1},{5,6},{6,5},{7,2},{8,13},{9,10},{10,... | collective-permute-start | bytes 122888 | tf_op jit(solution)/shard_map/ppermute | solution.py:37
  11.3 1.9 %collective-permute-start.2 = (bf16[160,128]{1,0:T(8,128)(2,1)S(1)}, bf16[160,128]{1,0:T(8,128)(2,1)S(1)}, u32[]{:S(2)}, u32[]{:S(2)}) collective-permute-start(bf16[160,128]{1,0:T(8,128)(2,1)S(1)} %fusion.12), channel_id=1, source_target_pairs={{0,5},{1,2},{2,1},{3,6},{4,7},{5,0},{6,3},{7,4},{8,11},{9,12},{10,... | collective-permute-start | bytes 122888 | tf_op jit(solution)/shard_map/ppermute | solution.py:37
  13.2 1.5 %collective-permute-start.8 = (bf16[160,128]{1,0:T(8,128)(2,1)S(1)}, bf16[160,128]{1,0:T(8,128)(2,1)S(1)}, u32[]{:S(2)}, u32[]{:S(2)}) collective-permute-start(bf16[160,128]{1,0:T(8,128)(2,1)S(1)} %fusion.13), channel_id=1, source_target_pairs={{0,5},{1,2},{2,1},{3,6},{4,7},{5,0},{6,3},{7,4},{8,11},{9,12},{10,... | collective-permute-start | bytes 122888 | tf_op jit(solution)/shard_map/ppermute | solution.py:37
  15.1 1.6 %collective-permute-start.3 = (bf16[160,128]{1,0:T(8,128)(2,1)S(1)}, bf16[160,128]{1,0:T(8,128)(2,1)S(1)}, u32[]{:S(2)}, u32[]{:S(2)}) collective-permute-start(bf16[160,128]{1,0:T(8,128)(2,1)S(1)} %fusion.3), channel_id=1, source_target_pairs={{0,9},{1,16},{2,19},{3,10},{4,21},{5,12},{6,15},{7,22},{8,25},{9,0... | collective-permute-start | bytes 122888 | tf_op jit(solution)/shard_map/ppermute | solution.py:37
  16.7 1.6 %collective-permute-start.9 = (bf16[160,128]{1,0:T(8,128)(2,1)S(1)}, bf16[160,128]{1,0:T(8,128)(2,1)S(1)}, u32[]{:S(2)}, u32[]{:S(2)}) collective-permute-start(bf16[160,128]{1,0:T(8,128)(2,1)S(1)} %fusion.4), channel_id=1, source_target_pairs={{0,9},{1,16},{2,19},{3,10},{4,21},{5,12},{6,15},{7,22},{8,25},{9,0... | collective-permute-start | bytes 122888 | tf_op jit(solution)/shard_map/ppermute | solution.py:37
  18.3 1.3 %collective-permute-start.15 = (bf16[160,128]{1,0:T(8,128)(2,1)S(1)}, bf16[160,128]{1,0:T(8,128)(2,1)S(1)}, u32[]{:S(2)}, u32[]{:S(2)}) collective-permute-start(bf16[160,128]{1,0:T(8,128)(2,1)S(1)} %fusion.5), channel_id=1, source_target_pairs={{0,9},{1,16},{2,19},{3,10},{4,21},{5,12},{6,15},{7,22},{8,25},{9,0... | collective-permute-start | bytes 122888 | tf_op jit(solution)/shard_map/ppermute | solution.py:37
  19.6 2.7 %collective-permute-start.4 = (bf16[160,128]{1,0:T(8,128)(2,1)S(1)}, bf16[160,128]{1,0:T(8,128)(2,1)S(1)}, u32[]{:S(2)}, u32[]{:S(2)}) collective-permute-start(bf16[160,128]{1,0:T(8,128)(2,1)S(1)} %fusion.9), channel_id=1, source_target_pairs={{0,17},{1,8},{2,11},{3,18},{4,13},{5,20},{6,23},{7,14},{8,1},{9,24... | collective-permute-start | bytes 122888 | tf_op jit(solution)/shard_map/ppermute | solution.py:37
  22.3 0.9 %collective-permute-start.10 = (bf16[160,128]{1,0:T(8,128)(2,1)S(1)}, bf16[160,128]{1,0:T(8,128)(2,1)S(1)}, u32[]{:S(2)}, u32[]{:S(2)}) collective-permute-start(bf16[160,128]{1,0:T(8,128)(2,1)S(1)} %fusion.10), channel_id=1, source_target_pairs={{0,17},{1,8},{2,11},{3,18},{4,13},{5,20},{6,23},{7,14},{8,1},{9,24... | collective-permute-start | bytes 122888 | tf_op jit(solution)/shard_map/ppermute | solution.py:37
  23.3 1.9 %collective-permute-start.16 = (bf16[160,128]{1,0:T(8,128)(2,1)S(1)}, bf16[160,128]{1,0:T(8,128)(2,1)S(1)}, u32[]{:S(2)}, u32[]{:S(2)}) collective-permute-start(bf16[160,128]{1,0:T(8,128)(2,1)S(1)} %fusion.11), channel_id=1, source_target_pairs={{0,17},{1,8},{2,11},{3,18},{4,13},{5,20},{6,23},{7,14},{8,1},{9,24... | collective-permute-start | bytes 122888 | tf_op jit(solution)/shard_map/ppermute | solution.py:37
  25.4 1.0 %collective-permute-start.5 = (bf16[160,128]{1,0:T(8,128)(2,1)S(1)}, bf16[160,128]{1,0:T(8,128)(2,1)S(1)}, u32[]{:S(2)}, u32[]{:S(2)}) collective-permute-start(bf16[160,128]{1,0:T(8,128)(2,1)S(1)} %add_convert_fusion.2), channel_id=1, source_target_pairs={{0,3},{1,4},{2,7},{3,0},{4,1},{5,6},{6,5},{7,2},{8,13},{9,10},{10,... | collective-permute-start | bytes 122888 | tf_op jit(solution)/shard_map/ppermute | solution.py:37
  26.4 0.5 collective-permute-done.10
  27.7 1.1 %collective-permute-start.17 = (bf16[160,128]{1,0:T(8,128)(2,1)S(1)}, bf16[160,128]{1,0:T(8,128)(2,1)S(1)}, u32[]{:S(2)}, u32[]{:S(2)}) collective-permute-start(bf16[160,128]{1,0:T(8,128)(2,1)S(1)} %add_convert_fusion), channel_id=1, source_target_pairs={{0,3},{1,4},{2,7},{3,0},{4,1},{5,6},{6,5},{7,2},{8,13},{9,10},{10,... | collective-permute-start | bytes 122888 | tf_op jit(solution)/shard_map/ppermute | solution.py:37
  28.9 1.0 %collective-permute-start.18 = (bf16[2,160,128]{2,1,0:T(8,128)(2,1)S(1)}, bf16[2,160,128]{2,1,0:T(8,128)(2,1)S(1)}, u32[]{:S(2)}, u32[]{:S(2)}) collective-permute-start(bf16[2,160,128]{2,1,0:T(8,128)(2,1)S(1)} %pad_maximum_fusion.refs_0_), channel_id=1, source_target_pairs={{0,1},{1,0},{2,3},{3,2},{4,5},{5,4},{6,7},{7,6},{8,9},{9,8},{10,11... | collective-permute-start | bytes 245768 | tf_op jit(solution)/shard_map/ppermute | solution.py:37
  29.9 0.5 collective-permute-done.11
  30.6 0.6 collective-permute-done.17
  31.2 1.4 %collective-permute-start.20 = (bf16[2,160,128]{2,1,0:T(8,128)(2,1)S(1)}, bf16[2,160,128]{2,1,0:T(8,128)(2,1)S(1)}, u32[]{:S(2)}, u32[]{:S(2)}) collective-permute-start(bf16[2,160,128]{2,1,0:T(8,128)(2,1)S(1)} %pad_maximum_fusion.2.refs_2_), channel_id=1, source_target_pairs={{0,1},{1,0},{2,3},{3,2},{4,5},{5,4},{6,7},{7,6},{8,9},{9,8},{10,11... | collective-permute-start | bytes 245768 | tf_op jit(solution)/shard_map/ppermute | solution.py:37
  32.9 0.6 collective-permute-done.20.refs_5_
  33.5 1.6 %rotation.1 = (bf16[1600,160]{1,0:T(8,128)(2,1)S(1)}, bf16[160,1664]{1,0:T(8,128)(2,1)S(1)}, bf16[160,1536]{1,0:T(8,128)(2,1)S(1)}) custom-call(bf16[2,160,128]{2,1,0:T(8,128)(2,1)S(1)} %pad_maximum_fusion.refs_0_, bf16[2,160,128]{2,1,0:T(8,128)(2,1)S(1)} %pad_maximum_fusion.1.refs_1_, bf16[2,160,128]{2,1,0:T(8,128)(2,1)S(1)} %pad_maximum_fusion.2.refs_2_, ...), custom_call_target="tpu_custom_call" | custom-call | flops 327680000 | bytes 4194304 | tf_op jit(solution)/shard_map/rotation/pallas_call | solution.py:326
  35.1 3.5 %half_rotation.1 = bf16[32,128,128]{2,1,0:T(8,128)(2,1)S(1)} custom-call(bf16[1600,160]{1,0:T(8,128)(2,1)S(1)} %get-tuple-element.21.chosen_ref, bf16[8,400,1600]{2,1,0:T(8,128)(2,1)S(1)} %get-tuple-element.22.three_ref), custom_call_target="tpu_custom_call" | custom-call | flops 1638400000 | bytes 10240000 | tf_op jit(solution)/shard_map/half_rotation/pallas_call | solution.py:340
  38.6 29.9 %all_to_all.5 = bf16[32,128,128]{2,1,0:T(8,128)(2,1)S(1)} all-to-all(bf16[32,128,128]{2,1,0:T(8,128)(2,1)S(1)} %half_rotation.1), channel_id=1, replica_groups=mesh['aux'=8,'orb'=4] {'aux','orb'}, dimensions={0} | all-to-all | bytes 2097152 | tf_op jit(solution)/shard_map/all_to_all | solution.py:355
  68.5 2.4 %owner_rows.1 = bf16[64,7200]{1,0:T(8,128)(2,1)} custom-call(bf16[8,4,128,128]{3,2,1,0:T(8,128)(2,1)S(1)} %bitcast.52, bf16[160,1664]{1,0:T(8,128)(2,1)S(1)} %get-tuple-element.23.left_ref, bf16[160,1536]{1,0:T(8,128)(2,1)S(1)} %get-tuple-element.24.rot_ref), custom_call_target="tpu_custom_call" | custom-call | flops 327680000 | bytes 8388608 | tf_op jit(solution)/shard_map/owner_rows/pallas_call | solution.py:357
  (49 shorter events, 3.5 us)
Async XLA Ops:
  0.0 33.5 %copy-start = (bf16[160,160]{1,0:T(8,128)(2,1)S(1)}, bf16[160,160]{1,0:T(8,128)(2,1)}, u32[]{:S(2)}) copy-start(bf16[160,160]{1,0:T(8,128)(2,1)} %constant.4.clone.refs_7_) | copy-start | bytes 153604
  0.0 32.6 %copy-start.1 = (f32[1440,160]{0,1:T(8,128)S(1)}, f32[1440,160]{0,1:T(8,128)}, u32[]{:S(2)}) copy-start(f32[1440,160]{0,1:T(8,128)} %param.6) | copy-start | bytes 2764804
  5.2 1.4 %collective-permute-start = (bf16[2,160,128]{2,1,0:T(8,128)(2,1)S(1)}, bf16[2,160,128]{2,1,0:T(8,128)(2,1)S(1)}, u32[]{:S(2)}, u32[]{:S(2)}) collective-permute-start(bf16[2,160,128]{2,1,0:T(8,128)(2,1)S(1)} %get-tuple-element.16), channel_id=1, source_target_pairs={{0,1},{1,0},{2,3},{3,2},{4,5},{5,4},{6,7},{7,6},{8,9},{9,8},{10,11... | collective-permute-start | bytes 245768 | tf_op jit(solution)/shard_map/ppermute | solution.py:37
  5.7 3.6 %collective-permute-start.6 = (bf16[2,160,128]{2,1,0:T(8,128)(2,1)S(1)}, bf16[2,160,128]{2,1,0:T(8,128)(2,1)S(1)}, u32[]{:S(2)}, u32[]{:S(2)}) collective-permute-start(bf16[2,160,128]{2,1,0:T(8,128)(2,1)S(1)} %get-tuple-element.18), channel_id=1, source_target_pairs={{0,1},{1,0},{2,3},{3,2},{4,5},{5,4},{6,7},{7,6},{8,9},{9,8},{10,11... | collective-permute-start | bytes 245768 | tf_op jit(solution)/shard_map/ppermute | solution.py:37
  5.8 3.9 %collective-permute-start.12 = (bf16[2,160,128]{2,1,0:T(8,128)(2,1)S(1)}, bf16[2,160,128]{2,1,0:T(8,128)(2,1)S(1)}, u32[]{:S(2)}, u32[]{:S(2)}) collective-permute-start(bf16[2,160,128]{2,1,0:T(8,128)(2,1)S(1)} %get-tuple-element.20), channel_id=1, source_target_pairs={{0,1},{1,0},{2,3},{3,2},{4,5},{5,4},{6,7},{7,6},{8,9},{9,8},{10,11... | collective-permute-start | bytes 245768 | tf_op jit(solution)/shard_map/ppermute | solution.py:37
  6.7 4.6 %collective-permute-start.1 = (bf16[160,128]{1,0:T(8,128)(2,1)S(1)}, bf16[160,128]{1,0:T(8,128)(2,1)S(1)}, u32[]{:S(2)}, u32[]{:S(2)}) collective-permute-start(bf16[160,128]{1,0:T(8,128)(2,1)S(1)} %fusion.6), channel_id=1, source_target_pairs={{0,3},{1,4},{2,7},{3,0},{4,1},{5,6},{6,5},{7,2},{8,13},{9,10},{10,... | collective-permute-start | bytes 122888 | tf_op jit(solution)/shard_map/ppermute | solution.py:37
  9.4 3.8 %collective-permute-start.7 = (bf16[160,128]{1,0:T(8,128)(2,1)S(1)}, bf16[160,128]{1,0:T(8,128)(2,1)S(1)}, u32[]{:S(2)}, u32[]{:S(2)}) collective-permute-start(bf16[160,128]{1,0:T(8,128)(2,1)S(1)} %fusion.7), channel_id=1, source_target_pairs={{0,3},{1,4},{2,7},{3,0},{4,1},{5,6},{6,5},{7,2},{8,13},{9,10},{10,... | collective-permute-start | bytes 122888 | tf_op jit(solution)/shard_map/ppermute | solution.py:37
  9.7 5.0 %collective-permute-start.13 = (bf16[160,128]{1,0:T(8,128)(2,1)S(1)}, bf16[160,128]{1,0:T(8,128)(2,1)S(1)}, u32[]{:S(2)}, u32[]{:S(2)}) collective-permute-start(bf16[160,128]{1,0:T(8,128)(2,1)S(1)} %fusion.8), channel_id=1, source_target_pairs={{0,3},{1,4},{2,7},{3,0},{4,1},{5,6},{6,5},{7,2},{8,13},{9,10},{10,... | collective-permute-start | bytes 122888 | tf_op jit(solution)/shard_map/ppermute | solution.py:37
  11.3 3.8 %collective-permute-start.2 = (bf16[160,128]{1,0:T(8,128)(2,1)S(1)}, bf16[160,128]{1,0:T(8,128)(2,1)S(1)}, u32[]{:S(2)}, u32[]{:S(2)}) collective-permute-start(bf16[160,128]{1,0:T(8,128)(2,1)S(1)} %fusion.12), channel_id=1, source_target_pairs={{0,5},{1,2},{2,1},{3,6},{4,7},{5,0},{6,3},{7,4},{8,11},{9,12},{10,... | collective-permute-start | bytes 122888 | tf_op jit(solution)/shard_map/ppermute | solution.py:37
  13.2 3.5 %collective-permute-start.8 = (bf16[160,128]{1,0:T(8,128)(2,1)S(1)}, bf16[160,128]{1,0:T(8,128)(2,1)S(1)}, u32[]{:S(2)}, u32[]{:S(2)}) collective-permute-start(bf16[160,128]{1,0:T(8,128)(2,1)S(1)} %fusion.13), channel_id=1, source_target_pairs={{0,5},{1,2},{2,1},{3,6},{4,7},{5,0},{6,3},{7,4},{8,11},{9,12},{10,... | collective-permute-start | bytes 122888 | tf_op jit(solution)/shard_map/ppermute | solution.py:37
  14.7 3.6 %collective-permute-start.14 = (bf16[160,128]{1,0:T(8,128)(2,1)S(1)}, bf16[160,128]{1,0:T(8,128)(2,1)S(1)}, u32[]{:S(2)}, u32[]{:S(2)}) collective-permute-start(bf16[160,128]{1,0:T(8,128)(2,1)S(1)} %fusion.14), channel_id=1, source_target_pairs={{0,5},{1,2},{2,1},{3,6},{4,7},{5,0},{6,3},{7,4},{8,11},{9,12},{10,... | collective-permute-start | bytes 122888 | tf_op jit(solution)/shard_map/ppermute | solution.py:37
  15.1 4.5 %collective-permute-start.3 = (bf16[160,128]{1,0:T(8,128)(2,1)S(1)}, bf16[160,128]{1,0:T(8,128)(2,1)S(1)}, u32[]{:S(2)}, u32[]{:S(2)}) collective-permute-start(bf16[160,128]{1,0:T(8,128)(2,1)S(1)} %fusion.3), channel_id=1, source_target_pairs={{0,9},{1,16},{2,19},{3,10},{4,21},{5,12},{6,15},{7,22},{8,25},{9,0... | collective-permute-start | bytes 122888 | tf_op jit(solution)/shard_map/ppermute | solution.py:37
  16.7 5.6 %collective-permute-start.9 = (bf16[160,128]{1,0:T(8,128)(2,1)S(1)}, bf16[160,128]{1,0:T(8,128)(2,1)S(1)}, u32[]{:S(2)}, u32[]{:S(2)}) collective-permute-start(bf16[160,128]{1,0:T(8,128)(2,1)S(1)} %fusion.4), channel_id=1, source_target_pairs={{0,9},{1,16},{2,19},{3,10},{4,21},{5,12},{6,15},{7,22},{8,25},{9,0... | collective-permute-start | bytes 122888 | tf_op jit(solution)/shard_map/ppermute | solution.py:37
  18.3 4.9 %collective-permute-start.15 = (bf16[160,128]{1,0:T(8,128)(2,1)S(1)}, bf16[160,128]{1,0:T(8,128)(2,1)S(1)}, u32[]{:S(2)}, u32[]{:S(2)}) collective-permute-start(bf16[160,128]{1,0:T(8,128)(2,1)S(1)} %fusion.5), channel_id=1, source_target_pairs={{0,9},{1,16},{2,19},{3,10},{4,21},{5,12},{6,15},{7,22},{8,25},{9,0... | collective-permute-start | bytes 122888 | tf_op jit(solution)/shard_map/ppermute | solution.py:37
  19.6 5.7 %collective-permute-start.4 = (bf16[160,128]{1,0:T(8,128)(2,1)S(1)}, bf16[160,128]{1,0:T(8,128)(2,1)S(1)}, u32[]{:S(2)}, u32[]{:S(2)}) collective-permute-start(bf16[160,128]{1,0:T(8,128)(2,1)S(1)} %fusion.9), channel_id=1, source_target_pairs={{0,17},{1,8},{2,11},{3,18},{4,13},{5,20},{6,23},{7,14},{8,1},{9,24... | collective-permute-start | bytes 122888 | tf_op jit(solution)/shard_map/ppermute | solution.py:37
  22.3 4.5 %collective-permute-start.10 = (bf16[160,128]{1,0:T(8,128)(2,1)S(1)}, bf16[160,128]{1,0:T(8,128)(2,1)S(1)}, u32[]{:S(2)}, u32[]{:S(2)}) collective-permute-start(bf16[160,128]{1,0:T(8,128)(2,1)S(1)} %fusion.10), channel_id=1, source_target_pairs={{0,17},{1,8},{2,11},{3,18},{4,13},{5,20},{6,23},{7,14},{8,1},{9,24... | collective-permute-start | bytes 122888 | tf_op jit(solution)/shard_map/ppermute | solution.py:37
  23.3 4.4 %collective-permute-start.16 = (bf16[160,128]{1,0:T(8,128)(2,1)S(1)}, bf16[160,128]{1,0:T(8,128)(2,1)S(1)}, u32[]{:S(2)}, u32[]{:S(2)}) collective-permute-start(bf16[160,128]{1,0:T(8,128)(2,1)S(1)} %fusion.11), channel_id=1, source_target_pairs={{0,17},{1,8},{2,11},{3,18},{4,13},{5,20},{6,23},{7,14},{8,1},{9,24... | collective-permute-start | bytes 122888 | tf_op jit(solution)/shard_map/ppermute | solution.py:37
  25.4 3.5 %collective-permute-start.5 = (bf16[160,128]{1,0:T(8,128)(2,1)S(1)}, bf16[160,128]{1,0:T(8,128)(2,1)S(1)}, u32[]{:S(2)}, u32[]{:S(2)}) collective-permute-start(bf16[160,128]{1,0:T(8,128)(2,1)S(1)} %add_convert_fusion.2), channel_id=1, source_target_pairs={{0,3},{1,4},{2,7},{3,0},{4,1},{5,6},{6,5},{7,2},{8,13},{9,10},{10,... | collective-permute-start | bytes 122888 | tf_op jit(solution)/shard_map/ppermute | solution.py:37
  26.9 3.5 %collective-permute-start.11 = (bf16[160,128]{1,0:T(8,128)(2,1)S(1)}, bf16[160,128]{1,0:T(8,128)(2,1)S(1)}, u32[]{:S(2)}, u32[]{:S(2)}) collective-permute-start(bf16[160,128]{1,0:T(8,128)(2,1)S(1)} %add_convert_fusion.1), channel_id=1, source_target_pairs={{0,3},{1,4},{2,7},{3,0},{4,1},{5,6},{6,5},{7,2},{8,13},{9,10},{10,... | collective-permute-start | bytes 122888 | tf_op jit(solution)/shard_map/ppermute | solution.py:37
  27.7 3.5 %collective-permute-start.17 = (bf16[160,128]{1,0:T(8,128)(2,1)S(1)}, bf16[160,128]{1,0:T(8,128)(2,1)S(1)}, u32[]{:S(2)}, u32[]{:S(2)}) collective-permute-start(bf16[160,128]{1,0:T(8,128)(2,1)S(1)} %add_convert_fusion), channel_id=1, source_target_pairs={{0,3},{1,4},{2,7},{3,0},{4,1},{5,6},{6,5},{7,2},{8,13},{9,10},{10,... | collective-permute-start | bytes 122888 | tf_op jit(solution)/shard_map/ppermute | solution.py:37
  28.9 4.0 %collective-permute-start.18 = (bf16[2,160,128]{2,1,0:T(8,128)(2,1)S(1)}, bf16[2,160,128]{2,1,0:T(8,128)(2,1)S(1)}, u32[]{:S(2)}, u32[]{:S(2)}) collective-permute-start(bf16[2,160,128]{2,1,0:T(8,128)(2,1)S(1)} %pad_maximum_fusion.refs_0_), channel_id=1, source_target_pairs={{0,1},{1,0},{2,3},{3,2},{4,5},{5,4},{6,7},{7,6},{8,9},{9,8},{10,11... | collective-permute-start | bytes 245768 | tf_op jit(solution)/shard_map/ppermute | solution.py:37
  30.4 2.5 %collective-permute-start.19 = (bf16[2,160,128]{2,1,0:T(8,128)(2,1)S(1)}, bf16[2,160,128]{2,1,0:T(8,128)(2,1)S(1)}, u32[]{:S(2)}, u32[]{:S(2)}) collective-permute-start(bf16[2,160,128]{2,1,0:T(8,128)(2,1)S(1)} %pad_maximum_fusion.1.refs_1_), channel_id=1, source_target_pairs={{0,1},{1,0},{2,3},{3,2},{4,5},{5,4},{6,7},{7,6},{8,9},{9,8},{10,11... | collective-permute-start | bytes 245768 | tf_op jit(solution)/shard_map/ppermute | solution.py:37
  31.2 2.3 %collective-permute-start.20 = (bf16[2,160,128]{2,1,0:T(8,128)(2,1)S(1)}, bf16[2,160,128]{2,1,0:T(8,128)(2,1)S(1)}, u32[]{:S(2)}, u32[]{:S(2)}) collective-permute-start(bf16[2,160,128]{2,1,0:T(8,128)(2,1)S(1)} %pad_maximum_fusion.2.refs_2_), channel_id=1, source_target_pairs={{0,1},{1,0},{2,3},{3,2},{4,5},{5,4},{6,7},{7,6},{8,9},{9,8},{10,11... | collective-permute-start | bytes 245768 | tf_op jit(solution)/shard_map/ppermute | solution.py:37

commit v7 on v6

--- a/solution.py
+++ b/solution.py
@@ -127,20 +127,34 @@
                 ref[j] = acc_ref[pl.ds(start, n_rows), :].astype(ref.dtype)
 
 
-def rotation_kernel(n_orb, n_dev, tracks, *refs):
-    *held_refs, hess_ref, sel_ref, chosen_ref, left_ref, rot_ref, fock_ref, u_ref = refs
+def swap_rows(tiles):
+    row = lax.broadcasted_iota(jnp.int32, tiles[0].shape, 0)
+    for step in (1, 2, 4):
+        low = (row // step) % 2 == 0
+        after = list(tiles)
+        for t in range(8):
+            if t & step == 0:
+                first, second = tiles[t], tiles[t | step]
+                after[t] = jnp.where(low, first, pltpu.roll(second, step, 0))
+                after[t | step] = jnp.where(low, pltpu.roll(first, 8 - step, 0), second)
+        tiles = after
+    return tiles
+
+
+def rotate_kernel(n_orb, n_dev, tracks, n_rows, main, *refs):
+    *held_refs, hess_ref, sel_ref, three_ref, sent_ref, left_ref, rot_ref, fock_ref, u_ref, chosen_ref, rem_ref, half_ref = refs
     chains = len(held_refs) // 2
     mine_refs, other_refs = held_refs[:chains], held_refs[chains:]
     n_occ, width = fock_ref.shape
     base = n_occ // LANES * LANES
     n_mo = chosen_ref.shape[0]
-    n_rows = mine_refs[0].shape[1]
-    step = math.gcd(n_rows, n_occ)
+    piece_rows = mine_refs[0].shape[1]
+    step = math.gcd(piece_rows, n_occ)
     me = my_index(n_orb)
     mine = half_of(me, n_dev)
-    for start in range(0, 4 * chains * n_rows, step):
+    for start in range(0, 4 * chains * piece_rows, step):
         tile, row = divmod(start, n_occ)
-        piece, at = divmod(start, n_rows)
+        piece, at = divmod(start, piece_rows)
         side, chain, j = piece // (2 * chains), piece // 2 % chains, piece % 2
         place = (j + bit(me, tracks[side][0])) % 2
         rows = slice(at, at + step)
@@ -162,29 +176,8 @@
     u_ref[:, :base] = u_oo[:, :base]
     u_ref[:, base:] = (rot - over_rot / 6.0).astype(BF16)
     u_ref[:, base:n_occ] = u_oo[:, base:]
-    l_oo = (over / 6.0 - eye).astype(BF16)
-    left_ref[:, :base] = l_oo[:, :base]
-    left_ref[:, base:] = (over_rot / 24.0 - rot / 2.0).astype(BF16)
-    left_ref[:, base:n_occ] = l_oo[:, base:]
     chosen = matmul(sel_ref[...], u_ref[...], NN)
     chosen_ref[...] = chosen.T[:n_mo].astype(BF16)
-
-
-def swap_rows(tiles):
-    row = lax.broadcasted_iota(jnp.int32, tiles[0].shape, 0)
-    for step in (1, 2, 4):
-        low = (row // step) % 2 == 0
-        after = list(tiles)
-        for t in range(8):
-            if t & step == 0:
-                first, second = tiles[t], tiles[t | step]
-                after[t] = jnp.where(low, first, pltpu.roll(second, step, 0))
-                after[t | step] = jnp.where(low, pltpu.roll(first, 8 - step, 0), second)
-        tiles = after
-    return tiles
-
-
-def half_kernel(n_rows, main, chosen_ref, three_ref, sent_ref, rem_ref, half_ref):
     q_loc, r_loc, n_mo = three_ref.shape
     rem = r_loc - main
     n_dev, dest_rows = sent_ref.shape[:2]
@@ -192,6 +185,10 @@
         product = matmul(three_ref[q], chosen_ref[...], NN)
         half_ref[q] = product[:main].T
         rem_ref[q * rem : (q + 1) * rem, :] = product[main:]
+    l_oo = (over / 6.0 - eye).astype(BF16)
+    left_ref[:, :base] = l_oo[:, :base]
+    left_ref[:, base:] = (over_rot / 24.0 - rot / 2.0).astype(BF16)
+    left_ref[:, base:n_occ] = l_oo[:, base:]
     turned = rem_ref[...].T
 
     def group(at, dest):
@@ -323,26 +320,19 @@
 
     dest_rows = -(-(main // LANES * n_rows * q_loc + n_rows) // 16) * 16
     wide = base + width
-    chosen, left, rot = pl.pallas_call(
-        functools.partial(rotation_kernel, n_orb, n_dev, tracks),
-        in_specs=[in_vmem] * (2 * chains + 2),
+    sent, left, rot = pl.pallas_call(
+        functools.partial(rotate_kernel, n_orb, n_dev, tracks, n_rows, main),
+        in_specs=[in_vmem] * (2 * chains + 3),
         out_specs=[in_vmem] * 3,
         out_shape=[
-            jax.ShapeDtypeStruct((n_mo, n_rows * n_dev), BF16),
+            jax.ShapeDtypeStruct((n_dev, dest_rows, LANES), BF16),
             jax.ShapeDtypeStruct((n_occ, wide), BF16),
             jax.ShapeDtypeStruct((n_occ, width), BF16),
         ],
-        scratch_shapes=[pltpu.VMEM((n_occ, width), F32), pltpu.VMEM((n_occ, wide), BF16)],
-        compiler_params=pltpu.CompilerParams(vmem_limit_bytes=16 * MIB),
-        cost_estimate=pl.CostEstimate(flops=8 * n_occ * n_occ * n_mo, bytes_accessed=4 * MIB, transcendentals=0),
-        name="rotation",
-    )(*held, *other, hess, sel)
-    sent = pl.pallas_call(
-        functools.partial(half_kernel, n_rows, main),
-        in_specs=[in_vmem] * 2,
-        out_specs=in_vmem,
-        out_shape=jax.ShapeDtypeStruct((n_dev, dest_rows, LANES), BF16),
         scratch_shapes=[
+            pltpu.VMEM((n_occ, width), F32),
+            pltpu.VMEM((n_occ, wide), BF16),
+            pltpu.VMEM((n_mo, n_rows * n_dev), BF16),
             pltpu.VMEM((q_loc * (r_loc - main), n_rows * n_dev), F32),
             pltpu.VMEM((q_loc, n_rows * n_dev, main), F32),
         ],
@@ -350,7 +340,7 @@
         cost_estimate=pl.CostEstimate(
             flops=2 * q_loc * r_loc * n_rows * n_dev * n_mo, bytes_accessed=2 * q_loc * r_loc * n_mo, transcendentals=0),
         name="half_rotation",
-    )(chosen, three_vmem)
+    )(*held, *other, hess, sel, three_vmem)
 
     got = lax.all_to_all(sent, BOTH, 0, 0, tiled=True).reshape(n_aux, n_orb, dest_rows, LANES)
     aux_step = min(n_aux, 8)

time: 71.1 us -> 70.9 us (level)
    pallas_call x2 -> x1, Pallas kernels: 5.07 us -> 4.89 us  [on_device(): pl.pallas_call(functools.partial(rotate_kernel, n_orb, n_dev, tracks, n_r...]
where the time goes in v7:
time: 70.9 us; the launch traced here: 70.7 us
  blocking collectives  29.9 us (42%)
  starting transfers between devices  24.4 us (34%)
  Pallas kernels  12.5 us (18%)
  waiting for transfers between devices  3.13 us (4%)
    all_to_all x1, blocking collectives, on_device(): lax.all_to_all(sent, BOTH, 0, 0, tiled=True)  29.9 us
    ppermute x21, starting transfers between devices, swap(): lax.ppermute(x, BOTH, [(d, d ^ mask) for d, mask in enumerate(masks)])  24.4 us
    pallas_call x1, Pallas kernels, on_device(): pl.pallas_call(functools.partial(fock_kernel, n_orb, n_dev, tracks), in_s...  5.17 us
    pallas_call x1, Pallas kernels, on_device(): pl.pallas_call(functools.partial(rotate_kernel, n_orb, n_dev, tracks, n_r...  4.89 us
    ppermute x21, waiting for transfers between devices, swap(): lax.ppermute(x, BOTH, [(d, d ^ mask) for d, mask in enumerate(masks)])  3.13 us
    pallas_call x1, Pallas kernels, on_device(): pl.pallas_call(functools.partial(owner_kernel, n_rows, aux_step, q_loc, r...  2.41 us
  transfers between devices with their start and end apart: 21, of which 7 were waited for; matrix products, arithmetic and copies ran while one was open for 1% of the time, Pallas kernels for 0%

profile of v7, /device:TPU:0, one launch (start us, length us, event | category | flops | bytes accessed | tf_op | source)
XLA Modules:
  0.0 70.7 jit_solution(11025927916421857681)
XLA Ops:
  0.0 5.2 %fock.1 = (f32[2,160,128]{2,1,0:T(8,128)S(1)}, f32[2,160,128]{2,1,0:T(8,128)S(1)}, f32[2,160,128]{2,1,0:T(8,128)S(1)}, bf16[2,160,128]{2,1,0:T(8,128)(2,1)S(1)},...) custom-call(bf16[8,400,1600]{2,1,0:T(8,128)(2,1)} %three_hbm.1, ...), custom_call_target="tpu_custom_call" | custom-call | flops 1638400000 | bytes 10240000 | tf_op jit(solution)/shard_map/fock/pallas_call | solution.py:277
  5.2 0.5 collective-permute-start
  5.8 0.4 collective-permute-start.12
  6.7 2.7 %collective-permute-start.1 = (bf16[160,128]{1,0:T(8,128)(2,1)S(1)}, bf16[160,128]{1,0:T(8,128)(2,1)S(1)}, u32[]{:S(2)}, u32[]{:S(2)}) collective-permute-start(bf16[160,128]{1,0:T(8,128)(2,1)S(1)} %fusion.6), channel_id=1, source_target_pairs={{0,3},{1,4},{2,7},{3,0},{4,1},{5,6},{6,5},{7,2},{8,13},{9,10},{10,... | collective-permute-start | bytes 122888 | tf_op jit(solution)/shard_map/ppermute | solution.py:37
  9.7 1.6 %collective-permute-start.13 = (bf16[160,128]{1,0:T(8,128)(2,1)S(1)}, bf16[160,128]{1,0:T(8,128)(2,1)S(1)}, u32[]{:S(2)}, u32[]{:S(2)}) collective-permute-start(bf16[160,128]{1,0:T(8,128)(2,1)S(1)} %fusion.8), channel_id=1, source_target_pairs={{0,3},{1,4},{2,7},{3,0},{4,1},{5,6},{6,5},{7,2},{8,13},{9,10},{10,... | collective-permute-start | bytes 122888 | tf_op jit(solution)/shard_map/ppermute | solution.py:37
  11.3 1.9 %collective-permute-start.2 = (bf16[160,128]{1,0:T(8,128)(2,1)S(1)}, bf16[160,128]{1,0:T(8,128)(2,1)S(1)}, u32[]{:S(2)}, u32[]{:S(2)}) collective-permute-start(bf16[160,128]{1,0:T(8,128)(2,1)S(1)} %fusion.12), channel_id=1, source_target_pairs={{0,5},{1,2},{2,1},{3,6},{4,7},{5,0},{6,3},{7,4},{8,11},{9,12},{10,... | collective-permute-start | bytes 122888 | tf_op jit(solution)/shard_map/ppermute | solution.py:37
  13.2 1.5 %collective-permute-start.8 = (bf16[160,128]{1,0:T(8,128)(2,1)S(1)}, bf16[160,128]{1,0:T(8,128)(2,1)S(1)}, u32[]{:S(2)}, u32[]{:S(2)}) collective-permute-start(bf16[160,128]{1,0:T(8,128)(2,1)S(1)} %fusion.13), channel_id=1, source_target_pairs={{0,5},{1,2},{2,1},{3,6},{4,7},{5,0},{6,3},{7,4},{8,11},{9,12},{10,... | collective-permute-start | bytes 122888 | tf_op jit(solution)/shard_map/ppermute | solution.py:37
  15.1 1.6 %collective-permute-start.3 = (bf16[160,128]{1,0:T(8,128)(2,1)S(1)}, bf16[160,128]{1,0:T(8,128)(2,1)S(1)}, u32[]{:S(2)}, u32[]{:S(2)}) collective-permute-start(bf16[160,128]{1,0:T(8,128)(2,1)S(1)} %fusion.3), channel_id=1, source_target_pairs={{0,9},{1,16},{2,19},{3,10},{4,21},{5,12},{6,15},{7,22},{8,25},{9,0... | collective-permute-start | bytes 122888 | tf_op jit(solution)/shard_map/ppermute | solution.py:37
  16.7 1.6 %collective-permute-start.9 = (bf16[160,128]{1,0:T(8,128)(2,1)S(1)}, bf16[160,128]{1,0:T(8,128)(2,1)S(1)}, u32[]{:S(2)}, u32[]{:S(2)}) collective-permute-start(bf16[160,128]{1,0:T(8,128)(2,1)S(1)} %fusion.4), channel_id=1, source_target_pairs={{0,9},{1,16},{2,19},{3,10},{4,21},{5,12},{6,15},{7,22},{8,25},{9,0... | collective-permute-start | bytes 122888 | tf_op jit(solution)/shard_map/ppermute | solution.py:37
  18.3 1.3 %collective-permute-start.15 = (bf16[160,128]{1,0:T(8,128)(2,1)S(1)}, bf16[160,128]{1,0:T(8,128)(2,1)S(1)}, u32[]{:S(2)}, u32[]{:S(2)}) collective-permute-start(bf16[160,128]{1,0:T(8,128)(2,1)S(1)} %fusion.5), channel_id=1, source_target_pairs={{0,9},{1,16},{2,19},{3,10},{4,21},{5,12},{6,15},{7,22},{8,25},{9,0... | collective-permute-start | bytes 122888 | tf_op jit(solution)/shard_map/ppermute | solution.py:37
  19.6 2.7 %collective-permute-start.4 = (bf16[160,128]{1,0:T(8,128)(2,1)S(1)}, bf16[160,128]{1,0:T(8,128)(2,1)S(1)}, u32[]{:S(2)}, u32[]{:S(2)}) collective-permute-start(bf16[160,128]{1,0:T(8,128)(2,1)S(1)} %fusion.9), channel_id=1, source_target_pairs={{0,17},{1,8},{2,11},{3,18},{4,13},{5,20},{6,23},{7,14},{8,1},{9,24... | collective-permute-start | bytes 122888 | tf_op jit(solution)/shard_map/ppermute | solution.py:37
  22.3 0.9 %collective-permute-start.10 = (bf16[160,128]{1,0:T(8,128)(2,1)S(1)}, bf16[160,128]{1,0:T(8,128)(2,1)S(1)}, u32[]{:S(2)}, u32[]{:S(2)}) collective-permute-start(bf16[160,128]{1,0:T(8,128)(2,1)S(1)} %fusion.10), channel_id=1, source_target_pairs={{0,17},{1,8},{2,11},{3,18},{4,13},{5,20},{6,23},{7,14},{8,1},{9,24... | collective-permute-start | bytes 122888 | tf_op jit(solution)/shard_map/ppermute | solution.py:37
  23.3 1.9 %collective-permute-start.16 = (bf16[160,128]{1,0:T(8,128)(2,1)S(1)}, bf16[160,128]{1,0:T(8,128)(2,1)S(1)}, u32[]{:S(2)}, u32[]{:S(2)}) collective-permute-start(bf16[160,128]{1,0:T(8,128)(2,1)S(1)} %fusion.11), channel_id=1, source_target_pairs={{0,17},{1,8},{2,11},{3,18},{4,13},{5,20},{6,23},{7,14},{8,1},{9,24... | collective-permute-start | bytes 122888 | tf_op jit(solution)/shard_map/ppermute | solution.py:37
  25.4 1.0 %collective-permute-start.5 = (bf16[160,128]{1,0:T(8,128)(2,1)S(1)}, bf16[160,128]{1,0:T(8,128)(2,1)S(1)}, u32[]{:S(2)}, u32[]{:S(2)}) collective-permute-start(bf16[160,128]{1,0:T(8,128)(2,1)S(1)} %add_convert_fusion.2), channel_id=1, source_target_pairs={{0,3},{1,4},{2,7},{3,0},{4,1},{5,6},{6,5},{7,2},{8,13},{9,10},{10,... | collective-permute-start | bytes 122888 | tf_op jit(solution)/shard_map/ppermute | solution.py:37
  26.4 0.5 collective-permute-done.10
  27.7 1.1 %collective-permute-start.17 = (bf16[160,128]{1,0:T(8,128)(2,1)S(1)}, bf16[160,128]{1,0:T(8,128)(2,1)S(1)}, u32[]{:S(2)}, u32[]{:S(2)}) collective-permute-start(bf16[160,128]{1,0:T(8,128)(2,1)S(1)} %add_convert_fusion), channel_id=1, source_target_pairs={{0,3},{1,4},{2,7},{3,0},{4,1},{5,6},{6,5},{7,2},{8,13},{9,10},{10,... | collective-permute-start | bytes 122888 | tf_op jit(solution)/shard_map/ppermute | solution.py:37
  28.9 1.0 %collective-permute-start.18 = (bf16[2,160,128]{2,1,0:T(8,128)(2,1)S(1)}, bf16[2,160,128]{2,1,0:T(8,128)(2,1)S(1)}, u32[]{:S(2)}, u32[]{:S(2)}) collective-permute-start(bf16[2,160,128]{2,1,0:T(8,128)(2,1)S(1)} %pad_maximum_fusion.refs_0_), channel_id=1, source_target_pairs={{0,1},{1,0},{2,3},{3,2},{4,5},{5,4},{6,7},{7,6},{8,9},{9,8},{10,11... | collective-permute-start | bytes 245768 | tf_op jit(solution)/shard_map/ppermute | solution.py:37
  29.9 0.5 collective-permute-done.11
  30.6 0.6 collective-permute-done.17
  31.2 1.4 %collective-permute-start.20 = (bf16[2,160,128]{2,1,0:T(8,128)(2,1)S(1)}, bf16[2,160,128]{2,1,0:T(8,128)(2,1)S(1)}, u32[]{:S(2)}, u32[]{:S(2)}) collective-permute-start(bf16[2,160,128]{2,1,0:T(8,128)(2,1)S(1)} %pad_maximum_fusion.2.refs_2_), channel_id=1, source_target_pairs={{0,1},{1,0},{2,3},{3,2},{4,5},{5,4},{6,7},{7,6},{8,9},{9,8},{10,11... | collective-permute-start | bytes 245768 | tf_op jit(solution)/shard_map/ppermute | solution.py:37
  32.9 0.6 collective-permute-done.20.refs_5_
  33.5 4.9 %half_rotation.1 = (bf16[32,128,128]{2,1,0:T(8,128)(2,1)S(1)}, bf16[160,1664]{1,0:T(8,128)(2,1)S(1)}, bf16[160,1536]{1,0:T(8,128)(2,1)S(1)}) custom-call(bf16[2,160,128]{2,1,0:T(8,128)(2,1)S(1)} %pad_maximum_fusion.refs_0_, bf16[2,160,128]{2,1,0:T(8,128)(2,1)S(1)} %pad_maximum_fusion.1.refs_1_, bf16[2,160,128]{2,1,0:T(8,128)(2,1)S(1)} %pad_maximum_fusion.2.refs_2_, ...), custom_call_target="tpu_custom_call" | custom-call | flops 1638400000 | bytes 10240000 | tf_op jit(solution)/shard_map/half_rotation/pallas_call | solution.py:323
  38.4 29.9 %all_to_all.5 = bf16[32,128,128]{2,1,0:T(8,128)(2,1)S(1)} all-to-all(bf16[32,128,128]{2,1,0:T(8,128)(2,1)S(1)} %get-tuple-element.22), channel_id=1, replica_groups=mesh['aux'=8,'orb'=4] {'aux','orb'}, dimensions={0} | all-to-all | bytes 2097152 | tf_op jit(solution)/shard_map/all_to_all | solution.py:345
  68.3 2.4 %owner_rows.1 = bf16[64,7200]{1,0:T(8,128)(2,1)} custom-call(bf16[8,4,128,128]{3,2,1,0:T(8,128)(2,1)S(1)} %bitcast.52, bf16[160,1664]{1,0:T(8,128)(2,1)S(1)} %get-tuple-element.23.left_ref, bf16[160,1536]{1,0:T(8,128)(2,1)S(1)} %get-tuple-element.24.rot_ref), custom_call_target="tpu_custom_call" | custom-call | flops 327680000 | bytes 8388608 | tf_op jit(solution)/shard_map/owner_rows/pallas_call | solution.py:347
  (48 shorter events, 3.0 us)
Async XLA Ops:
  0.0 33.5 %copy-start = (bf16[160,160]{1,0:T(8,128)(2,1)S(1)}, bf16[160,160]{1,0:T(8,128)(2,1)}, u32[]{:S(2)}) copy-start(bf16[160,160]{1,0:T(8,128)(2,1)} %constant.4.clone.refs_7_) | copy-start | bytes 153604
  0.0 32.6 %copy-start.1 = (f32[1440,160]{0,1:T(8,128)S(1)}, f32[1440,160]{0,1:T(8,128)}, u32[]{:S(2)}) copy-start(f32[1440,160]{0,1:T(8,128)} %param.6) | copy-start | bytes 2764804
  5.2 1.4 %collective-permute-start = (bf16[2,160,128]{2,1,0:T(8,128)(2,1)S(1)}, bf16[2,160,128]{2,1,0:T(8,128)(2,1)S(1)}, u32[]{:S(2)}, u32[]{:S(2)}) collective-permute-start(bf16[2,160,128]{2,1,0:T(8,128)(2,1)S(1)} %get-tuple-element.16), channel_id=1, source_target_pairs={{0,1},{1,0},{2,3},{3,2},{4,5},{5,4},{6,7},{7,6},{8,9},{9,8},{10,11... | collective-permute-start | bytes 245768 | tf_op jit(solution)/shard_map/ppermute | solution.py:37
  5.7 3.6 %collective-permute-start.6 = (bf16[2,160,128]{2,1,0:T(8,128)(2,1)S(1)}, bf16[2,160,128]{2,1,0:T(8,128)(2,1)S(1)}, u32[]{:S(2)}, u32[]{:S(2)}) collective-permute-start(bf16[2,160,128]{2,1,0:T(8,128)(2,1)S(1)} %get-tuple-element.18), channel_id=1, source_target_pairs={{0,1},{1,0},{2,3},{3,2},{4,5},{5,4},{6,7},{7,6},{8,9},{9,8},{10,11... | collective-permute-start | bytes 245768 | tf_op jit(solution)/shard_map/ppermute | solution.py:37
  5.8 3.9 %collective-permute-start.12 = (bf16[2,160,128]{2,1,0:T(8,128)(2,1)S(1)}, bf16[2,160,128]{2,1,0:T(8,128)(2,1)S(1)}, u32[]{:S(2)}, u32[]{:S(2)}) collective-permute-start(bf16[2,160,128]{2,1,0:T(8,128)(2,1)S(1)} %get-tuple-element.20), channel_id=1, source_target_pairs={{0,1},{1,0},{2,3},{3,2},{4,5},{5,4},{6,7},{7,6},{8,9},{9,8},{10,11... | collective-permute-start | bytes 245768 | tf_op jit(solution)/shard_map/ppermute | solution.py:37
  6.7 4.6 %collective-permute-start.1 = (bf16[160,128]{1,0:T(8,128)(2,1)S(1)}, bf16[160,128]{1,0:T(8,128)(2,1)S(1)}, u32[]{:S(2)}, u32[]{:S(2)}) collective-permute-start(bf16[160,128]{1,0:T(8,128)(2,1)S(1)} %fusion.6), channel_id=1, source_target_pairs={{0,3},{1,4},{2,7},{3,0},{4,1},{5,6},{6,5},{7,2},{8,13},{9,10},{10,... | collective-permute-start | bytes 122888 | tf_op jit(solution)/shard_map/ppermute | solution.py:37
  9.4 3.8 %collective-permute-start.7 = (bf16[160,128]{1,0:T(8,128)(2,1)S(1)}, bf16[160,128]{1,0:T(8,128)(2,1)S(1)}, u32[]{:S(2)}, u32[]{:S(2)}) collective-permute-start(bf16[160,128]{1,0:T(8,128)(2,1)S(1)} %fusion.7), channel_id=1, source_target_pairs={{0,3},{1,4},{2,7},{3,0},{4,1},{5,6},{6,5},{7,2},{8,13},{9,10},{10,... | collective-permute-start | bytes 122888 | tf_op jit(solution)/shard_map/ppermute | solution.py:37
  9.7 5.0 %collective-permute-start.13 = (bf16[160,128]{1,0:T(8,128)(2,1)S(1)}, bf16[160,128]{1,0:T(8,128)(2,1)S(1)}, u32[]{:S(2)}, u32[]{:S(2)}) collective-permute-start(bf16[160,128]{1,0:T(8,128)(2,1)S(1)} %fusion.8), channel_id=1, source_target_pairs={{0,3},{1,4},{2,7},{3,0},{4,1},{5,6},{6,5},{7,2},{8,13},{9,10},{10,... | collective-permute-start | bytes 122888 | tf_op jit(solution)/shard_map/ppermute | solution.py:37
  11.3 3.8 %collective-permute-start.2 = (bf16[160,128]{1,0:T(8,128)(2,1)S(1)}, bf16[160,128]{1,0:T(8,128)(2,1)S(1)}, u32[]{:S(2)}, u32[]{:S(2)}) collective-permute-start(bf16[160,128]{1,0:T(8,128)(2,1)S(1)} %fusion.12), channel_id=1, source_target_pairs={{0,5},{1,2},{2,1},{3,6},{4,7},{5,0},{6,3},{7,4},{8,11},{9,12},{10,... | collective-permute-start | bytes 122888 | tf_op jit(solution)/shard_map/ppermute | solution.py:37
  13.2 3.5 %collective-permute-start.8 = (bf16[160,128]{1,0:T(8,128)(2,1)S(1)}, bf16[160,128]{1,0:T(8,128)(2,1)S(1)}, u32[]{:S(2)}, u32[]{:S(2)}) collective-permute-start(bf16[160,128]{1,0:T(8,128)(2,1)S(1)} %fusion.13), channel_id=1, source_target_pairs={{0,5},{1,2},{2,1},{3,6},{4,7},{5,0},{6,3},{7,4},{8,11},{9,12},{10,... | collective-permute-start | bytes 122888 | tf_op jit(solution)/shard_map/ppermute | solution.py:37
  14.7 3.6 %collective-permute-start.14 = (bf16[160,128]{1,0:T(8,128)(2,1)S(1)}, bf16[160,128]{1,0:T(8,128)(2,1)S(1)}, u32[]{:S(2)}, u32[]{:S(2)}) collective-permute-start(bf16[160,128]{1,0:T(8,128)(2,1)S(1)} %fusion.14), channel_id=1, source_target_pairs={{0,5},{1,2},{2,1},{3,6},{4,7},{5,0},{6,3},{7,4},{8,11},{9,12},{10,... | collective-permute-start | bytes 122888 | tf_op jit(solution)/shard_map/ppermute | solution.py:37
  15.1 4.5 %collective-permute-start.3 = (bf16[160,128]{1,0:T(8,128)(2,1)S(1)}, bf16[160,128]{1,0:T(8,128)(2,1)S(1)}, u32[]{:S(2)}, u32[]{:S(2)}) collective-permute-start(bf16[160,128]{1,0:T(8,128)(2,1)S(1)} %fusion.3), channel_id=1, source_target_pairs={{0,9},{1,16},{2,19},{3,10},{4,21},{5,12},{6,15},{7,22},{8,25},{9,0... | collective-permute-start | bytes 122888 | tf_op jit(solution)/shard_map/ppermute | solution.py:37
  16.7 5.6 %collective-permute-start.9 = (bf16[160,128]{1,0:T(8,128)(2,1)S(1)}, bf16[160,128]{1,0:T(8,128)(2,1)S(1)}, u32[]{:S(2)}, u32[]{:S(2)}) collective-permute-start(bf16[160,128]{1,0:T(8,128)(2,1)S(1)} %fusion.4), channel_id=1, source_target_pairs={{0,9},{1,16},{2,19},{3,10},{4,21},{5,12},{6,15},{7,22},{8,25},{9,0... | collective-permute-start | bytes 122888 | tf_op jit(solution)/shard_map/ppermute | solution.py:37
  18.3 4.9 %collective-permute-start.15 = (bf16[160,128]{1,0:T(8,128)(2,1)S(1)}, bf16[160,128]{1,0:T(8,128)(2,1)S(1)}, u32[]{:S(2)}, u32[]{:S(2)}) collective-permute-start(bf16[160,128]{1,0:T(8,128)(2,1)S(1)} %fusion.5), channel_id=1, source_target_pairs={{0,9},{1,16},{2,19},{3,10},{4,21},{5,12},{6,15},{7,22},{8,25},{9,0... | collective-permute-start | bytes 122888 | tf_op jit(solution)/shard_map/ppermute | solution.py:37
  19.6 5.7 %collective-permute-start.4 = (bf16[160,128]{1,0:T(8,128)(2,1)S(1)}, bf16[160,128]{1,0:T(8,128)(2,1)S(1)}, u32[]{:S(2)}, u32[]{:S(2)}) collective-permute-start(bf16[160,128]{1,0:T(8,128)(2,1)S(1)} %fusion.9), channel_id=1, source_target_pairs={{0,17},{1,8},{2,11},{3,18},{4,13},{5,20},{6,23},{7,14},{8,1},{9,24... | collective-permute-start | bytes 122888 | tf_op jit(solution)/shard_map/ppermute | solution.py:37
  22.3 4.5 %collective-permute-start.10 = (bf16[160,128]{1,0:T(8,128)(2,1)S(1)}, bf16[160,128]{1,0:T(8,128)(2,1)S(1)}, u32[]{:S(2)}, u32[]{:S(2)}) collective-permute-start(bf16[160,128]{1,0:T(8,128)(2,1)S(1)} %fusion.10), channel_id=1, source_target_pairs={{0,17},{1,8},{2,11},{3,18},{4,13},{5,20},{6,23},{7,14},{8,1},{9,24... | collective-permute-start | bytes 122888 | tf_op jit(solution)/shard_map/ppermute | solution.py:37
  23.3 4.4 %collective-permute-start.16 = (bf16[160,128]{1,0:T(8,128)(2,1)S(1)}, bf16[160,128]{1,0:T(8,128)(2,1)S(1)}, u32[]{:S(2)}, u32[]{:S(2)}) collective-permute-start(bf16[160,128]{1,0:T(8,128)(2,1)S(1)} %fusion.11), channel_id=1, source_target_pairs={{0,17},{1,8},{2,11},{3,18},{4,13},{5,20},{6,23},{7,14},{8,1},{9,24... | collective-permute-start | bytes 122888 | tf_op jit(solution)/shard_map/ppermute | solution.py:37
  25.4 3.5 %collective-permute-start.5 = (bf16[160,128]{1,0:T(8,128)(2,1)S(1)}, bf16[160,128]{1,0:T(8,128)(2,1)S(1)}, u32[]{:S(2)}, u32[]{:S(2)}) collective-permute-start(bf16[160,128]{1,0:T(8,128)(2,1)S(1)} %add_convert_fusion.2), channel_id=1, source_target_pairs={{0,3},{1,4},{2,7},{3,0},{4,1},{5,6},{6,5},{7,2},{8,13},{9,10},{10,... | collective-permute-start | bytes 122888 | tf_op jit(solution)/shard_map/ppermute | solution.py:37
  26.9 3.5 %collective-permute-start.11 = (bf16[160,128]{1,0:T(8,128)(2,1)S(1)}, bf16[160,128]{1,0:T(8,128)(2,1)S(1)}, u32[]{:S(2)}, u32[]{:S(2)}) collective-permute-start(bf16[160,128]{1,0:T(8,128)(2,1)S(1)} %add_convert_fusion.1), channel_id=1, source_target_pairs={{0,3},{1,4},{2,7},{3,0},{4,1},{5,6},{6,5},{7,2},{8,13},{9,10},{10,... | collective-permute-start | bytes 122888 | tf_op jit(solution)/shard_map/ppermute | solution.py:37
  27.7 3.5 %collective-permute-start.17 = (bf16[160,128]{1,0:T(8,128)(2,1)S(1)}, bf16[160,128]{1,0:T(8,128)(2,1)S(1)}, u32[]{:S(2)}, u32[]{:S(2)}) collective-permute-start(bf16[160,128]{1,0:T(8,128)(2,1)S(1)} %add_convert_fusion), channel_id=1, source_target_pairs={{0,3},{1,4},{2,7},{3,0},{4,1},{5,6},{6,5},{7,2},{8,13},{9,10},{10,... | collective-permute-start | bytes 122888 | tf_op jit(solution)/shard_map/ppermute | solution.py:37
  28.9 4.0 %collective-permute-start.18 = (bf16[2,160,128]{2,1,0:T(8,128)(2,1)S(1)}, bf16[2,160,128]{2,1,0:T(8,128)(2,1)S(1)}, u32[]{:S(2)}, u32[]{:S(2)}) collective-permute-start(bf16[2,160,128]{2,1,0:T(8,128)(2,1)S(1)} %pad_maximum_fusion.refs_0_), channel_id=1, source_target_pairs={{0,1},{1,0},{2,3},{3,2},{4,5},{5,4},{6,7},{7,6},{8,9},{9,8},{10,11... | collective-permute-start | bytes 245768 | tf_op jit(solution)/shard_map/ppermute | solution.py:37
  30.4 2.5 %collective-permute-start.19 = (bf16[2,160,128]{2,1,0:T(8,128)(2,1)S(1)}, bf16[2,160,128]{2,1,0:T(8,128)(2,1)S(1)}, u32[]{:S(2)}, u32[]{:S(2)}) collective-permute-start(bf16[2,160,128]{2,1,0:T(8,128)(2,1)S(1)} %pad_maximum_fusion.1.refs_1_), channel_id=1, source_target_pairs={{0,1},{1,0},{2,3},{3,2},{4,5},{5,4},{6,7},{7,6},{8,9},{9,8},{10,11... | collective-permute-start | bytes 245768 | tf_op jit(solution)/shard_map/ppermute | solution.py:37
  31.2 2.3 %collective-permute-start.20 = (bf16[2,160,128]{2,1,0:T(8,128)(2,1)S(1)}, bf16[2,160,128]{2,1,0:T(8,128)(2,1)S(1)}, u32[]{:S(2)}, u32[]{:S(2)}) collective-permute-start(bf16[2,160,128]{2,1,0:T(8,128)(2,1)S(1)} %pad_maximum_fusion.2.refs_2_), channel_id=1, source_target_pairs={{0,1},{1,0},{2,3},{3,2},{4,5},{5,4},{6,7},{7,6},{8,9},{9,8},{10,11... | collective-permute-start | bytes 245768 | tf_op jit(solution)/shard_map/ppermute | solution.py:37

commit v8 on v7

--- a/solution.py
+++ b/solution.py
@@ -271,7 +271,7 @@
     whole = lambda *shape: pl.BlockSpec(shape, lambda *_: (0,) * len(shape))
     in_vmem = pl.BlockSpec(memory_space=pltpu.VMEM)
 
-    chains = 3
+    chains = 2
     half_shape = (2, tiles * n_occ // (4 * chains), LANES)
     in_hbm = pl.BlockSpec(memory_space=pltpu.HBM)
     *parts, three_vmem = pl.pallas_call(

time: 70.9 us -> 71 us (level)
  starting transfers between devices: 24.4 us -> 18.6 us
  waiting for transfers between devices: 3.13 us -> 7.7 us
  blocking collectives: 29.9 us -> 31.3 us
    ppermute x21 -> x14, starting transfers between devices: 24.4 us -> 18.6 us  [swap(): lax.ppermute(x, BOTH, [(d, d ^ mask) for d, mask in enumerate(masks)])]
    ppermute x21 -> x14, waiting for transfers between devices: 3.13 us -> 7.7 us  [swap(): lax.ppermute(x, BOTH, [(d, d ^ mask) for d, mask in enumerate(masks)])]
    all_to_all x1, blocking collectives: 29.9 us -> 31.3 us  [on_device(): lax.all_to_all(sent, BOTH, 0, 0, tiled=True)]
  transfers between devices with their start and end apart: 21 -> 14, of which waited for: 7 -> 10; matrix products, arithmetic and copies ran while one was open for 1% -> 1% of each run, Pallas kernels for 0% -> 0%
where the time goes in v8:
time: 71 us; the launch traced here: 70.8 us
  blocking collectives  31.3 us (44%)
  starting transfers between devices  18.6 us (26%)
  Pallas kernels  12.5 us (18%)
  waiting for transfers between devices  7.7 us (11%)
    all_to_all x1, blocking collectives, on_device(): lax.all_to_all(sent, BOTH, 0, 0, tiled=True)  31.3 us
    ppermute x14, starting transfers between devices, swap(): lax.ppermute(x, BOTH, [(d, d ^ mask) for d, mask in enumerate(masks)])  18.6 us
    ppermute x14, waiting for transfers between devices, swap(): lax.ppermute(x, BOTH, [(d, d ^ mask) for d, mask in enumerate(masks)])  7.7 us
    pallas_call x1, Pallas kernels, on_device(): pl.pallas_call(functools.partial(fock_kernel, n_orb, n_dev, tracks), in_s...  5.17 us
    pallas_call x1, Pallas kernels, on_device(): pl.pallas_call(functools.partial(rotate_kernel, n_orb, n_dev, tracks, n_r...  4.87 us
    pallas_call x1, Pallas kernels, on_device(): pl.pallas_call(functools.partial(owner_kernel, n_rows, aux_step, q_loc, r...  2.41 us
  transfers between devices with their start and end apart: 14, of which 10 were waited for; matrix products, arithmetic and copies ran while one was open for 1% of the time, Pallas kernels for 0%

profile of v8, /device:TPU:0, one launch (start us, length us, event | category | flops | bytes accessed | tf_op | source)
XLA Modules:
  0.0 70.8 jit_solution(5692485968321358724)
XLA Ops:
  0.0 5.2 %fock.1 = (f32[2,240,128]{2,1,0:T(8,128)S(1)}, f32[2,240,128]{2,1,0:T(8,128)S(1)}, bf16[2,240,128]{2,1,0:T(8,128)(2,1)S(1)}, bf16[2,240,128]{2,1,0:T(8,128)(2,1)S(1)}, bf16[8,400,1600]{2,1,0:T(8,128)(2,1)S(1)}) custom-call(bf16[8,400,1600]{2,1,0:T(8,128)(2,1)} %three_hbm.1, bf16[8,160,400]{2,1,0:T(8,128)(2,1)} %bitcast.37), custom_call_target="tpu_custom_call" | custom-call | flops 1638400000 | bytes 10240000 | tf_op jit(solution)/shard_map/fock/pallas_call | solution.py:277
  5.2 0.5 collective-permute-start
  5.8 0.9 %collective-permute-done = bf16[2,240,128]{2,1,0:T(8,128)(2,1)S(1)} collective-permute-done((bf16[2,240,128]{2,1,0:T(8,128)(2,1)S(1)}, bf16[2,240,128]{2,1,0:T(8,128)(2,1)S(1)}, u32[]{:S(2)}, u32[]{:S(2)}) %collective-permute-start) | collective-permute-done | bytes 122912 | tf_op jit(solution)/shard_map/ppermute | solution.py:37
  6.7 2.7 %collective-permute-start.1 = (bf16[240,128]{1,0:T(8,128)(2,1)S(1)}, bf16[240,128]{1,0:T(8,128)(2,1)S(1)}, u32[]{:S(2)}, u32[]{:S(2)}) collective-permute-start(bf16[240,128]{1,0:T(8,128)(2,1)S(1)} %fusion.4), channel_id=1, source_target_pairs={{0,3},{1,4},{2,7},{3,0},{4,1},{5,6},{6,5},{7,2},{8,13},{9,10},{10,... | collective-permute-start | bytes 184328 | tf_op jit(solution)/shard_map/ppermute | solution.py:37
  9.7 1.5 %collective-permute-done.1 = bf16[240,128]{1,0:T(8,128)(2,1)S(1)} collective-permute-done((bf16[240,128]{1,0:T(8,128)(2,1)S(1)}, bf16[240,128]{1,0:T(8,128)(2,1)S(1)}, u32[]{:S(2)}, u32[]{:S(2)}) %collective-permute-start.1) | collective-permute-done | bytes 61472 | tf_op jit(solution)/shard_map/ppermute | solution.py:37
  11.3 2.1 %collective-permute-start.2 = (bf16[240,128]{1,0:T(8,128)(2,1)S(1)}, bf16[240,128]{1,0:T(8,128)(2,1)S(1)}, u32[]{:S(2)}, u32[]{:S(2)}) collective-permute-start(bf16[240,128]{1,0:T(8,128)(2,1)S(1)} %fusion.8), channel_id=1, source_target_pairs={{0,5},{1,2},{2,1},{3,6},{4,7},{5,0},{6,3},{7,4},{8,11},{9,12},{10,... | collective-permute-start | bytes 184328 | tf_op jit(solution)/shard_map/ppermute | solution.py:37
  13.5 1.2 %collective-permute-start.8 = (bf16[240,128]{1,0:T(8,128)(2,1)S(1)}, bf16[240,128]{1,0:T(8,128)(2,1)S(1)}, u32[]{:S(2)}, u32[]{:S(2)}) collective-permute-start(bf16[240,128]{1,0:T(8,128)(2,1)S(1)} %fusion.9), channel_id=1, source_target_pairs={{0,5},{1,2},{2,1},{3,6},{4,7},{5,0},{6,3},{7,4},{8,11},{9,12},{10,... | collective-permute-start | bytes 184328 | tf_op jit(solution)/shard_map/ppermute | solution.py:37
  14.7 0.6 collective-permute-done.2
  15.4 1.6 %collective-permute-start.3 = (bf16[240,128]{1,0:T(8,128)(2,1)S(1)}, bf16[240,128]{1,0:T(8,128)(2,1)S(1)}, u32[]{:S(2)}, u32[]{:S(2)}) collective-permute-start(bf16[240,128]{1,0:T(8,128)(2,1)S(1)} %fusion.2), channel_id=1, source_target_pairs={{0,9},{1,16},{2,19},{3,10},{4,21},{5,12},{6,15},{7,22},{8,25},{9,0... | collective-permute-start | bytes 184328 | tf_op jit(solution)/shard_map/ppermute | solution.py:37
  17.2 1.3 %collective-permute-start.9 = (bf16[240,128]{1,0:T(8,128)(2,1)S(1)}, bf16[240,128]{1,0:T(8,128)(2,1)S(1)}, u32[]{:S(2)}, u32[]{:S(2)}) collective-permute-start(bf16[240,128]{1,0:T(8,128)(2,1)S(1)} %fusion.3), channel_id=1, source_target_pairs={{0,9},{1,16},{2,19},{3,10},{4,21},{5,12},{6,15},{7,22},{8,25},{9,0... | collective-permute-start | bytes 184328 | tf_op jit(solution)/shard_map/ppermute | solution.py:37
  18.5 0.6 collective-permute-done.3
  19.1 3.1 %collective-permute-start.4 = (bf16[240,128]{1,0:T(8,128)(2,1)S(1)}, bf16[240,128]{1,0:T(8,128)(2,1)S(1)}, u32[]{:S(2)}, u32[]{:S(2)}) collective-permute-start(bf16[240,128]{1,0:T(8,128)(2,1)S(1)} %fusion.6), channel_id=1, source_target_pairs={{0,17},{1,8},{2,11},{3,18},{4,13},{5,20},{6,23},{7,14},{8,1},{9,24... | collective-permute-start | bytes 184328 | tf_op jit(solution)/shard_map/ppermute | solution.py:37
  22.3 1.8 %collective-permute-start.10 = (bf16[240,128]{1,0:T(8,128)(2,1)S(1)}, bf16[240,128]{1,0:T(8,128)(2,1)S(1)}, u32[]{:S(2)}, u32[]{:S(2)}) collective-permute-start(bf16[240,128]{1,0:T(8,128)(2,1)S(1)} %fusion.7), channel_id=1, source_target_pairs={{0,17},{1,8},{2,11},{3,18},{4,13},{5,20},{6,23},{7,14},{8,1},{9,24... | collective-permute-start | bytes 184328 | tf_op jit(solution)/shard_map/ppermute | solution.py:37
  24.0 0.6 collective-permute-done.4
  24.7 1.9 %collective-permute-start.5 = (bf16[240,128]{1,0:T(8,128)(2,1)S(1)}, bf16[240,128]{1,0:T(8,128)(2,1)S(1)}, u32[]{:S(2)}, u32[]{:S(2)}) collective-permute-start(bf16[240,128]{1,0:T(8,128)(2,1)S(1)} %add_convert_fusion.1), channel_id=1, source_target_pairs={{0,3},{1,4},{2,7},{3,0},{4,1},{5,6},{6,5},{7,2},{8,13},{9,10},{10,... | collective-permute-start | bytes 184328 | tf_op jit(solution)/shard_map/ppermute | solution.py:37
  26.5 0.4 collective-permute-done.10
  27.0 1.3 %collective-permute-start.11 = (bf16[240,128]{1,0:T(8,128)(2,1)S(1)}, bf16[240,128]{1,0:T(8,128)(2,1)S(1)}, u32[]{:S(2)}, u32[]{:S(2)}) collective-permute-start(bf16[240,128]{1,0:T(8,128)(2,1)S(1)} %add_convert_fusion), channel_id=1, source_target_pairs={{0,3},{1,4},{2,7},{3,0},{4,1},{5,6},{6,5},{7,2},{8,13},{9,10},{10,... | collective-permute-start | bytes 184328 | tf_op jit(solution)/shard_map/ppermute | solution.py:37
  28.6 2.1 %collective-permute-done.11 = bf16[240,128]{1,0:T(8,128)(2,1)S(1)} collective-permute-done((bf16[240,128]{1,0:T(8,128)(2,1)S(1)}, bf16[240,128]{1,0:T(8,128)(2,1)S(1)}, u32[]{:S(2)}, u32[]{:S(2)}) %collective-permute-start.11) | collective-permute-done | bytes 61472 | tf_op jit(solution)/shard_map/ppermute | solution.py:37
  30.7 0.5 collective-permute-start.13
  31.2 0.3 pad.4.refs_4_
  31.5 0.6 collective-permute-done.13.refs_3_
  32.2 4.9 %half_rotation.1 = (bf16[32,128,128]{2,1,0:T(8,128)(2,1)S(1)}, bf16[160,1664]{1,0:T(8,128)(2,1)S(1)}, bf16[160,1536]{1,0:T(8,128)(2,1)S(1)}) custom-call(bf16[2,240,128]{2,1,0:T(8,128)(2,1)S(1)} %pad_maximum_fusion.refs_0_, bf16[2,240,128]{2,1,0:T(8,128)(2,1)S(1)} %pad_maximum_fusion.1.refs_1_, bf16[2,240,128]{2,1,0:T(8,128)(2,1)S(1)} %collective-permute-done.12.refs_2_, ...), custom_call_target="tpu_custom_call" | custom-call | flops 1638400000 | bytes 10240000 | tf_op jit(solution)/shard_map/half_rotation/pallas_call | solution.py:323
  37.1 31.3 %all_to_all.5 = bf16[32,128,128]{2,1,0:T(8,128)(2,1)S(1)} all-to-all(bf16[32,128,128]{2,1,0:T(8,128)(2,1)S(1)} %get-tuple-element.18), channel_id=1, replica_groups=mesh['aux'=8,'orb'=4] {'aux','orb'}, dimensions={0} | all-to-all | bytes 2097152 | tf_op jit(solution)/shard_map/all_to_all | solution.py:345
  68.4 2.4 %owner_rows.1 = bf16[64,7200]{1,0:T(8,128)(2,1)} custom-call(bf16[8,4,128,128]{3,2,1,0:T(8,128)(2,1)S(1)} %bitcast.36, bf16[160,1664]{1,0:T(8,128)(2,1)S(1)} %get-tuple-element.19.left_ref, bf16[160,1536]{1,0:T(8,128)(2,1)S(1)} %get-tuple-element.20.rot_ref), custom_call_target="tpu_custom_call" | custom-call | flops 327680000 | bytes 8388608 | tf_op jit(solution)/shard_map/owner_rows/pallas_call | solution.py:347
  (27 shorter events, 1.3 us)
Async XLA Ops:
  0.0 32.2 %copy-start = (bf16[160,160]{1,0:T(8,128)(2,1)S(1)}, bf16[160,160]{1,0:T(8,128)(2,1)}, u32[]{:S(2)}) copy-start(bf16[160,160]{1,0:T(8,128)(2,1)} %constant.4.clone.refs_5_) | copy-start | bytes 153604
  0.0 31.2 %copy-start.1 = (f32[1440,160]{0,1:T(8,128)S(1)}, f32[1440,160]{0,1:T(8,128)}, u32[]{:S(2)}) copy-start(f32[1440,160]{0,1:T(8,128)} %param.6) | copy-start | bytes 2764804
  5.2 1.5 %collective-permute-start = (bf16[2,240,128]{2,1,0:T(8,128)(2,1)S(1)}, bf16[2,240,128]{2,1,0:T(8,128)(2,1)S(1)}, u32[]{:S(2)}, u32[]{:S(2)}) collective-permute-start(bf16[2,240,128]{2,1,0:T(8,128)(2,1)S(1)} %get-tuple-element.14), channel_id=1, source_target_pairs={{0,1},{1,0},{2,3},{3,2},{4,5},{5,4},{6,7},{7,6},{8,9},{9,8},{10,11... | collective-permute-start | bytes 368648 | tf_op jit(solution)/shard_map/ppermute | solution.py:37
  5.7 3.7 %collective-permute-start.6 = (bf16[2,240,128]{2,1,0:T(8,128)(2,1)S(1)}, bf16[2,240,128]{2,1,0:T(8,128)(2,1)S(1)}, u32[]{:S(2)}, u32[]{:S(2)}) collective-permute-start(bf16[2,240,128]{2,1,0:T(8,128)(2,1)S(1)} %get-tuple-element.16), channel_id=1, source_target_pairs={{0,1},{1,0},{2,3},{3,2},{4,5},{5,4},{6,7},{7,6},{8,9},{9,8},{10,11... | collective-permute-start | bytes 368648 | tf_op jit(solution)/shard_map/ppermute | solution.py:37
  6.7 4.6 %collective-permute-start.1 = (bf16[240,128]{1,0:T(8,128)(2,1)S(1)}, bf16[240,128]{1,0:T(8,128)(2,1)S(1)}, u32[]{:S(2)}, u32[]{:S(2)}) collective-permute-start(bf16[240,128]{1,0:T(8,128)(2,1)S(1)} %fusion.4), channel_id=1, source_target_pairs={{0,3},{1,4},{2,7},{3,0},{4,1},{5,6},{6,5},{7,2},{8,13},{9,10},{10,... | collective-permute-start | bytes 184328 | tf_op jit(solution)/shard_map/ppermute | solution.py:37
  9.4 4.0 %collective-permute-start.7 = (bf16[240,128]{1,0:T(8,128)(2,1)S(1)}, bf16[240,128]{1,0:T(8,128)(2,1)S(1)}, u32[]{:S(2)}, u32[]{:S(2)}) collective-permute-start(bf16[240,128]{1,0:T(8,128)(2,1)S(1)} %fusion.5), channel_id=1, source_target_pairs={{0,3},{1,4},{2,7},{3,0},{4,1},{5,6},{6,5},{7,2},{8,13},{9,10},{10,... | collective-permute-start | bytes 184328 | tf_op jit(solution)/shard_map/ppermute | solution.py:37
  11.3 4.0 %collective-permute-start.2 = (bf16[240,128]{1,0:T(8,128)(2,1)S(1)}, bf16[240,128]{1,0:T(8,128)(2,1)S(1)}, u32[]{:S(2)}, u32[]{:S(2)}) collective-permute-start(bf16[240,128]{1,0:T(8,128)(2,1)S(1)} %fusion.8), channel_id=1, source_target_pairs={{0,5},{1,2},{2,1},{3,6},{4,7},{5,0},{6,3},{7,4},{8,11},{9,12},{10,... | collective-permute-start | bytes 184328 | tf_op jit(solution)/shard_map/ppermute | solution.py:37
  13.5 3.7 %collective-permute-start.8 = (bf16[240,128]{1,0:T(8,128)(2,1)S(1)}, bf16[240,128]{1,0:T(8,128)(2,1)S(1)}, u32[]{:S(2)}, u32[]{:S(2)}) collective-permute-start(bf16[240,128]{1,0:T(8,128)(2,1)S(1)} %fusion.9), channel_id=1, source_target_pairs={{0,5},{1,2},{2,1},{3,6},{4,7},{5,0},{6,3},{7,4},{8,11},{9,12},{10,... | collective-permute-start | bytes 184328 | tf_op jit(solution)/shard_map/ppermute | solution.py:37
  15.4 3.7 %collective-permute-start.3 = (bf16[240,128]{1,0:T(8,128)(2,1)S(1)}, bf16[240,128]{1,0:T(8,128)(2,1)S(1)}, u32[]{:S(2)}, u32[]{:S(2)}) collective-permute-start(bf16[240,128]{1,0:T(8,128)(2,1)S(1)} %fusion.2), channel_id=1, source_target_pairs={{0,9},{1,16},{2,19},{3,10},{4,21},{5,12},{6,15},{7,22},{8,25},{9,0... | collective-permute-start | bytes 184328 | tf_op jit(solution)/shard_map/ppermute | solution.py:37
  17.2 5.0 %collective-permute-start.9 = (bf16[240,128]{1,0:T(8,128)(2,1)S(1)}, bf16[240,128]{1,0:T(8,128)(2,1)S(1)}, u32[]{:S(2)}, u32[]{:S(2)}) collective-permute-start(bf16[240,128]{1,0:T(8,128)(2,1)S(1)} %fusion.3), channel_id=1, source_target_pairs={{0,9},{1,16},{2,19},{3,10},{4,21},{5,12},{6,15},{7,22},{8,25},{9,0... | collective-permute-start | bytes 184328 | tf_op jit(solution)/shard_map/ppermute | solution.py:37
  19.1 5.5 %collective-permute-start.4 = (bf16[240,128]{1,0:T(8,128)(2,1)S(1)}, bf16[240,128]{1,0:T(8,128)(2,1)S(1)}, u32[]{:S(2)}, u32[]{:S(2)}) collective-permute-start(bf16[240,128]{1,0:T(8,128)(2,1)S(1)} %fusion.6), channel_id=1, source_target_pairs={{0,17},{1,8},{2,11},{3,18},{4,13},{5,20},{6,23},{7,14},{8,1},{9,24... | collective-permute-start | bytes 184328 | tf_op jit(solution)/shard_map/ppermute | solution.py:37
  22.3 4.6 %collective-permute-start.10 = (bf16[240,128]{1,0:T(8,128)(2,1)S(1)}, bf16[240,128]{1,0:T(8,128)(2,1)S(1)}, u32[]{:S(2)}, u32[]{:S(2)}) collective-permute-start(bf16[240,128]{1,0:T(8,128)(2,1)S(1)} %fusion.7), channel_id=1, source_target_pairs={{0,17},{1,8},{2,11},{3,18},{4,13},{5,20},{6,23},{7,14},{8,1},{9,24... | collective-permute-start | bytes 184328 | tf_op jit(solution)/shard_map/ppermute | solution.py:37
  24.7 3.8 %collective-permute-start.5 = (bf16[240,128]{1,0:T(8,128)(2,1)S(1)}, bf16[240,128]{1,0:T(8,128)(2,1)S(1)}, u32[]{:S(2)}, u32[]{:S(2)}) collective-permute-start(bf16[240,128]{1,0:T(8,128)(2,1)S(1)} %add_convert_fusion.1), channel_id=1, source_target_pairs={{0,3},{1,4},{2,7},{3,0},{4,1},{5,6},{6,5},{7,2},{8,13},{9,10},{10,... | collective-permute-start | bytes 184328 | tf_op jit(solution)/shard_map/ppermute | solution.py:37
  27.0 3.7 %collective-permute-start.11 = (bf16[240,128]{1,0:T(8,128)(2,1)S(1)}, bf16[240,128]{1,0:T(8,128)(2,1)S(1)}, u32[]{:S(2)}, u32[]{:S(2)}) collective-permute-start(bf16[240,128]{1,0:T(8,128)(2,1)S(1)} %add_convert_fusion), channel_id=1, source_target_pairs={{0,3},{1,4},{2,7},{3,0},{4,1},{5,6},{6,5},{7,2},{8,13},{9,10},{10,... | collective-permute-start | bytes 184328 | tf_op jit(solution)/shard_map/ppermute | solution.py:37
  28.4 3.1 %collective-permute-start.12 = (bf16[2,240,128]{2,1,0:T(8,128)(2,1)S(1)}, bf16[2,240,128]{2,1,0:T(8,128)(2,1)S(1)}, u32[]{:S(2)}, u32[]{:S(2)}) collective-permute-start(bf16[2,240,128]{2,1,0:T(8,128)(2,1)S(1)} %pad_maximum_fusion.refs_0_), channel_id=1, source_target_pairs={{0,1},{1,0},{2,3},{3,2},{4,5},{5,4},{6,7},{7,6},{8,9},{9,8},{10,11... | collective-permute-start | bytes 368648 | tf_op jit(solution)/shard_map/ppermute | solution.py:37
  30.7 1.5 %collective-permute-start.13 = (bf16[2,240,128]{2,1,0:T(8,128)(2,1)S(1)}, bf16[2,240,128]{2,1,0:T(8,128)(2,1)S(1)}, u32[]{:S(2)}, u32[]{:S(2)}) collective-permute-start(bf16[2,240,128]{2,1,0:T(8,128)(2,1)S(1)} %pad_maximum_fusion.1.refs_1_), channel_id=1, source_target_pairs={{0,1},{1,0},{2,3},{3,2},{4,5},{5,4},{6,7},{7,6},{8,9},{9,8},{10,11... | collective-permute-start | bytes 368648 | tf_op jit(solution)/shard_map/ppermute | solution.py:37
